TPU v7x, 128 devices: a whole 4x4x4 slice. The times are simulated.
128 devices in a mesh: cuts: 8 (over y, core), shard: 16 (over z, x).
Axes of the slice: x: 4, y: 4, z: 4, core: 2. Of those that a mesh axis runs over, the one named last changes fastest.
Arguments:
- tokens: bfloat16 [512, 8192], P('cuts', 'shard'), may hold values from -6 to 6
- grad_out: bfloat16 [512, 8192], P('cuts', 'shard'), may hold values from -6 to 6
- counts: int32 [512], P('cuts'), may hold values from 1 to 8, as said below
- gate_weight: bfloat16 [28672, 8192], P(('cuts', 'shard')), may hold values from -0.0625 to 0.0625
- up_weight: bfloat16 [28672, 8192], P(('cuts', 'shard')), may hold values from -0.0625 to 0.0625
- down_weight: bfloat16 [28672, 8192], P(('cuts', 'shard')), may hold values from -0.03125 to 0.03125
Outputs:
- grad_in: bfloat16 [512, 8192], P('cuts', 'shard')
- grad_gate: bfloat16 [28672, 8192], P(('cuts', 'shard'))
- grad_up: bfloat16 [28672, 8192], P(('cuts', 'shard'))
- grad_down: bfloat16 [28672, 8192], P(('cuts', 'shard'))
Inputs may be any that keep to these rules, and one draw needn't show every extreme that they name: `counts`: some token has 8 and some token has 1.
All inputs are finite; a program needn't handle non-finite values.
Results may differ from a plain program's by a relative error of at most 0.0049.
Values may be sent and summed in bfloat16 or wider, within the bound.
No kernel may reach another device: no remote copies, remote signals or barrier semaphores. Data moves between devices by JAX's collectives and lax.ppermute only.
A program may use at most 192 MiB of HBM per device.

v0:
```python
import jax
import jax.numpy as jnp
from jax import lax
from jax.sharding import PartitionSpec as P


def level_ranks(counts, levels):
    level = jnp.arange(levels, dtype=jnp.int32)[:, None]
    used = (counts[None, :] > level).astype(jnp.int32)
    ranked = jnp.cumsum(used, axis=1) - 1
    return (used, ranked)


def slot_table(used, ranked, capacity):
    slot = jnp.arange(capacity, dtype=jnp.int32)[None, :, None]
    return (used[:, None, :] == 1) & (ranked[:, None, :] == slot)


def place_rows(table, rows):
    placed = jnp.einsum(
        "spt,tf->spf", table.astype(jnp.bfloat16), rows, preferred_element_type=jnp.float32
    )
    return placed.astype(jnp.bfloat16)


def collect_rows(used, ranked, blocks):
    index = jnp.maximum(ranked, 0)
    picked = jax.vmap(lambda block, where: block[where])(blocks, index)
    return jnp.sum(picked * used.astype(jnp.float32)[:, :, None], axis=0)


def body(tokens, grad_out, counts, gate_weight, up_weight, down_weight):
    levels = lax.axis_size("cuts")
    capacity = tokens.shape[0]
    used, ranked = level_ranks(counts, levels)
    table = slot_table(used, ranked, capacity)
    send_x = place_rows(table, tokens)
    send_g = place_rows(table, grad_out)
    recv_x, recv_g = (
        lax.all_to_all(send_x, "cuts", split_axis=0, concat_axis=0, tiled=True),
        lax.all_to_all(send_g, "cuts", split_axis=0, concat_axis=0, tiled=True),
    )
    full_x, full_g = (
        lax.all_gather(recv_x, "shard", axis=2, tiled=True),
        lax.all_gather(recv_g, "shard", axis=2, tiled=True),
    )
    width = full_x.shape[2]
    flat_x = full_x.reshape(levels * capacity, width)
    flat_g = full_g.reshape(levels * capacity, width)
    by_feature = (((1,), (1,)), ((), ()))
    by_row = (((0,), (0,)), ((), ()))
    gate = lax.dot_general(flat_x, gate_weight, by_feature, preferred_element_type=jnp.float32)
    upper = lax.dot_general(flat_x, up_weight, by_feature, preferred_element_type=jnp.float32)
    sigma = jax.nn.sigmoid(gate)
    hidden = (gate * sigma * upper).astype(jnp.bfloat16)
    dhidden = lax.dot_general(flat_g, down_weight, by_feature, preferred_element_type=jnp.float32)
    dgate = (dhidden * upper * sigma * (1.0 + gate * (1.0 - sigma))).astype(jnp.bfloat16)
    dup = (dhidden * gate * sigma).astype(jnp.bfloat16)
    grad_down = lax.dot_general(hidden, flat_g, by_row, preferred_element_type=jnp.float32).astype(
        jnp.bfloat16
    )
    grad_gate = lax.dot_general(dgate, flat_x, by_row, preferred_element_type=jnp.float32).astype(
        jnp.bfloat16
    )
    grad_up = lax.dot_general(dup, flat_x, by_row, preferred_element_type=jnp.float32).astype(
        jnp.bfloat16
    )
    terms = jnp.dot(dgate, gate_weight, preferred_element_type=jnp.float32)
    terms = terms + jnp.dot(dup, up_weight, preferred_element_type=jnp.float32)
    terms = terms.reshape(levels, capacity, width)
    shared = lax.psum_scatter(terms, "shard", scatter_dimension=2, tiled=True)
    back = lax.all_to_all(shared, "cuts", split_axis=0, concat_axis=0, tiled=True)
    grad_in = collect_rows(used, ranked, back)
    return (grad_in.astype(jnp.bfloat16), grad_gate, grad_up, grad_down)


def solution(mesh):
    return jax.shard_map(
        body,
        mesh=mesh,
        in_specs=(
            P("cuts", "shard"),
            P("cuts", "shard"),
            P("cuts"),
            P(("cuts", "shard"), None),
            P(("cuts", "shard"), None),
            P(("cuts", "shard"), None),
        ),
        out_specs=(
            P("cuts", "shard"),
            P(("cuts", "shard"), None),
            P(("cuts", "shard"), None),
            P(("cuts", "shard"), None),
        ),
        check_vma=False,
    )
```

profile of v0, /device:TPU:0, one launch (start us, length us, event | category | flops | bytes accessed | tf_op | source)
XLA Modules:
  0.0 344.0 jit_solution(7801491277427020563)
XLA Ops:
  7.2 0.0 copy-start
  7.2 0.0 all-gather.5.cloned.1.call-start
  7.2 0.7 fusion.11
  7.9 0.2 reduce_window_sum.11
  8.1 0.0 copy-done
  8.1 0.3 convolution_convert_fusion.3
  8.4 14.9 %all_to_all.15 = bf16[8,64,512]{2,1,0:T(8,128)(2,1)} all-to-all(bf16[8,64,512]{2,1,0:T(8,128)(2,1)S(1)} %convolution_convert_fusion.3), channel_id=1, replica_groups=mesh['cuts'=8,'shard'=16] {'cuts'}, dimensions={0} | all-to-all | bytes 1048576 | tf_op jit(solution)/shard_map/all_to_all | solution.py:40
  23.3 0.0 all-gather.5.cloned.1.call-update
  23.3 0.0 all-gather.3.cloned.1.call-start
  23.3 1.1 convolution_convert_fusion.4
  24.5 13.5 %all_to_all.16 = bf16[8,64,512]{2,1,0:T(8,128)(2,1)} all-to-all(bf16[8,64,512]{2,1,0:T(8,128)(2,1)S(1)} %convolution_convert_fusion.4), channel_id=1, replica_groups=mesh['cuts'=8,'shard'=16] {'cuts'}, dimensions={0} | all-to-all | bytes 1048576 | tf_op jit(solution)/shard_map/all_to_all | solution.py:41
  37.9 0.0 all-gather.3.cloned.1.call-update
  38.0 0.0 reduce-scatter.2.cloned.1.call-start
  38.0 64.3 %all-gather.5.cloned.1.call-done = bf16[8,64,8192]{2,1,0:T(8,128)(2,1)} async-done(((bf16[8,64,512]{2,1,0:T(8,128)(2,1)}), bf16[8,64,8192]{2,1,0:T(8,128)(2,1)}) %all-gather.5.cloned.1.call-update) | async-done | bytes 8388624 | tf_op jit(solution)/shard_map/all_gather | solution.py:44
  102.3 0.0 copy-start.2
  102.3 0.0 copy-start.4
  102.3 7.2 %fusion.15 = f32[512,224]{0,1:T(8,128)S(1)} fusion(bf16[512,8192]{1,0:T(8,128)(2,1)} %bitcast.30, bf16[224,8192]{1,0:T(8,128)(2,1)} %param.9), kind=kOutput, calls=%fused_computation.29 | convolution fusion | flops 1879048192 | bytes 12517376 | tf_op jit(solution)/shard_map/dot_general | solution.py:52
  109.5 0.0 copy-done.2
  109.5 0.6 copy-done.4
  110.1 2.7 fusion.14
  112.8 0.0 copy-start.5
  112.8 69.4 %all-gather.3.cloned.1.call-done = bf16[8,64,8192]{2,1,0:T(8,128)(2,1)} async-done(((bf16[8,64,512]{2,1,0:T(8,128)(2,1)}), bf16[8,64,8192]{2,1,0:T(8,128)(2,1)}) %all-gather.3.cloned.1.call-update) | async-done | bytes 8388624 | tf_op jit(solution)/shard_map/all_gather | solution.py:45
  182.2 0.0 copy-start.3
  182.2 7.4 %multiply_convert_fusion.1 = (bf16[512,224]{0,1:T(8,128)(2,1)S(1)}, bf16[512,224]{0,1:T(8,128)(2,1)S(1)}) fusion(f32[512,224]{0,1:T(8,128)S(1)} %fusion.15, f32[512,224]{0,1:T(8,128)S(1)} %fusion.14, bf16[512,8192]{1,0:T(8,128)(2,1)} %bitcast.35, bf16[224,8192]{1,0:T(8,128)(2,1)} %param.11), kind=kOutput, calls=%fused_computation.9 | convolution fusion | flops 1880539136 | bytes 13434880 | tf_op jit(solution)/shard_map/dot_general | solution.py:56
  189.5 0.0 copy-done.5
  189.6 0.0 copy-done.3
  189.6 2.4 fusion.16
  192.0 10.4 %convolution_add_fusion = f32[512,8192]{1,0:T(8,128)} fusion(f32[512,8192]{1,0:T(8,128)S(1)} %fusion.16, bf16[512,224]{0,1:T(8,128)(2,1)S(1)} %get-tuple-element.4, bf16[224,8192]{1,0:T(8,128)(2,1)} %param.10), kind=kOutput, calls=%fused_computation.1 | convolution fusion | flops 1883242496 | bytes 37453824 | tf_op jit(solution)/shard_map/dot_general | solution.py:69
  202.4 0.0 reduce-scatter.2.cloned.1.call-update
  202.4 0.1 reshape.75
  202.5 7.6 %convolution_convert_fusion.1 = bf16[224,8192]{1,0:T(8,128)(2,1)} fusion(bf16[512,224]{0,1:T(8,128)(2,1)S(1)} %get-tuple-element.4, bf16[512,8192]{1,0:T(8,128)(2,1)} %bitcast.31), kind=kOutput, calls=%fused_computation.3 | convolution fusion | flops 1880883200 | bytes 12288000 | tf_op jit(solution)/shard_map/dot_general | solution.py:65
  210.1 0.0 copy-start.6
  210.1 102.5 %reduce-scatter.2.cloned.1.call-done = f32[8,64,512]{2,1,0:T(8,128)} async-done(((f32[8,64,8192]{2,1,0:T(8,128)}), f32[8,64,512]{2,1,0:T(8,128)}) %reduce-scatter.2.cloned.1.call-update) | async-done | bytes 1048592 | tf_op jit(solution)/shard_map/reduce_scatter | solution.py:71
  312.5 4.2 %all-to-all-start.2 = ((f32[8,64,512]{2,1,0:T(8,128)}), f32[8,64,512]{2,1,0:T(8,128)S(1)}, u32[]{:S(2)}, u32[]{:S(2)}) async-start(f32[8,64,512]{2,1,0:T(8,128)} %reduce-scatter.2.cloned.1.call-done), calls=%async_computation.3 | async-start | bytes 2097152 | tf_op jit(solution)/shard_map/all_to_all | solution.py:72
  316.7 7.4 %convolution_convert_fusion.2 = bf16[224,8192]{1,0:T(8,128)(2,1)} fusion(bf16[512,224]{0,1:T(8,128)(2,1)S(1)} %get-tuple-element.5, bf16[512,8192]{1,0:T(8,128)(2,1)} %bitcast.32), kind=kOutput, calls=%fused_computation.4 | convolution fusion | flops 1880883200 | bytes 12288000 | tf_op jit(solution)/shard_map/dot_general | solution.py:62
  324.1 0.0 copy-done.6
  324.1 0.0 copy-start.1
  324.1 7.4 %convolution_convert_fusion = bf16[224,8192]{1,0:T(8,128)(2,1)} fusion(bf16[512,8192]{1,0:T(8,128)(2,1)} %bitcast.36, f32[512,224]{0,1:T(8,128)S(1)} %copy-done.6, f32[512,224]{0,1:T(8,128)S(1)} %fusion.15), kind=kOutput, calls=%fused_computation.2 | convolution fusion | flops 1881571328 | bytes 12976128 | tf_op jit(solution)/shard_map/dot_general | solution.py:59
  331.5 1.2 all-to-all-done.2
  332.7 4.0 %gather_fusion = f32[512,512]{1,0:T(8,128)S(1)} fusion(f32[8,64,512]{2,1,0:T(8,128)S(1)} %all-to-all-done.2, s32[512]{0:T(512)S(1)} %reshape.75), kind=kCustom, calls=%fused_computation | custom fusion | bytes 2101248 | tf_op jit(solution)/shard_map/vmap()/gather | solution.py:28
  336.7 0.8 multiply_reduce_fusion
  337.4 0.0 copy-done.1
  (2 shorter events, 0.0 us)
Async XLA Ops:
  7.2 1.0 copy-start
  7.2 95.1 %all-gather.5.cloned.1.call-start = ((), (), s32[]{:S(2)}) async-start(), calls=%async_computation.5 | async-start | bytes 8912896 | tf_op jit(solution)/shard_map/all_gather | solution.py:44
  23.3 158.9 %all-gather.3.cloned.1.call-start = ((), (), s32[]{:S(2)}) async-start(), calls=%async_computation.4 | async-start | bytes 8912896 | tf_op jit(solution)/shard_map/all_gather | solution.py:45
  38.0 274.6 %reduce-scatter.2.cloned.1.call-start = ((), (), s32[]{:S(2)}) async-start(), calls=%async_computation.6 | async-start | bytes 17825792 | tf_op jit(solution)/shard_map/reduce_scatter | solution.py:71
  102.3 7.3 %copy-start.2 = (bf16[8,64,8192]{2,1,0:T(8,128)(2,1)S(1)}, bf16[8,64,8192]{2,1,0:T(8,128)(2,1)}, u32[]{:S(2)}) copy-start(bf16[8,64,8192]{2,1,0:T(8,128)(2,1)} %all-gather.5.cloned.1.call-done) | copy-start | bytes 25165828
  102.3 7.9 %copy-start.4 = (bf16[224,8192]{1,0:T(8,128)(2,1)S(1)}, bf16[224,8192]{1,0:T(8,128)(2,1)}, u32[]{:S(2)}) copy-start(bf16[224,8192]{1,0:T(8,128)(2,1)} %param.10) | copy-start | bytes 11010052
  112.8 76.7 %copy-start.5 = (f32[512,224]{0,1:T(8,128)}, f32[512,224]{0,1:T(8,128)S(1)}, u32[]{:S(2)}) copy-start(f32[512,224]{0,1:T(8,128)S(1)} %fusion.14) | copy-start | bytes 1376260
  182.2 7.4 %copy-start.3 = (bf16[224,8192]{1,0:T(8,128)(2,1)S(1)}, bf16[224,8192]{1,0:T(8,128)(2,1)}, u32[]{:S(2)}) copy-start(bf16[224,8192]{1,0:T(8,128)(2,1)} %param.9) | copy-start | bytes 11010052
  210.1 114.1 %copy-start.6 = (f32[512,224]{0,1:T(8,128)S(1)}, f32[512,224]{0,1:T(8,128)}, u32[]{:S(2)}) copy-start(f32[512,224]{0,1:T(8,128)} %copy-done.5) | copy-start | bytes 1376260
  312.5 20.2 %all-to-all-start.2 = ((f32[8,64,512]{2,1,0:T(8,128)}), f32[8,64,512]{2,1,0:T(8,128)S(1)}, u32[]{:S(2)}, u32[]{:S(2)}) async-start(f32[8,64,512]{2,1,0:T(8,128)} %reduce-scatter.2.cloned.1.call-done), calls=%async_computation.3 | async-start | bytes 2097152 | tf_op jit(solution)/shard_map/all_to_all | solution.py:72
  324.1 13.3 %copy-start.1 = (bf16[64,512]{1,0:T(8,128)(2,1)S(1)}, bf16[64,512]{1,0:T(8,128)(2,1)}, u32[]{:S(2)}) copy-start(bf16[64,512]{1,0:T(8,128)(2,1)} %param.6) | copy-start | bytes 196612
Sparse Core Ops, SparseCore 0:
  23.4 78.8 all-gather.4
  104.4 77.7 all-gather.2
  202.5 109.9 reduce-scatter.1
where the time goes:
time: 345 us; the launch traced here: 344 us
  waiting for transfers between devices  237 us (69%)
  matrix products  53.8 us (16%)
  blocking collectives  28.3 us (8%)
  between operations  13.8 us (4%)
  local copies, waits for them, and re-layouts  4.67 us (1%)
  starting transfers between devices  4.32 us (1%)
    reduce_scatter x1, waiting for transfers between devices, body(): shared = lax.psum_scatter(terms, 'shard', scatter_dimension=2, tiled=True)  102 us
    all_gather x1, waiting for transfers between devices, body(): lax.all_gather(recv_g, 'shard', axis=2, tiled=True)  69.4 us
    all_gather x1, waiting for transfers between devices, body(): lax.all_gather(recv_x, 'shard', axis=2, tiled=True)  64.3 us
    all_to_all x1, blocking collectives, body(): lax.all_to_all(send_x, 'cuts', split_axis=0, concat_axis=0, tiled=True)  14.9 us
    all_to_all x1, blocking collectives, body(): lax.all_to_all(send_g, 'cuts', split_axis=0, concat_axis=0, tiled=True)  13.5 us
    dot_general x1, matrix products, body(): terms = terms + jnp.dot(dup, up_weight, preferred_element_type=jnp.float32)  10.4 us
    dot_general x1, matrix products, body(): lax.dot_general(dup, flat_x, by_row, preferred_element_type=jnp.float32)  7.58 us
    dot_general x1, matrix products, body(): lax.dot_general(dgate, flat_x, by_row, preferred_element_type=jnp.float32)  7.39 us
  transfers between devices with their start and end apart: 4, of which 4 were waited for; matrix products, arithmetic and copies ran while one was open for 10% of the time, Pallas kernels for 0%

commit v1 on v0

v1 whole, which is shorter than its diff:
```python
import functools

import jax
import jax.numpy as jnp
from jax import lax
from jax.experimental import pallas as pl
from jax.experimental.pallas import tpu as pltpu
from jax.sharding import PartitionSpec as P

F32 = jnp.float32
BF16 = jnp.bfloat16
NT = (((1,), (1,)), ((), ()))
NN = (((1,), (0,)), ((), ()))
SIDE = 4
BLOCK = 512


def dot(a, b, dims):
    return lax.dot_general(a, b, dims, preferred_element_type=F32)


def moves(axis, step):
    if axis == "x":
        return "shard", [(z * 4 + x, z * 4 + (x + step) % 4) for z in range(4) for x in range(4)]
    if axis == "z":
        return "shard", [(z * 4 + x, (z + step) % 4 * 4 + x) for z in range(4) for x in range(4)]
    if axis == "y":
        return "cuts", [(y * 2 + c, (y + step) % 4 * 2 + c) for y in range(4) for c in range(2)]
    return "cuts", [(y * 2 + c, y * 2 + 1 - c) for y in range(4) for c in range(2)]


def shift(value, axis, step=1):
    name, pairs = moves(axis, step)
    return lax.ppermute(value, name, pairs)


def forward_kernel(rel, x_ref, g_ref, wg_ref, wu_ref, wd_ref, keep_ref, ht_ref, dgt_ref, dut_ref, dg_ref, du_ref, gate, up, dh, rows):
    step = pl.program_id(0)

    @pl.when(step == 0)
    def _():
        gate[...] = jnp.zeros_like(gate)
        up[...] = jnp.zeros_like(up)
        dh[...] = jnp.zeros_like(dh)

    for k in range(x_ref.shape[1]):
        cols = slice(k * BLOCK, (k + 1) * BLOCK)
        x = x_ref[:, k].reshape(512, BLOCK)
        g = g_ref[:, k].reshape(512, BLOCK)
        gate[...] += dot(wg_ref[:, cols], x, NT)
        up[...] += dot(wu_ref[:, cols], x, NT)
        dh[...] += dot(wd_ref[:, cols], g, NT)

    @pl.when(step == pl.num_programs(0) - 1)
    def _():
        keep = keep_ref[...]
        gv = gate[...]
        sig = 1.0 / (1.0 + jnp.exp(-gv))
        silu = gv * sig
        dhv = dh[...] * keep
        uv = up[...]
        ht_ref[...] = (silu * uv * keep).astype(BF16)
        dg = dhv * uv * sig * (1.0 + gv * (1.0 - sig))
        du = dhv * silu
        dgt_ref[...] = dg.astype(BF16)
        dut_ref[...] = du.astype(BF16)
        for value, out in ((dg, dg_ref), (du, du_ref)):
            rows[...] = value.T.astype(BF16).reshape(8, 64, 224)
            for r in range(8):
                out[r // 4, :, r % 4] = rows[rel[r]].reshape(2, 32, 224)


def forward(rel, both, wg, wu, wd, keep):
    width = 1024
    per = width // BLOCK
    wspec = pl.BlockSpec((224, width), lambda s, rel: (0, s))
    tspec = pl.BlockSpec((224, 512), lambda s, rel: (0, 0))
    dspec = pl.BlockSpec((2, 2, 4, 32, 224), lambda s, rel: (0, 0, 0, 0, 0))
    return pl.pallas_call(
        forward_kernel,
        grid_spec=pltpu.PrefetchScalarGridSpec(
            num_scalar_prefetch=1,
            grid=(8192 // width,),
            in_specs=[
                pl.BlockSpec((8, per, 64, BLOCK), lambda s, rel: (0, s, 0, 0)),
                pl.BlockSpec((8, per, 64, BLOCK), lambda s, rel: (0, s, 1, 0)),
                wspec, wspec, wspec,
                pl.BlockSpec((1, 512), lambda s, rel: (0, 0)),
            ],
            out_specs=[tspec, tspec, tspec, dspec, dspec],
            scratch_shapes=[pltpu.VMEM((224, 512), F32)] * 3 + [pltpu.VMEM((8, 64, 224), BF16)],
        ),
        out_shape=[jax.ShapeDtypeStruct((224, 512), BF16)] * 3
        + [jax.ShapeDtypeStruct((2, 2, 4, 32, 224), BF16)] * 2,
        compiler_params=pltpu.CompilerParams(vmem_limit_bytes=48 * 2**20),
        cost_estimate=pl.CostEstimate(flops=6 * 512 * 224 * 8192, bytes_accessed=28 * 2**20, transcendentals=512 * 224),
    )(rel, both, both, wg, wu, wd, keep)


def weight_grad_kernel(x_ref, g_ref, ht_ref, dgt_ref, dut_ref, gg_ref, gu_ref, gd_ref):
    for k in range(x_ref.shape[1]):
        cols = slice(k * BLOCK, (k + 1) * BLOCK)
        x = x_ref[:, k].reshape(512, BLOCK)
        g = g_ref[:, k].reshape(512, BLOCK)
        gg_ref[:, cols] = dot(dgt_ref[...], x, NN).astype(BF16)
        gu_ref[:, cols] = dot(dut_ref[...], x, NN).astype(BF16)
        gd_ref[:, cols] = dot(ht_ref[...], g, NN).astype(BF16)


def weight_grads(both, ht, dgt, dut):
    width = 1024
    per = width // BLOCK
    wspec = pl.BlockSpec((224, width), lambda s: (0, s))
    tspec = pl.BlockSpec((224, 512), lambda s: (0, 0))
    return pl.pallas_call(
        weight_grad_kernel,
        grid=(8192 // width,),
        in_specs=[
            pl.BlockSpec((8, per, 64, BLOCK), lambda s: (0, s, 0, 0)),
            pl.BlockSpec((8, per, 64, BLOCK), lambda s: (0, s, 1, 0)),
            tspec, tspec, tspec,
        ],
        out_specs=[wspec] * 3,
        out_shape=[jax.ShapeDtypeStruct((224, 8192), BF16)] * 3,
        compiler_params=pltpu.CompilerParams(vmem_limit_bytes=48 * 2**20),
        cost_estimate=pl.CostEstimate(flops=6 * 512 * 224 * 8192, bytes_accessed=28 * 2**20, transcendentals=0),
    )(both, both, ht, dgt, dut)


def partner_kernel(tab, dg_ref, du_ref, wg_ref, wu_ref, p_ref, q_ref):
    dg = dg_ref[0].reshape(256, 224)
    du = du_ref[0].reshape(256, 224)
    for dx in range(SIDE):
        cols = pl.ds(pl.multiple_of(tab[4 + dx] * BLOCK, BLOCK), BLOCK)
        total = dot(dg, wg_ref[:, cols], NN) + dot(du, wu_ref[:, cols], NN)
        p_ref[dx, 0] = total[:128].astype(BF16)
        q_ref[0, dx] = total[128:].astype(BF16)


def partner_terms(tab, dg, du, wg, wu):
    dspec = pl.BlockSpec((1, 2, 4, 32, 224), lambda dz, tab: (1, 0, 0, 0, 0))
    wspec = pl.BlockSpec((224, 4 * BLOCK), lambda dz, tab: (0, tab[dz]))
    return pl.pallas_call(
        partner_kernel,
        grid_spec=pltpu.PrefetchScalarGridSpec(
            num_scalar_prefetch=1,
            grid=(SIDE,),
            in_specs=[dspec, dspec, wspec, wspec],
            out_specs=[
                pl.BlockSpec((4, 1, 128, BLOCK), lambda dz, tab: (0, dz, 0, 0)),
                pl.BlockSpec((1, 4, 128, BLOCK), lambda dz, tab: (dz, 0, 0, 0)),
            ],
        ),
        out_shape=[jax.ShapeDtypeStruct((4, 4, 128, BLOCK), BF16)] * 2,
        compiler_params=pltpu.CompilerParams(vmem_limit_bytes=48 * 2**20),
        cost_estimate=pl.CostEstimate(flops=4 * 256 * 224 * 8192, bytes_accessed=12 * 2**20, transcendentals=0),
    )(tab, dg, du, wg, wu)


def own_kernel(by_x, tab, dg_ref, du_ref, wg_ref, wu_ref, add_ref, *outs):
    dz = pl.program_id(0)
    dg = dg_ref[0].reshape(128, 224)
    du = du_ref[0].reshape(128, 224)
    for dx in range(SIDE):
        cols = pl.ds(pl.multiple_of(tab[4 + dx] * BLOCK, BLOCK), BLOCK)
        total = dot(dg, wg_ref[:, cols], NN) + dot(du, wu_ref[:, cols], NN)
        if by_x:
            outs[dx][0] = (total + add_ref[dx, 0].astype(F32)).astype(BF16)
        else:
            done = (total + add_ref[0, dx].astype(F32)).astype(BF16)
            for k in range(SIDE):
                @pl.when(dz == k)
                def _(k=k, done=done, dx=dx):
                    outs[k][dx] = done


def own_terms(by_x, tab, dg, du, wg, wu, add):
    half = 0 if by_x else 1
    dspec = pl.BlockSpec((1, 1, 4, 32, 224), lambda dz, tab: (0, half, 0, 0, 0))
    wspec = pl.BlockSpec((224, 4 * BLOCK), lambda dz, tab: (0, tab[dz]))
    if by_x:
        aspec = pl.BlockSpec((4, 1, 128, BLOCK), lambda dz, tab: (0, dz, 0, 0))
        ospec = pl.BlockSpec((1, 128, BLOCK), lambda dz, tab: (dz, 0, 0))
    else:
        aspec = pl.BlockSpec((1, 4, 128, BLOCK), lambda dz, tab: (dz, 0, 0, 0))
        ospec = pl.BlockSpec((4, 128, BLOCK), lambda dz, tab: (0, 0, 0))
    return pl.pallas_call(
        functools.partial(own_kernel, by_x),
        grid_spec=pltpu.PrefetchScalarGridSpec(
            num_scalar_prefetch=1,
            grid=(SIDE,),
            in_specs=[dspec, dspec, wspec, wspec, aspec],
            out_specs=[ospec] * 4,
        ),
        out_shape=[jax.ShapeDtypeStruct((4, 128, BLOCK), BF16)] * 4,
        compiler_params=pltpu.CompilerParams(vmem_limit_bytes=48 * 2**20),
        cost_estimate=pl.CostEstimate(flops=4 * 128 * 224 * 8192, bytes_accessed=12 * 2**20, transcendentals=0),
    )(tab, dg, du, wg, wu, add)


def sum_kernel(a, b, c, d, *outs):
    for k in range(SIDE):
        outs[k][...] = (
            (a[k].astype(F32) + b[k].astype(F32)) + (c[k].astype(F32) + d[k].astype(F32))
        ).astype(BF16)


def sum_apart(parts):
    return pl.pallas_call(
        sum_kernel,
        out_shape=[jax.ShapeDtypeStruct((128, BLOCK), BF16)] * 4,
        cost_estimate=pl.CostEstimate(flops=3 * 4 * 128 * 512, bytes_accessed=5 * 2**19, transcendentals=0),
    )(*parts)


def join_kernel(*refs):
    ins, outs = refs[:8], refs[8:]
    for h in range(2):
        total = (ins[4 * h][...].astype(F32) + ins[4 * h + 1][...].astype(F32)) + (
            ins[4 * h + 2][...].astype(F32) + ins[4 * h + 3][...].astype(F32)
        )
        for k in range(SIDE):
            outs[k][h * 32:(h + 1) * 32] = total[k * 32:(k + 1) * 32].astype(BF16)


def join_apart(first, second):
    return pl.pallas_call(
        join_kernel,
        out_shape=[jax.ShapeDtypeStruct((64, BLOCK), BF16)] * 4,
        cost_estimate=pl.CostEstimate(flops=2**19, bytes_accessed=5 * 2**18, transcendentals=0),
    )(*first, *second)


def exchange(pieces, axis):
    return [pieces[0]] + [shift(pieces[d], axis, d) for d in (1, 3, 2)]


def body(tokens, grad_out, counts, gate_weight, up_weight, down_weight):
    c = lax.axis_index("cuts")
    s = lax.axis_index("shard")
    y, core, z, x = c // 2, c % 2, s // 4, s % 4
    step = jnp.arange(SIDE, dtype=jnp.int32)
    near = (y + step) % 4 * 2
    rel = jnp.concatenate([near + core, near + 1 - core]).astype(jnp.int32)
    tab = jnp.concatenate([(z + step) % 4, (x + step) % 4]).astype(jnp.int32)

    both = lax.all_gather(jnp.concatenate([tokens, grad_out], 0), ("cuts", "shard"), tiled=False)
    both = both.reshape(8, 16, 128, BLOCK)
    all_counts = lax.all_gather(counts, "cuts", tiled=True)
    keep = (all_counts > c).astype(F32).reshape(1, 512)

    ht, dgt, dut, dg, du = forward(rel, both, gate_weight, up_weight, down_weight, keep)
    first, second = partner_terms(tab, dg, du, gate_weight, up_weight)
    first, second = shift(first, "core"), shift(second, "core")
    first = own_terms(True, tab, dg, du, gate_weight, up_weight, first)
    second = own_terms(False, tab, dg, du, gate_weight, up_weight, second)
    first = exchange(first, "x")
    second = exchange(second, "z")
    grad_gate, grad_up, grad_down = weight_grads(both, ht, dgt, dut)
    first = exchange(sum_apart(first), "z")
    second = exchange(sum_apart(second), "x")
    parts = exchange(join_apart(first, second), "y")
    total = (parts[0].astype(F32) + parts[1].astype(F32)) + (parts[2].astype(F32) + parts[3].astype(F32))
    return (total.astype(BF16), grad_gate, grad_up, grad_down)


def solution(mesh):
    return jax.shard_map(
        body,
        mesh=mesh,
        in_specs=(
            P("cuts", "shard"),
            P("cuts", "shard"),
            P("cuts"),
            P(("cuts", "shard"), None),
            P(("cuts", "shard"), None),
            P(("cuts", "shard"), None),
        ),
        out_specs=(
            P("cuts", "shard"),
            P(("cuts", "shard"), None),
            P(("cuts", "shard"), None),
            P(("cuts", "shard"), None),
        ),
        check_vma=False,
    )
```

time: 345 us -> 212 us (0.61)
  waiting for transfers between devices: 237 us -> 96 us
  matrix products: 53.8 us -> 0 us
  Pallas kernels: 0 us -> 53.1 us
  starting transfers between devices: 4.32 us -> 26.2 us
  blocking collectives: 28.3 us -> 9.56 us
    reduce_scatter x1 -> x0, waiting for transfers between devices: 102 us -> none  [body(): shared = lax.psum_scatter(terms, 'shard', scatter_dimension=2, tiled=True)]
    all_gather x2 -> x1, waiting for transfers between devices: 134 us -> 73.2 us  [body(): lax.all_gather(jnp.concatenate([tokens, grad_out], 0), ('cuts', 'shard'),...]
    dot_general x10 -> x0, matrix products: 53.8 us -> none  [the longest x1 10.4 us: body(): terms = terms + jnp.dot(dup, up_weight, preferred_element_type=jnp.float32)]
    pallas_call x0 -> x8, Pallas kernels: none -> 53.1 us  [the longest x1 14.2 us: weight_grads(): pl.pallas_call(weight_grad_kernel, grid=(8192 // width,), in_specs=[pl.Bl...]
    all_to_all x2 -> x0, blocking collectives: 28.3 us -> none  [the longest x1 14.9 us: body(): lax.all_to_all(send_x, 'cuts', split_axis=0, concat_axis=0, tiled=True)]
    ppermute x0 -> x17, starting transfers between devices: none -> 26.2 us  [shift(): return lax.ppermute(value, name, pairs)]
    ppermute x0 -> x17, waiting for transfers between devices: none -> 22.8 us  [shift(): return lax.ppermute(value, name, pairs)]
    unnamed x0 -> x1, blocking collectives: none -> 9.56 us
  transfers between devices with their start and end apart: 4 -> 18, of which waited for: 4 -> 9; matrix products, arithmetic and copies ran while one was open for 10% -> 1% of each run, Pallas kernels for 0% -> 15%
where the time goes in v1:
time: 212 us; the launch traced here: 210 us
  waiting for transfers between devices  96 us (45%)
  Pallas kernels  53.1 us (25%)
  starting transfers between devices  26.2 us (12%)
  between operations  14.9 us (7%)
  blocking collectives  9.56 us (5%)
  local copies, waits for them, and re-layouts  7.94 us (4%)
  other arithmetic  2.38 us (1%)
    all_gather x1, waiting for transfers between devices, body(): lax.all_gather(jnp.concatenate([tokens, grad_out], 0), ('cuts', 'shard'),...  73.2 us
    ppermute x17, starting transfers between devices, shift(): return lax.ppermute(value, name, pairs)  26.2 us
    ppermute x17, waiting for transfers between devices, shift(): return lax.ppermute(value, name, pairs)  22.8 us
    pallas_call x1, Pallas kernels, weight_grads(): pl.pallas_call(weight_grad_kernel, grid=(8192 // width,), in_specs=[pl.Bl...  14.2 us
    pallas_call x1, Pallas kernels, forward(): pl.pallas_call(forward_kernel, grid_spec=pltpu.PrefetchScalarGridSpec(num...  14.2 us
    pallas_call x2, Pallas kernels, own_terms(): pl.pallas_call(functools.partial(own_kernel, by_x), grid_spec=pltpu.Prefe...  11.8 us
    unnamed x1, blocking collectives  9.56 us
    unnamed x31, local copies, waits for them, and re-layouts  7.94 us
  transfers between devices with their start and end apart: 18, of which 9 were waited for; matrix products, arithmetic and copies ran while one was open for 1% of the time, Pallas kernels for 15%

profile of v1, /device:TPU:0, one launch (start us, length us, event | category | flops | bytes accessed | tf_op | source)
XLA Modules:
  0.0 210.1 jit_solution(5249157556143275259)
XLA Ops:
  7.2 0.0 all-gather.3.cloned.1.call-start
  7.2 1.5 pad_maximum_fusion
  8.7 0.0 all-gather.3.cloned.1.call-update
  8.8 1.2 dynamic-slice
  10.7 0.9 dynamic-update-slice
  11.6 9.6 %all-reduce = s32[512]{0:T(512)S(1)} all-reduce(s32[512]{0:T(512)S(1)} %dynamic-update-slice), channel_id=1, replica_groups=mesh['cuts'=8,'shard'=16] {'cuts'}, use_global_device_ids=true, to_apply=%add | all-reduce | flops 512 | bytes 4096
  21.2 0.1 pad_add_fusion.1.rel
  21.2 0.1 pad_add_fusion.tab
  21.3 73.2 %all-gather.3.cloned.1.call-done = bf16[16384,512]{1,0:T(8,128)(2,1)} async-done(((bf16[128,512]{1,0:T(8,128)(2,1)}), bf16[16384,512]{1,0:T(8,128)(2,1)}) %all-gather.3.cloned.1.call-update) | async-done | bytes 16777232 | tf_op jit(solution)/shard_map/all_gather | solution.py:247
  94.5 2.0 copy-done
  96.6 14.2 %shard_map.93 = (bf16[224,512]{1,0:T(8,128)(2,1)S(1)}, bf16[224,512]{1,0:T(8,128)(2,1)S(1)}, bf16[224,512]{1,0:T(8,128)(2,1)S(1)}, bf16[2,2,4,32,224]{4,3,2,1,0:...) custom-call(s32[8]{0:T(128)S(1)} %pad_add_fusion.1.rel, bf16[8,16,128,512]{3,2,1,0:T(8,128)(2,1)} %bitcast.4, ...), custom_call_target="tpu_custom_call" | custom-call | flops 5637144576 | bytes 29360128 | tf_op jit(solution)/shard_map/pallas_call | solution.py:79
  110.8 5.9 %shard_map.94 = (bf16[4,4,128,512]{3,2,1,0:T(8,128)(2,1)S(1)}, bf16[4,4,128,512]{3,2,1,0:T(8,128)(2,1)S(1)}) custom-call(s32[8]{0:T(128)S(1)} %pad_add_fusion.tab, bf16[2,2,4,32,224]{4,3,2,1,0:T(8,128)(2,1)S(1)} %get-tuple-element.34.dg_ref, bf16[2,2,4,32,224]{4,3,2,1,0:T(8,128)(2,1)S(1)} %get-tuple-element.35.du_ref, bf16[224,8192]{1,0:T(8,128)(2,1)} %wg_ref.7, ...), custom_call_target="tpu_custom_call" | custom-call | flops 1879048192 | bytes 12582912 | tf_op jit(solution)/shard_map/pallas_call | solution.py:143
  116.7 0.3 collective-permute-start.7
  117.1 0.3 collective-permute-start
  117.3 3.6 %collective-permute-done.7.add_ref = bf16[4,4,128,512]{3,2,1,0:T(8,128)(2,1)S(1)} collective-permute-done((bf16[4,4,128,512]{3,2,1,0:T(8,128)(2,1)S(1)}, bf16[4,4,128,512]{3,2,1,0:T(8,128)(2,1)S(1)}, u32[]{:S(2)}, u32[]{:S(2)}) %collective-permute-start.7) | collective-permute-done | bytes 2097184 | tf_op jit(solution)/shard_map/ppermute | solution.py:34
  121.0 6.6 %shard_map.97 = (bf16[4,128,512]{2,1,0:T(8,128)(2,1)S(1)}, bf16[4,128,512]{2,1,0:T(8,128)(2,1)S(1)}, bf16[4,128,512]{2,1,0:T(8,128)(2,1)S(1)}, bf16[4,128,512]{2,1,0:T(8,128)(2,1)S(1)}) custom-call(s32[8]{0:T(128)S(1)} %pad_add_fusion.tab, bf16[2,2,4,32,224]{4,3,2,1,0:T(8,128)(2,1)S(1)} %get-tuple-element.34.dg_ref, ...), custom_call_target="tpu_custom_call" | custom-call | flops 939524096 | bytes 12582912 | tf_op jit(solution)/shard_map/pallas_call | solution.py:187
  127.6 0.0 copy-start.2
  127.6 0.8 copy-done.2
  128.4 2.7 %collective-permute-start.10 = (bf16[4,128,512]{2,1,0:T(8,128)(2,1)S(1)}, bf16[4,128,512]{2,1,0:T(8,128)(2,1)S(1)}, u32[]{:S(2)}, u32[]{:S(2)}) collective-permute-start(bf16[4,128,512]{2,1,0:T(8,128)(2,1)S(1)} %get-tuple-element.49), channel_id=1, source_target_pairs={{0,8},{1,9},{2,10},{3,11},{4,12},{5,13},{6,14},{7,15},{8,0},{9,1},... | collective-permute-start | bytes 1572872 | tf_op jit(solution)/shard_map/ppermute | solution.py:34
  131.1 0.7 collective-permute-start.8
  131.7 2.6 %collective-permute-start.9 = (bf16[4,128,512]{2,1,0:T(8,128)(2,1)S(1)}, bf16[4,128,512]{2,1,0:T(8,128)(2,1)S(1)}, u32[]{:S(2)}, u32[]{:S(2)}) collective-permute-start(bf16[4,128,512]{2,1,0:T(8,128)(2,1)S(1)} %get-tuple-element.48), channel_id=1, source_target_pairs={{0,12},{1,13},{2,14},{3,15},{4,0},{5,1},{6,2},{7,3},{8,4},{9,5},{1... | collective-permute-start | bytes 1572872 | tf_op jit(solution)/shard_map/ppermute | solution.py:34
  134.3 0.0 collective-permute-done.add_ref
  134.3 5.2 %shard_map.95 = (bf16[4,128,512]{2,1,0:T(8,128)(2,1)S(1)}, bf16[4,128,512]{2,1,0:T(8,128)(2,1)S(1)}, bf16[4,128,512]{2,1,0:T(8,128)(2,1)S(1)}, bf16[4,128,512]{2,1,0:T(8,128)(2,1)S(1)}) custom-call(s32[8]{0:T(128)S(1)} %pad_add_fusion.tab, bf16[2,2,4,32,224]{4,3,2,1,0:T(8,128)(2,1)S(1)} %get-tuple-element.34.dg_ref, ...), custom_call_target="tpu_custom_call" | custom-call | flops 939524096 | bytes 12582912 | tf_op jit(solution)/shard_map/pallas_call | solution.py:187
  139.5 0.0 copy-start.1
  139.5 0.8 copy-done.1
  140.3 0.8 collective-permute-start.1
  141.1 2.5 %collective-permute-start.2 = (bf16[4,128,512]{2,1,0:T(8,128)(2,1)S(1)}, bf16[4,128,512]{2,1,0:T(8,128)(2,1)S(1)}, u32[]{:S(2)}, u32[]{:S(2)}) collective-permute-start(bf16[4,128,512]{2,1,0:T(8,128)(2,1)S(1)} %get-tuple-element.39), channel_id=1, source_target_pairs={{0,3},{1,0},{2,1},{3,2},{4,7},{5,4},{6,5},{7,6},{8,11},{9,8},{10,9... | collective-permute-start | bytes 1572872 | tf_op jit(solution)/shard_map/ppermute | solution.py:34
  143.5 1.2 collective-permute-done.10.d
  144.7 3.0 %collective-permute-start.3 = (bf16[4,128,512]{2,1,0:T(8,128)(2,1)S(1)}, bf16[4,128,512]{2,1,0:T(8,128)(2,1)}, u32[]{:S(2)}, u32[]{:S(2)}) collective-permute-start(bf16[4,128,512]{2,1,0:T(8,128)(2,1)S(1)} %get-tuple-element.40), channel_id=1, source_target_pairs={{0,2},{1,3},{2,0},{3,1},{4,6},{5,7},{6,4},{7,5},{8,10},{9,11},{10,... | collective-permute-start | bytes 1572872 | tf_op jit(solution)/shard_map/ppermute | solution.py:34
  147.7 7.6 %collective-permute-done.8.b = bf16[4,128,512]{2,1,0:T(8,128)(2,1)S(1)} collective-permute-done((bf16[4,128,512]{2,1,0:T(8,128)(2,1)S(1)}, bf16[4,128,512]{2,1,0:T(8,128)(2,1)S(1)}, u32[]{:S(2)}, u32[]{:S(2)}) %collective-permute-start.8) | collective-permute-done | bytes 524320 | tf_op jit(solution)/shard_map/ppermute | solution.py:34
  155.2 0.0 collective-permute-done.9.c
  155.2 0.0 copy-done.5
  155.2 0.8 copy-done.6
  156.0 0.8 copy-done.7
  156.8 2.4 %shard_map.98 = (bf16[128,512]{1,0:T(8,128)(2,1)}, bf16[128,512]{1,0:T(8,128)(2,1)}, bf16[128,512]{1,0:T(8,128)(2,1)}, bf16[128,512]{1,0:T(8,128)(2,1)}) custom-call(bf16[4,128,512]{2,1,0:T(8,128)(2,1)} %copy-done.2, bf16[4,128,512]{2,1,0:T(8,128)(2,1)} %copy-done.6, bf16[4,128,512]{2,1,0:T(8,128)(2,1)} %copy-done.7, bf16[4,128,512]{2,1,0:T(8,128)(2,1)} %copy-done.5), custom_call_target="tpu_custom_call" | custom-call | flops 786432 | bytes 2621440 | tf_op jit(solution)/shard_map/pallas_call | solution.py:209
  159.2 1.5 collective-permute-start.11
  160.7 1.8 collective-permute-start.12
  162.5 0.0 collective-permute-done.1.b
  162.5 1.8 collective-permute-start.13
  164.2 1.6 collective-permute-done.2.c
  165.9 2.1 %collective-permute-done.3.d = bf16[4,128,512]{2,1,0:T(8,128)(2,1)} collective-permute-done((bf16[4,128,512]{2,1,0:T(8,128)(2,1)S(1)}, bf16[4,128,512]{2,1,0:T(8,128)(2,1)}, u32[]{:S(2)}, u32[]{:S(2)}) %collective-permute-start.3) | collective-permute-done | bytes 524320 | tf_op jit(solution)/shard_map/ppermute | solution.py:34
  168.0 0.0 copy-done.3
  168.0 2.4 %shard_map.96 = (bf16[128,512]{1,0:T(8,128)(2,1)}, bf16[128,512]{1,0:T(8,128)(2,1)}, bf16[128,512]{1,0:T(8,128)(2,1)}, bf16[128,512]{1,0:T(8,128)(2,1)}) custom-call(bf16[4,128,512]{2,1,0:T(8,128)(2,1)} %copy-done.1, bf16[4,128,512]{2,1,0:T(8,128)(2,1)} %copy-done.3, bf16[4,128,512]{2,1,0:T(8,128)(2,1)} %copy-done.4, ...), custom_call_target="tpu_custom_call" | custom-call | flops 786432 | bytes 2621440 | tf_op jit(solution)/shard_map/pallas_call | solution.py:209
  170.4 0.0 collective-permute-start.4
  170.4 3.2 %collective-permute-start.5 = (bf16[128,512]{1,0:T(8,128)(2,1)}, bf16[128,512]{1,0:T(8,128)(2,1)S(1)}, u32[]{:S(2)}, u32[]{:S(2)}) collective-permute-start(bf16[128,512]{1,0:T(8,128)(2,1)} %get-tuple-element.43), channel_id=1, source_target_pairs={{0,12},{1,13},{2,14},{3,15},{4,0},{5,1},{6,2},{7,3},{8,4},{9,5},{1... | collective-permute-start | bytes 393224 | tf_op jit(solution)/shard_map/ppermute | solution.py:34
  173.6 0.0 collective-permute-done.11.refs_5_
  173.6 0.0 collective-permute-start.6
  173.6 0.0 collective-permute-done.12.refs_6_
  173.7 0.0 collective-permute-done.13.refs_7_
  173.7 3.9 %collective-permute-done.4.refs_1_ = bf16[128,512]{1,0:T(8,128)(2,1)S(1)} collective-permute-done((bf16[128,512]{1,0:T(8,128)(2,1)}, bf16[128,512]{1,0:T(8,128)(2,1)S(1)}, u32[]{:S(2)}, u32[]{:S(2)}) %collective-permute-start.4) | collective-permute-done | bytes 131104 | tf_op jit(solution)/shard_map/ppermute | solution.py:34
  177.5 0.3 collective-permute-done.5.refs_2_
  177.9 2.4 %collective-permute-done.6.refs_3_ = bf16[128,512]{1,0:T(8,128)(2,1)S(1)} collective-permute-done((bf16[128,512]{1,0:T(8,128)(2,1)}, bf16[128,512]{1,0:T(8,128)(2,1)S(1)}, u32[]{:S(2)}, u32[]{:S(2)}) %collective-permute-start.6) | collective-permute-done | bytes 131104 | tf_op jit(solution)/shard_map/ppermute | solution.py:34
  180.3 0.0 copy-done.9
  180.3 0.6 copy-done.12
  181.0 2.1 shard_map.99
  183.0 1.7 collective-permute-start.14
  184.7 1.5 collective-permute-start.15
  186.3 2.0 collective-permute-start.16
  188.3 14.2 %shard_map.100 = (bf16[224,8192]{1,0:T(8,128)(2,1)}, bf16[224,8192]{1,0:T(8,128)(2,1)}, bf16[224,8192]{1,0:T(8,128)(2,1)}) custom-call(bf16[8,16,128,512]{3,2,1,0:T(8,128)(2,1)} %bitcast.6, bf16[8,16,128,512]{3,2,1,0:T(8,128)(2,1)} %bitcast.7, bf16[224,512]{1,0:T(8,128)(2,1)S(1)} %get-tuple-element.58.ht_ref, ...), custom_call_target="tpu_custom_call" | custom-call | flops 5637144576 | bytes 29360128 | tf_op jit(solution)/shard_map/pallas_call | solution.py:115
  202.5 0.0 collective-permute-done.14
  202.5 0.0 collective-permute-done.15
  202.5 0.0 collective-permute-done.16
  202.5 0.0 copy-done.13
  202.5 0.7 add_convert_fusion
  (20 shorter events, 0.1 us)
Async XLA Ops:
  7.2 87.4 %all-gather.3.cloned.1.call-start = ((), (), s32[]{:S(2)}) async-start(), calls=%async_computation | async-start | bytes 16908288 | tf_op jit(solution)/shard_map/all_gather | solution.py:247
  94.5 2.0 copy-start
  116.7 4.2 %collective-permute-start.7 = (bf16[4,4,128,512]{3,2,1,0:T(8,128)(2,1)S(1)}, bf16[4,4,128,512]{3,2,1,0:T(8,128)(2,1)S(1)}, u32[]{:S(2)}, u32[]{:S(2)}) collective-permute-start(bf16[4,4,128,512]{3,2,1,0:T(8,128)(2,1)S(1)} %get-tuple-element.45), channel_id=1, source_target_pairs={{0,16},{16,0},{32,48},{48,32},{64,80},{80,64},{96,112},{112,96},{1... | collective-permute-start | bytes 6291464 | tf_op jit(solution)/shard_map/ppermute | solution.py:34
  117.1 17.2 %collective-permute-start = (bf16[4,4,128,512]{3,2,1,0:T(8,128)(2,1)S(1)}, bf16[4,4,128,512]{3,2,1,0:T(8,128)(2,1)S(1)}, u32[]{:S(2)}, u32[]{:S(2)}) collective-permute-start(bf16[4,4,128,512]{3,2,1,0:T(8,128)(2,1)S(1)} %get-tuple-element.36), channel_id=1, source_target_pairs={{0,16},{16,0},{32,48},{48,32},{64,80},{80,64},{96,112},{112,96},{1... | collective-permute-start | bytes 6291464 | tf_op jit(solution)/shard_map/ppermute | solution.py:34
  127.6 0.8 copy-start.2
  128.4 16.3 %collective-permute-start.10 = (bf16[4,128,512]{2,1,0:T(8,128)(2,1)S(1)}, bf16[4,128,512]{2,1,0:T(8,128)(2,1)S(1)}, u32[]{:S(2)}, u32[]{:S(2)}) collective-permute-start(bf16[4,128,512]{2,1,0:T(8,128)(2,1)S(1)} %get-tuple-element.49), channel_id=1, source_target_pairs={{0,8},{1,9},{2,10},{3,11},{4,12},{5,13},{6,14},{7,15},{8,0},{9,1},... | collective-permute-start | bytes 1572872 | tf_op jit(solution)/shard_map/ppermute | solution.py:34
  131.1 24.2 %collective-permute-start.8 = (bf16[4,128,512]{2,1,0:T(8,128)(2,1)S(1)}, bf16[4,128,512]{2,1,0:T(8,128)(2,1)S(1)}, u32[]{:S(2)}, u32[]{:S(2)}) collective-permute-start(bf16[4,128,512]{2,1,0:T(8,128)(2,1)S(1)} %get-tuple-element.47), channel_id=1, source_target_pairs={{0,4},{1,5},{2,6},{3,7},{4,8},{5,9},{6,10},{7,11},{8,12},{9,13},{1... | collective-permute-start | bytes 1572872 | tf_op jit(solution)/shard_map/ppermute | solution.py:34
  131.7 23.5 %collective-permute-start.9 = (bf16[4,128,512]{2,1,0:T(8,128)(2,1)S(1)}, bf16[4,128,512]{2,1,0:T(8,128)(2,1)S(1)}, u32[]{:S(2)}, u32[]{:S(2)}) collective-permute-start(bf16[4,128,512]{2,1,0:T(8,128)(2,1)S(1)} %get-tuple-element.48), channel_id=1, source_target_pairs={{0,12},{1,13},{2,14},{3,15},{4,0},{5,1},{6,2},{7,3},{8,4},{9,5},{1... | collective-permute-start | bytes 1572872 | tf_op jit(solution)/shard_map/ppermute | solution.py:34
  139.5 0.8 copy-start.1
  140.3 22.2 %collective-permute-start.1 = (bf16[4,128,512]{2,1,0:T(8,128)(2,1)S(1)}, bf16[4,128,512]{2,1,0:T(8,128)(2,1)S(1)}, u32[]{:S(2)}, u32[]{:S(2)}) collective-permute-start(bf16[4,128,512]{2,1,0:T(8,128)(2,1)S(1)} %get-tuple-element.38), channel_id=1, source_target_pairs={{0,1},{1,2},{2,3},{3,0},{4,5},{5,6},{6,7},{7,4},{8,9},{9,10},{10,1... | collective-permute-start | bytes 1572872 | tf_op jit(solution)/shard_map/ppermute | solution.py:34
  141.1 24.8 %collective-permute-start.2 = (bf16[4,128,512]{2,1,0:T(8,128)(2,1)S(1)}, bf16[4,128,512]{2,1,0:T(8,128)(2,1)S(1)}, u32[]{:S(2)}, u32[]{:S(2)}) collective-permute-start(bf16[4,128,512]{2,1,0:T(8,128)(2,1)S(1)} %get-tuple-element.39), channel_id=1, source_target_pairs={{0,3},{1,0},{2,1},{3,2},{4,7},{5,4},{6,5},{7,6},{8,11},{9,8},{10,9... | collective-permute-start | bytes 1572872 | tf_op jit(solution)/shard_map/ppermute | solution.py:34
  144.7 10.5 %copy-start.5 = (bf16[4,128,512]{2,1,0:T(8,128)(2,1)}, bf16[4,128,512]{2,1,0:T(8,128)(2,1)S(1)}, u32[]{:S(2)}) copy-start(bf16[4,128,512]{2,1,0:T(8,128)(2,1)S(1)} %collective-permute-done.10.d) | copy-start | bytes 1572868
  144.7 23.3 %collective-permute-start.3 = (bf16[4,128,512]{2,1,0:T(8,128)(2,1)S(1)}, bf16[4,128,512]{2,1,0:T(8,128)(2,1)}, u32[]{:S(2)}, u32[]{:S(2)}) collective-permute-start(bf16[4,128,512]{2,1,0:T(8,128)(2,1)S(1)} %get-tuple-element.40), channel_id=1, source_target_pairs={{0,2},{1,3},{2,0},{3,1},{4,6},{5,7},{6,4},{7,5},{8,10},{9,11},{10,... | collective-permute-start | bytes 1572872 | tf_op jit(solution)/shard_map/ppermute | solution.py:34
  155.2 0.8 copy-start.6
  156.0 0.8 copy-start.7
  159.2 14.4 %collective-permute-start.11 = (bf16[128,512]{1,0:T(8,128)(2,1)}, bf16[128,512]{1,0:T(8,128)(2,1)S(1)}, u32[]{:S(2)}, u32[]{:S(2)}) collective-permute-start(bf16[128,512]{1,0:T(8,128)(2,1)} %get-tuple-element.51), channel_id=1, source_target_pairs={{0,1},{1,2},{2,3},{3,0},{4,5},{5,6},{6,7},{7,4},{8,9},{9,10},{10,1... | collective-permute-start | bytes 393224 | tf_op jit(solution)/shard_map/ppermute | solution.py:34
  160.7 13.0 %collective-permute-start.12 = (bf16[128,512]{1,0:T(8,128)(2,1)}, bf16[128,512]{1,0:T(8,128)(2,1)}, u32[]{:S(2)}, u32[]{:S(2)}) collective-permute-start(bf16[128,512]{1,0:T(8,128)(2,1)} %get-tuple-element.52), channel_id=1, source_target_pairs={{0,3},{1,0},{2,1},{3,2},{4,7},{5,4},{6,5},{7,6},{8,11},{9,8},{10,9... | collective-permute-start | bytes 393224 | tf_op jit(solution)/shard_map/ppermute | solution.py:34
  162.5 5.5 %copy-start.3 = (bf16[4,128,512]{2,1,0:T(8,128)(2,1)}, bf16[4,128,512]{2,1,0:T(8,128)(2,1)S(1)}, u32[]{:S(2)}) copy-start(bf16[4,128,512]{2,1,0:T(8,128)(2,1)S(1)} %collective-permute-done.1.b) | copy-start | bytes 1572868
  162.5 11.2 %collective-permute-start.13 = (bf16[128,512]{1,0:T(8,128)(2,1)}, bf16[128,512]{1,0:T(8,128)(2,1)S(1)}, u32[]{:S(2)}, u32[]{:S(2)}) collective-permute-start(bf16[128,512]{1,0:T(8,128)(2,1)} %get-tuple-element.53), channel_id=1, source_target_pairs={{0,2},{1,3},{2,0},{3,1},{4,6},{5,7},{6,4},{7,5},{8,10},{9,11},{10,... | collective-permute-start | bytes 393224 | tf_op jit(solution)/shard_map/ppermute | solution.py:34
  165.9 2.1 %copy-start.4 = (bf16[4,128,512]{2,1,0:T(8,128)(2,1)}, bf16[4,128,512]{2,1,0:T(8,128)(2,1)S(1)}, u32[]{:S(2)}) copy-start(bf16[4,128,512]{2,1,0:T(8,128)(2,1)S(1)} %collective-permute-done.2.c) | copy-start | bytes 1572868
  170.4 7.1 %collective-permute-start.4 = (bf16[128,512]{1,0:T(8,128)(2,1)}, bf16[128,512]{1,0:T(8,128)(2,1)S(1)}, u32[]{:S(2)}, u32[]{:S(2)}) collective-permute-start(bf16[128,512]{1,0:T(8,128)(2,1)} %get-tuple-element.42), channel_id=1, source_target_pairs={{0,4},{1,5},{2,6},{3,7},{4,8},{5,9},{6,10},{7,11},{8,12},{9,13},{1... | collective-permute-start | bytes 393224 | tf_op jit(solution)/shard_map/ppermute | solution.py:34
  170.4 7.5 %collective-permute-start.5 = (bf16[128,512]{1,0:T(8,128)(2,1)}, bf16[128,512]{1,0:T(8,128)(2,1)S(1)}, u32[]{:S(2)}, u32[]{:S(2)}) collective-permute-start(bf16[128,512]{1,0:T(8,128)(2,1)} %get-tuple-element.43), channel_id=1, source_target_pairs={{0,12},{1,13},{2,14},{3,15},{4,0},{5,1},{6,2},{7,3},{8,4},{9,5},{1... | collective-permute-start | bytes 393224 | tf_op jit(solution)/shard_map/ppermute | solution.py:34
  173.6 6.7 %copy-start.8 = (bf16[128,512]{1,0:T(8,128)(2,1)}, bf16[128,512]{1,0:T(8,128)(2,1)S(1)}, u32[]{:S(2)}) copy-start(bf16[128,512]{1,0:T(8,128)(2,1)S(1)} %collective-permute-done.11.refs_5_) | copy-start | bytes 393220
  173.6 6.7 %collective-permute-start.6 = (bf16[128,512]{1,0:T(8,128)(2,1)}, bf16[128,512]{1,0:T(8,128)(2,1)S(1)}, u32[]{:S(2)}, u32[]{:S(2)}) collective-permute-start(bf16[128,512]{1,0:T(8,128)(2,1)} %get-tuple-element.44), channel_id=1, source_target_pairs={{0,8},{1,9},{2,10},{3,11},{4,12},{5,13},{6,14},{7,15},{8,0},{9,1},... | collective-permute-start | bytes 393224 | tf_op jit(solution)/shard_map/ppermute | solution.py:34
  173.7 6.7 %copy-start.9 = (bf16[128,512]{1,0:T(8,128)(2,1)}, bf16[128,512]{1,0:T(8,128)(2,1)S(1)}, u32[]{:S(2)}) copy-start(bf16[128,512]{1,0:T(8,128)(2,1)S(1)} %collective-permute-done.13.refs_7_) | copy-start | bytes 393220
  177.5 2.8 %copy-start.10 = (bf16[128,512]{1,0:T(8,128)(2,1)}, bf16[128,512]{1,0:T(8,128)(2,1)S(1)}, u32[]{:S(2)}) copy-start(bf16[128,512]{1,0:T(8,128)(2,1)S(1)} %collective-permute-done.4.refs_1_) | copy-start | bytes 393220
  177.9 2.5 %copy-start.11 = (bf16[128,512]{1,0:T(8,128)(2,1)}, bf16[128,512]{1,0:T(8,128)(2,1)S(1)}, u32[]{:S(2)}) copy-start(bf16[128,512]{1,0:T(8,128)(2,1)S(1)} %collective-permute-done.5.refs_2_) | copy-start | bytes 393220
  180.3 0.7 copy-start.12
  183.0 19.5 %collective-permute-start.14 = (bf16[64,512]{1,0:T(8,128)(2,1)}, bf16[64,512]{1,0:T(8,128)(2,1)S(1)}, u32[]{:S(2)}, u32[]{:S(2)}) collective-permute-start(bf16[64,512]{1,0:T(8,128)(2,1)} %get-tuple-element.55), channel_id=1, source_target_pairs={{0,32},{16,48},{32,64},{48,80},{64,96},{80,112},{96,0},{112,16},{1... | collective-permute-start | bytes 196616 | tf_op jit(solution)/shard_map/ppermute | solution.py:34
  184.7 17.8 %collective-permute-start.15 = (bf16[64,512]{1,0:T(8,128)(2,1)}, bf16[64,512]{1,0:T(8,128)(2,1)S(1)}, u32[]{:S(2)}, u32[]{:S(2)}) collective-permute-start(bf16[64,512]{1,0:T(8,128)(2,1)} %get-tuple-element.56), channel_id=1, source_target_pairs={{0,96},{16,112},{32,0},{48,16},{64,32},{80,48},{96,64},{112,80},{1... | collective-permute-start | bytes 196616 | tf_op jit(solution)/shard_map/ppermute | solution.py:34
  186.3 16.3 %collective-permute-start.16 = (bf16[64,512]{1,0:T(8,128)(2,1)}, bf16[64,512]{1,0:T(8,128)(2,1)S(1)}, u32[]{:S(2)}, u32[]{:S(2)}) collective-permute-start(bf16[64,512]{1,0:T(8,128)(2,1)} %get-tuple-element.57), channel_id=1, source_target_pairs={{0,64},{16,80},{32,96},{48,112},{64,0},{80,16},{96,32},{112,48},{1... | collective-permute-start | bytes 196616 | tf_op jit(solution)/shard_map/ppermute | solution.py:34
  188.3 14.3 %copy-start.13 = (bf16[64,512]{1,0:T(8,128)(2,1)S(1)}, bf16[64,512]{1,0:T(8,128)(2,1)}, u32[]{:S(2)}) copy-start(bf16[64,512]{1,0:T(8,128)(2,1)} %get-tuple-element.54) | copy-start | bytes 196612
Sparse Core Ops, SparseCore 0:
  11.7 82.7 all-gather.2

commit v2 on v0

v2 whole, which is shorter than its diff:
```python
import functools

import jax
import jax.numpy as jnp
from jax import lax
from jax.experimental import pallas as pl
from jax.experimental.pallas import tpu as pltpu
from jax.sharding import PartitionSpec as P

F32 = jnp.float32
BF16 = jnp.bfloat16
NT = (((1,), (1,)), ((), ()))
NN = (((1,), (0,)), ((), ()))
SIDE = 4
wait = lax.optimization_barrier
BLOCK = 512
MIB = 2**20


def dot(a, b, dims):
    return lax.dot_general(a, b, dims, preferred_element_type=F32)


def moves(axis, step):
    if axis == "x":
        return "shard", [(z * 4 + x, z * 4 + (x + step) % 4) for z in range(4) for x in range(4)]
    if axis == "z":
        return "shard", [(z * 4 + x, (z + step) % 4 * 4 + x) for z in range(4) for x in range(4)]
    if axis == "y":
        return "cuts", [(y * 2 + c, (y + step) % 4 * 2 + c) for y in range(4) for c in range(2)]
    return "cuts", [(y * 2 + c, y * 2 + 1 - c) for y in range(4) for c in range(2)]


def across(first, third, core, axis):
    pairs = []
    for y in range(4):
        for c in range(2):
            for z in range(4):
                for x in range(4):
                    step = -1 if c == 0 else 1
                    to_z, to_x = (z, (x + step) % 4) if axis == "x" else ((z + step) % 4, x)
                    pairs.append(((y * 2 + c) * 16 + z * 4 + x, (y * 2 + c) * 16 + to_z * 4 + to_x))
    return lax.ppermute(jnp.where(core == 0, first, third), ("cuts", "shard"), pairs)


def shift(value, axis, step=1):
    name, pairs = moves(axis, step)
    return lax.ppermute(value, name, pairs)


VMEM = pl.BlockSpec(memory_space=pltpu.VMEM)
ANY = pl.BlockSpec(memory_space=pl.ANY)
SMEM = pl.BlockSpec(memory_space=pltpu.SMEM)


def lanes(tab, at):
    return pl.ds(pl.multiple_of(tab[at] * BLOCK, BLOCK), BLOCK)


def wide(tab, at):
    return pl.ds(pl.multiple_of(tab[at] * 4 * BLOCK, 4 * BLOCK), 4 * BLOCK)


def sigmoid(v):
    return 1.0 / (1.0 + jnp.exp(-v))


def forward_kernel(es, first, last, tab, wg, wu, wd, *refs):
    refs, (bg, bu, bd, sems) = refs[:-4], refs[-4:]
    pieces, refs = refs[:4 * len(es)], refs[4 * len(es):]
    before = () if first else refs[:3]
    refs = refs[len(before):]
    keep_ref = refs[0] if last else None
    outs = refs[1:] if last else refs
    copies = []
    for n, e in enumerate(es):
        cols = wide(tab, 32 + e)
        copies += [
            [pltpu.make_async_copy(wg.at[:, cols], bg.at[n], sems.at[n, 0])],
            [pltpu.make_async_copy(wu.at[:, cols], bu.at[n], sems.at[n, 1])],
            [
                pltpu.make_async_copy(wd.at[:, lanes(tab, 16 + 4 * e + d)], bd.at[n, d], sems.at[n, 2 + d])
                for d in range(SIDE)
            ],
        ]
    for group in copies:
        for copy in group:
            copy.start()
    sums = ([], [], [])
    for n in range(len(es)):
        for m in range(3):
            data = pieces[4 * n + 2 * (m // 2):4 * n + 2 * (m // 2) + 2]
            for copy in copies[3 * n + m]:
                copy.wait()
            for side in range(2):
                cols = slice(side * 256, side * 256 + 256)
                total = outs[m][:, cols] if n else None if first else before[m][:, cols]
                for d in range(SIDE):
                    w = bd[n, d] if m == 2 else (bg, bu)[m][n, :, lanes(tab, 36 + d)]
                    term = dot(w, data[side][d], NT)
                    total = term if total is None else total + term
                if last:
                    sums[m].append(total)
                else:
                    outs[m][:, cols] = total
    if last:
        ht_ref, dgt_ref, dut_ref, own_ref, far_ref = outs
        for side, out in ((1, far_ref), (0, own_ref)):
            cols = slice(side * 256, side * 256 + 256)
            keep = keep_ref[:, cols]
            gv, uv, dhv = sums[0][side], sums[1][side], sums[2][side] * keep
            sig = sigmoid(gv)
            silu = gv * sig
            ht_ref[:, cols] = (silu * uv * keep).astype(BF16)
            dg = dhv * uv * sig * (1.0 + gv * (1.0 - sig))
            du = dhv * silu
            dgt_ref[:, cols] = dg.astype(BF16)
            dut_ref[:, cols] = du.astype(BF16)
            for k, value in enumerate((dg, du)):
                turned = value.T.astype(BF16)
                for b in range(SIDE):
                    for half in range(2):
                        low = b * 64 + half * 32
                        out[k, half, b * 32:b * 32 + 32] = turned[low:low + 32]


def forward(es, tab, weights, pieces, before, keep):
    first, last, count = not before, keep is not None, len(es)
    operands = [tab, *weights, *pieces, *before]
    if last:
        operands.append(keep)
        out_shape = [jax.ShapeDtypeStruct((224, 512), BF16)] * 3 + [jax.ShapeDtypeStruct((2, 2, 128, 224), BF16)] * 2
    else:
        out_shape = [jax.ShapeDtypeStruct((224, 512), F32)] * 3
    return pl.pallas_call(
        functools.partial(forward_kernel, es, first, last),
        in_specs=[SMEM] + [ANY] * 3 + [VMEM] * (len(operands) - 4),
        out_specs=[VMEM] * len(out_shape),
        out_shape=out_shape,
        scratch_shapes=[
            pltpu.VMEM((count, 224, 4 * BLOCK), BF16),
            pltpu.VMEM((count, 224, 4 * BLOCK), BF16),
            pltpu.VMEM((count, 4, 224, BLOCK), BF16),
            pltpu.SemaphoreType.DMA((count, 6)),
        ],
        compiler_params=pltpu.CompilerParams(vmem_limit_bytes=(6 + 7 * count) * MIB),
        cost_estimate=pl.CostEstimate(flops=count * 6 * 512 * 224 * 2048, bytes_accessed=count * 8 * MIB, transcendentals=0),
    )(*operands)


def token_grad_kernel(tab, dgt_ref, dut_ref, *refs):
    pieces, outs = refs[:8], refs[8:]
    for e in range(SIDE):
        @pl.when(pl.program_id(0) == e)
        def _(e=e):
            for d in range(SIDE):
                x0, x1 = pieces[2 * e][d], pieces[2 * e + 1][d]
                for row, out in zip((dgt_ref, dut_ref), outs):
                    out[:, lanes(tab, 36 + d)] = (dot(row[:, :256], x0, NN) + dot(row[:, 256:], x1, NN)).astype(BF16)


def down_grad_kernel(tab, ht_ref, *refs):
    pieces, out = refs[:8], refs[8]
    d = pl.program_id(0)
    for e in range(SIDE):
        g0, g1 = pieces[2 * e][d], pieces[2 * e + 1][d]
        out[:, lanes(tab, 36 + e)] = (dot(ht_ref[:, :256], g0, NN) + dot(ht_ref[:, 256:], g1, NN)).astype(BF16)


def weight_grads(kernel, tab, rows, own, far):
    pieces = [p for e in range(SIDE) for p in (own[e], far[e])]
    count = len(rows)
    return pl.pallas_call(
        kernel,
        grid_spec=pltpu.PrefetchScalarGridSpec(
            num_scalar_prefetch=1,
            grid=(SIDE,),
            in_specs=[VMEM] * (count + len(pieces)),
            out_specs=[pl.BlockSpec((224, 4 * BLOCK), lambda k, tab: (0, tab[32 + k]))] * count,
        ),
        out_shape=[jax.ShapeDtypeStruct((224, 8192), BF16)] * count,
        compiler_params=pltpu.CompilerParams(vmem_limit_bytes=14 * MIB),
        cost_estimate=pl.CostEstimate(flops=count * 2 * 512 * 224 * 8192, bytes_accessed=count * 6 * MIB, transcendentals=0),
    )(tab, *rows, *pieces)


def input_grad_kernel(tab, own_ref, far_ref, *refs):
    weights, outs, (held, sems) = refs[:4], refs[4:12], refs[12:]
    rows = [ref[k].reshape(256, 224) for ref in (own_ref, far_ref) for k in range(2)]

    def fetch(dz):
        return [
            pltpu.make_async_copy(w.at[:, wide(tab, 32 + dz)], held.at[dz % 2, n], sems.at[dz % 2, n])
            for n, w in enumerate(weights)
        ]

    copies = fetch(0)
    for copy in copies:
        copy.start()
    for dz in range(SIDE):
        current = copies
        if dz < SIDE - 1:
            copies = fetch(dz + 1)
            for copy in copies:
                copy.start()
        for copy in current:
            copy.wait()
        for dx in range(SIDE):
            cols = lanes(tab, 36 + dx)
            w = [held[dz % 2, n, :, cols] for n in range(4)]
            total = (dot(rows[0], w[0], NN) + dot(rows[1], w[1], NN)) + (dot(rows[2], w[2], NN) + dot(rows[3], w[3], NN))
            done = total.astype(BF16)
            outs[dx][dz] = done[:128]
            outs[4 + dz][dx] = done[128:]


def input_grads(tab, own, far, weights):
    return pl.pallas_call(
        input_grad_kernel,
        in_specs=[SMEM] + [VMEM] * 2 + [ANY] * 4,
        out_specs=[VMEM] * 8,
        out_shape=[jax.ShapeDtypeStruct((4, 128, BLOCK), BF16)] * 8,
        scratch_shapes=[pltpu.VMEM((2, 4, 224, 4 * BLOCK), BF16), pltpu.SemaphoreType.DMA((2, 4))],
        compiler_params=pltpu.CompilerParams(vmem_limit_bytes=16 * MIB),
        cost_estimate=pl.CostEstimate(flops=8 * 256 * 224 * 8192, bytes_accessed=18 * MIB, transcendentals=0),
    )(tab, own, far, *weights)


def sum_kernel(a, b, c, d, *outs):
    for k in range(SIDE):
        outs[k][...] = (
            (a[k].astype(F32) + b[k].astype(F32)) + (c[k].astype(F32) + d[k].astype(F32))
        ).astype(BF16)


def sum_apart(parts):
    return pl.pallas_call(
        sum_kernel,
        out_shape=[jax.ShapeDtypeStruct((128, BLOCK), BF16)] * 4,
        compiler_params=pltpu.CompilerParams(vmem_limit_bytes=4 * MIB),
        cost_estimate=pl.CostEstimate(flops=3 * 4 * 128 * 512, bytes_accessed=5 * 2**19, transcendentals=0),
    )(*parts)


def join_kernel(*refs):
    ins, outs = refs[:8], refs[8:]
    for h in range(2):
        total = (ins[4 * h][...].astype(F32) + ins[4 * h + 1][...].astype(F32)) + (
            ins[4 * h + 2][...].astype(F32) + ins[4 * h + 3][...].astype(F32)
        )
        for k in range(SIDE):
            outs[k][h * 32:(h + 1) * 32] = total[k * 32:(k + 1) * 32].astype(BF16)


def join_apart(first, second):
    return pl.pallas_call(
        join_kernel,
        out_shape=[jax.ShapeDtypeStruct((64, BLOCK), BF16)] * 4,
        compiler_params=pltpu.CompilerParams(vmem_limit_bytes=4 * MIB),
        cost_estimate=pl.CostEstimate(flops=2**19, bytes_accessed=5 * 2**18, transcendentals=0),
    )(*first, *second)


def exchange(pieces, axis):
    return [pieces[0]] + [shift(pieces[d], axis, d) for d in (1, 3, 2)]


def exchange_in_two(first, second, fill):
    near = [shift(p[d], axis, d) for p, axis in (first, second) for d in (1, 3)]
    near, done0 = wait((near, fill[0]()))
    ends = [first[0][2], second[0][2]]
    ends, near = wait((ends, near))
    ends = [shift(ends[0], first[1], 2), shift(ends[1], second[1], 2)]
    ends, done1 = wait((ends, fill[1]()))
    return [first[0][0], *near[:2], ends[0]], [second[0][0], *near[2:], ends[1]], done0, done1


def around(value, axis):
    return [value] + [shift(value, axis, -e % SIDE) for e in (1, 2, 3)]


def body(tokens, grad_out, counts, gate_weight, up_weight, down_weight):
    c = lax.axis_index("cuts")
    s = lax.axis_index("shard")
    core, z, x = c % 2, s // 4, s % 4
    step = jnp.arange(SIDE, dtype=jnp.int32)
    zs, xs = (z + step) % 4, (x + step) % 4
    by_z = zs[:, None] * 4 + xs[None, :]
    tab = jnp.concatenate([by_z.reshape(16), by_z.T.reshape(16), zs, xs]).astype(jnp.int32)
    weights = (gate_weight, up_weight, down_weight)

    row = jnp.pad(counts.astype(BF16)[None, :], ((0, 15), (0, BLOCK - 64)))
    blocks = around(jnp.concatenate([tokens, grad_out, row], 0), "y")
    blocks, far_gate, far_up = wait((blocks, shift(gate_weight, "core"), shift(up_weight, "core")))

    x0 = jnp.concatenate([b[:64] for b in blocks], 0)
    g0 = jnp.concatenate([b[64:128] for b in blocks], 0)
    own_counts = jnp.concatenate([b[128:129, :64] for b in blocks], 1)
    ahead = shift(x0, "x", 3)
    held, ahead = wait((g0, ahead))
    x0 = [x0, ahead, shift(x0, "x", 2), shift(x0, "x", 1)]
    g0 = [g0, shift(g0, "z", 3), shift(g0, "z", 2), shift(held, "z", 1)]
    x0, g0 = wait((x0, g0))
    x0, g0 = jnp.stack(x0), jnp.stack(g0)

    own_x, own_g, far_x, far_g = {0: x0}, {0: g0}, {}, {}

    def swap(e):
        far_x[e], far_g[e] = shift(own_x[e], "core"), shift(own_g[e], "core")

    def add(es, before, keep=None):
        pieces = [p[e] for e in es for p in (own_x, far_x, own_g, far_g)]
        return forward(es, tab, weights, pieces, before, keep)

    near = [shift(x0, "z", 3), shift(x0, "z", 1), shift(g0, "x", 3), shift(g0, "x", 1)]
    swap(0)
    all_counts = jnp.concatenate([own_counts, shift(own_counts, "core")], 1)
    keep = (all_counts.astype(F32) > c.astype(F32)).astype(F32)
    sums = add((0,), ())
    near, sums, keep = wait((near, sums, keep))
    own_x[1], own_x[3], own_g[1], own_g[3] = near
    ends = [across(own_x[1], own_x[3], core, "z"), across(own_g[1], own_g[3], core, "x")]
    swap(1)
    swap(3)
    sums = add((1, 3), sums)
    ends, sums = wait((ends, sums))
    own_x[2], own_g[2] = ends
    swap(2)
    ht, dgt, dut, dg_own, dg_far = add((2,), sums, keep)
    dg_far = shift(dg_far, "core")
    terms = input_grads(tab, dg_own, dg_far, (gate_weight, up_weight, far_gate, far_up))
    first, second, grads, down = exchange_in_two(
        (terms[:4], "x"),
        (terms[4:], "z"),
        (
            lambda: weight_grads(token_grad_kernel, tab, (dgt, dut), own_x, far_x),
            lambda: weight_grads(down_grad_kernel, tab, (ht,), own_g, far_g),
        ),
    )
    first = exchange(sum_apart(first), "z")
    second = exchange(sum_apart(second), "x")
    parts = exchange(join_apart(first, second), "y")
    total = (parts[0].astype(F32) + parts[1].astype(F32)) + (parts[2].astype(F32) + parts[3].astype(F32))
    return (total.astype(BF16), *grads, *down)


def solution(mesh):
    return jax.shard_map(
        body,
        mesh=mesh,
        in_specs=(
            P("cuts", "shard"),
            P("cuts", "shard"),
            P("cuts"),
            P(("cuts", "shard"), None),
            P(("cuts", "shard"), None),
            P(("cuts", "shard"), None),
        ),
        out_specs=(
            P("cuts", "shard"),
            P(("cuts", "shard"), None),
            P(("cuts", "shard"), None),
            P(("cuts", "shard"), None),
        ),
        check_vma=False,
    )
```

time: 345 us -> 169 us (0.49)
  waiting for transfers between devices: 237 us -> 49.5 us
  matrix products: 53.8 us -> 0 us
  starting transfers between devices: 4.32 us -> 58 us
  Pallas kernels: 0 us -> 36.1 us
  blocking collectives: 28.3 us -> 0 us
  local copies, waits for them, and re-layouts: 4.67 us -> 18.8 us
  between operations: 13.8 us -> 0.9 us
  other arithmetic: 1.67 us -> 5.21 us
    all_gather x2 -> x0, waiting for transfers between devices: 134 us -> none  [the longest x1 69.4 us: body(): lax.all_gather(recv_g, 'shard', axis=2, tiled=True)]
    reduce_scatter x1 -> x0, waiting for transfers between devices: 102 us -> none  [body(): shared = lax.psum_scatter(terms, 'shard', scatter_dimension=2, tiled=True)]
    ppermute x0 -> x42, starting transfers between devices: none -> 58 us  [the longest x40 51.7 us: shift(): return lax.ppermute(value, name, pairs)]
    dot_general x10 -> x0, matrix products: 53.8 us -> none  [the longest x1 10.4 us: body(): terms = terms + jnp.dot(dup, up_weight, preferred_element_type=jnp.float32)]
    ppermute x0 -> x42, waiting for transfers between devices: none -> 49.5 us  [the longest x40 48.6 us: shift(): return lax.ppermute(value, name, pairs)]
    pallas_call x0 -> x9, Pallas kernels: none -> 36.1 us  [the longest x3 15.1 us: forward(): pl.pallas_call(functools.partial(forward_kernel, es, first, last), in_spe...]
    all_to_all x2 -> x0, blocking collectives: 28.3 us -> none  [the longest x1 14.9 us: body(): lax.all_to_all(send_x, 'cuts', split_axis=0, concat_axis=0, tiled=True)]
    unnamed x14 -> x42, local copies, waits for them, and re-layouts: 0.62 us -> 18.4 us
  transfers between devices with their start and end apart: 4 -> 42, of which waited for: 4 -> 20; matrix products, arithmetic and copies ran while one was open for 10% -> 3% of each run, Pallas kernels for 0% -> 15%
where the time goes in v2:
time: 169 us; the launch traced here: 168 us
  starting transfers between devices  58 us (34%)
  waiting for transfers between devices  49.5 us (29%)
  Pallas kernels  36.1 us (21%)
  local copies, waits for them, and re-layouts  18.8 us (11%)
  other arithmetic  5.21 us (3%)
    ppermute x40, starting transfers between devices, shift(): return lax.ppermute(value, name, pairs)  51.7 us
    ppermute x40, waiting for transfers between devices, shift(): return lax.ppermute(value, name, pairs)  48.6 us
    unnamed x42, local copies, waits for them, and re-layouts  18.4 us
    pallas_call x3, Pallas kernels, forward(): pl.pallas_call(functools.partial(forward_kernel, es, first, last), in_spe...  15.1 us
    pallas_call x2, Pallas kernels, weight_grads(): pl.pallas_call(kernel, grid_spec=pltpu.PrefetchScalarGridSpec(num_scalar_...  13.3 us
    pallas_call x1, Pallas kernels, input_grads(): pl.pallas_call(input_grad_kernel, in_specs=[SMEM] + [VMEM] * 2 + [ANY] *...  7.01 us
    ppermute x2, starting transfers between devices, across(): lax.ppermute(jnp.where(core == 0, first, third), ('cuts', 'shard'), pairs)  6.33 us
  transfers between devices with their start and end apart: 42, of which 20 were waited for; matrix products, arithmetic and copies ran while one was open for 3% of the time, Pallas kernels for 15%

profile of v2, /device:TPU:0, one launch (start us, length us, event | category | flops | bytes accessed | tf_op | source)
XLA Modules:
  0.0 168.5 jit_solution(1198562603742857334)
XLA Ops:
  1.9 0.9 fusion.1
  2.8 1.7 %collective-permute-start.2 = (bf16[144,512]{1,0:T(8,128)(2,1)S(1)}, bf16[144,512]{1,0:T(8,128)(2,1)S(1)}, u32[]{:S(2)}, u32[]{:S(2)}) collective-permute-start(bf16[144,512]{1,0:T(8,128)(2,1)S(1)} %fusion.1), channel_id=1, source_target_pairs={{0,32},{16,48},{32,64},{48,80},{64,96},{80,112},{96,0},{112,16},{1... | collective-permute-start | bytes 442376 | tf_op jit(solution)/shard_map/ppermute | solution.py:48
  4.5 2.9 %collective-permute-start.1 = (bf16[144,512]{1,0:T(8,128)(2,1)S(1)}, bf16[144,512]{1,0:T(8,128)(2,1)S(1)}, u32[]{:S(2)}, u32[]{:S(2)}) collective-permute-start(bf16[144,512]{1,0:T(8,128)(2,1)S(1)} %fusion.1), channel_id=1, source_target_pairs={{0,64},{16,80},{32,96},{48,112},{64,0},{80,16},{96,32},{112,48},{1... | collective-permute-start | bytes 442376 | tf_op jit(solution)/shard_map/ppermute | solution.py:48
  7.4 1.3 collective-permute-start
  8.7 1.3 collective-permute-done.2
  10.0 4.3 %collective-permute-done.1 = bf16[144,512]{1,0:T(8,128)(2,1)S(1)} collective-permute-done((bf16[144,512]{1,0:T(8,128)(2,1)S(1)}, bf16[144,512]{1,0:T(8,128)(2,1)S(1)}, u32[]{:S(2)}, u32[]{:S(2)}) %collective-permute-start.1) | collective-permute-done | bytes 147488 | tf_op jit(solution)/shard_map/ppermute | solution.py:48
  14.4 1.8 %copy-done.11 = bf16[224,8192]{1,0:T(8,128)(2,1)} copy-done((bf16[224,8192]{1,0:T(8,128)(2,1)}, bf16[224,8192]{1,0:T(8,128)(2,1)S(1)}, u32[]{:S(2)}) %copy-start.11) | copy-done | bytes 3670040
  16.2 1.8 %copy-done.13 = bf16[224,8192]{1,0:T(8,128)(2,1)} copy-done((bf16[224,8192]{1,0:T(8,128)(2,1)}, bf16[224,8192]{1,0:T(8,128)(2,1)S(1)}, u32[]{:S(2)}) %copy-start.13) | copy-done | bytes 3670040
  18.1 2.8 %collective-permute-start.5 = (bf16[256,512]{1,0:T(8,128)(2,1)S(1)}, bf16[256,512]{1,0:T(8,128)(2,1)S(1)}, u32[]{:S(2)}, u32[]{:S(2)}) collective-permute-start(bf16[256,512]{1,0:T(8,128)(2,1)S(1)} %pad_maximum_fusion.2), channel_id=1, source_target_pairs={{0,3},{1,0},{2,1},{3,2},{4,7},{5,4},{6,5},{7,6},{8,11},{9,8},{10,9... | collective-permute-start | bytes 786440 | tf_op jit(solution)/shard_map/ppermute | solution.py:48
  21.0 2.3 %collective-permute-start.6 = (bf16[256,512]{1,0:T(8,128)(2,1)S(1)}, bf16[256,512]{1,0:T(8,128)(2,1)S(1)}, u32[]{:S(2)}, u32[]{:S(2)}) collective-permute-start(bf16[256,512]{1,0:T(8,128)(2,1)S(1)} %pad_maximum_fusion.2), channel_id=1, source_target_pairs={{0,2},{1,3},{2,0},{3,1},{4,6},{5,7},{6,4},{7,5},{8,10},{9,11},{10,... | collective-permute-start | bytes 786440 | tf_op jit(solution)/shard_map/ppermute | solution.py:48
  23.3 4.0 %collective-permute-start.9 = (bf16[256,512]{1,0:T(8,128)(2,1)S(1)}, bf16[256,512]{1,0:T(8,128)(2,1)S(1)}, u32[]{:S(2)}, u32[]{:S(2)}) collective-permute-start(bf16[256,512]{1,0:T(8,128)(2,1)S(1)} %pad_maximum_fusion.3), channel_id=1, source_target_pairs={{0,8},{1,9},{2,10},{3,11},{4,12},{5,13},{6,14},{7,15},{8,0},{9,1},... | collective-permute-start | bytes 786440 | tf_op jit(solution)/shard_map/ppermute | solution.py:48
  27.2 0.7 collective-permute-start.8
  27.9 3.7 %collective-permute-done.5 = bf16[256,512]{1,0:T(8,128)(2,1)S(1)} collective-permute-done((bf16[256,512]{1,0:T(8,128)(2,1)S(1)}, bf16[256,512]{1,0:T(8,128)(2,1)S(1)}, u32[]{:S(2)}, u32[]{:S(2)}) %collective-permute-start.5) | collective-permute-done | bytes 262176 | tf_op jit(solution)/shard_map/ppermute | solution.py:48
  31.6 1.9 %collective-permute-start.10 = (bf16[256,512]{1,0:T(8,128)(2,1)S(1)}, bf16[256,512]{1,0:T(8,128)(2,1)S(1)}, u32[]{:S(2)}, u32[]{:S(2)}) collective-permute-start(bf16[256,512]{1,0:T(8,128)(2,1)S(1)} %pad_maximum_fusion.3), channel_id=1, source_target_pairs={{0,4},{1,5},{2,6},{3,7},{4,8},{5,9},{6,10},{7,11},{8,12},{9,13},{1... | collective-permute-start | bytes 786440 | tf_op jit(solution)/shard_map/ppermute | solution.py:48
  33.5 1.5 collective-permute-done.7
  35.0 3.5 %collective-permute-done.8 = bf16[256,512]{1,0:T(8,128)(2,1)S(1)} collective-permute-done((bf16[256,512]{1,0:T(8,128)(2,1)S(1)}, bf16[256,512]{1,0:T(8,128)(2,1)S(1)}, u32[]{:S(2)}, u32[]{:S(2)}) %collective-permute-start.8) | collective-permute-done | bytes 262176 | tf_op jit(solution)/shard_map/ppermute | solution.py:48
  38.5 1.5 collective-permute-done.10
  40.2 1.1 pad_maximum_fusion.refs_0_
  42.4 3.4 %collective-permute-start.13 = (bf16[4,256,512]{2,1,0:T(8,128)(2,1)S(1)}, bf16[4,256,512]{2,1,0:T(8,128)(2,1)S(1)}, u32[]{:S(2)}, u32[]{:S(2)}) collective-permute-start(bf16[4,256,512]{2,1,0:T(8,128)(2,1)S(1)} %pad_maximum_fusion.1.refs_2_.refs_0_), channel_id=1, source_target_pairs={{0,3},{1,0},{2,1},{3,2},{4,7},{5,4},{6,5},{7,6},{8,11},{9,8},{10,9... | collective-permute-start | bytes 3145736 | tf_op jit(solution)/shard_map/ppermute | solution.py:48
  45.8 1.0 copy-done.8
  46.8 3.2 %collective-permute-start.11 = (bf16[4,256,512]{2,1,0:T(8,128)(2,1)}, bf16[4,256,512]{2,1,0:T(8,128)(2,1)}, u32[]{:S(2)}, u32[]{:S(2)}) collective-permute-start(bf16[4,256,512]{2,1,0:T(8,128)(2,1)} %pad_maximum_fusion.refs_0_), channel_id=1, source_target_pairs={{0,12},{1,13},{2,14},{3,15},{4,0},{5,1},{6,2},{7,3},{8,4},{9,5},{1... | collective-permute-start | bytes 3145736 | tf_op jit(solution)/shard_map/ppermute | solution.py:48
  50.5 2.0 %copy-done = bf16[224,8192]{1,0:T(8,128)(2,1)S(1)} copy-done((bf16[224,8192]{1,0:T(8,128)(2,1)S(1)}, bf16[224,8192]{1,0:T(8,128)(2,1)}, u32[]{:S(2)}) %copy-start) | copy-done | bytes 3670040
  52.5 2.0 %copy-done.2 = bf16[224,8192]{1,0:T(8,128)(2,1)S(1)} copy-done((bf16[224,8192]{1,0:T(8,128)(2,1)S(1)}, bf16[224,8192]{1,0:T(8,128)(2,1)}, u32[]{:S(2)}) %copy-start.2) | copy-done | bytes 3670040
  54.6 2.0 %copy-done.5 = bf16[224,8192]{1,0:T(8,128)(2,1)S(1)} copy-done((bf16[224,8192]{1,0:T(8,128)(2,1)S(1)}, bf16[224,8192]{1,0:T(8,128)(2,1)}, u32[]{:S(2)}) %copy-start.5) | copy-done | bytes 3670040
  56.6 1.2 copy-done.9
  57.8 4.3 %shard_map.93 = (f32[224,512]{1,0:T(8,128)S(1)}, f32[224,512]{1,0:T(8,128)S(1)}, f32[224,512]{1,0:T(8,128)S(1)}) custom-call(s32[40]{0:T(128)S(1)} %pad_add_fusion.tab, bf16[224,8192]{1,0:T(8,128)(2,1)S(1)} %copy-done, bf16[224,8192]{1,0:T(8,128)(2,1)S(1)} %copy-done.2, bf16[224,8192]{1,0:T(8,128)(2,1)S(1)} %copy-done.5, ...), custom_call_target="tpu_custom_call" | custom-call | flops 1409286144 | bytes 8388608 | tf_op jit(solution)/shard_map/pallas_call | solution.py:135
  62.1 0.8 copy-done.15
  62.9 0.8 copy-done.17
  63.7 0.8 copy-done.19
  64.5 5.0 %collective-permute-done.14.refs_6_ = bf16[4,256,512]{2,1,0:T(8,128)(2,1)S(1)} collective-permute-done((bf16[4,256,512]{2,1,0:T(8,128)(2,1)S(1)}, bf16[4,256,512]{2,1,0:T(8,128)(2,1)S(1)}, u32[]{:S(2)}, u32[]{:S(2)}) %collective-permute-start.14) | collective-permute-done | bytes 1048608 | tf_op jit(solution)/shard_map/ppermute | solution.py:48
  69.4 3.0 %collective-permute-done.12.refs_4_.refs_6_ = bf16[4,256,512]{2,1,0:T(8,128)(2,1)} collective-permute-done((bf16[4,256,512]{2,1,0:T(8,128)(2,1)}, bf16[4,256,512]{2,1,0:T(8,128)(2,1)}, u32[]{:S(2)}, u32[]{:S(2)}) %collective-permute-start.12) | collective-permute-done | bytes 1048608 | tf_op jit(solution)/shard_map/ppermute | solution.py:48
  73.5 2.4 %collective-permute-start.19 = (bf16[4,256,512]{2,1,0:T(8,128)(2,1)S(1)}, bf16[4,256,512]{2,1,0:T(8,128)(2,1)S(1)}, u32[]{:S(2)}, u32[]{:S(2)}) collective-permute-start(bf16[4,256,512]{2,1,0:T(8,128)(2,1)S(1)} %broadcast_select_fusion), channel_id=1, source_target_pairs={{0,3},{1,0},{2,1},{3,2},{4,7},{5,4},{6,5},{7,6},{8,11},{9,8},{10,9... | collective-permute-start | bytes 3145736 | tf_op jit(solution)/shard_map/ppermute | solution.py:43
  75.9 1.3 broadcast_select_fusion.1
  77.3 3.9 %collective-permute-start.18 = (bf16[4,256,512]{2,1,0:T(8,128)(2,1)S(1)}, bf16[4,256,512]{2,1,0:T(8,128)(2,1)S(1)}, u32[]{:S(2)}, u32[]{:S(2)}) collective-permute-start(bf16[4,256,512]{2,1,0:T(8,128)(2,1)S(1)} %broadcast_select_fusion.1), channel_id=1, source_target_pairs={{0,12},{1,13},{2,14},{3,15},{4,0},{5,1},{6,2},{7,3},{8,4},{9,5},{1... | collective-permute-start | bytes 3145736 | tf_op jit(solution)/shard_map/ppermute | solution.py:43
  81.3 2.0 %copy-done.3 = bf16[224,8192]{1,0:T(8,128)(2,1)S(1)} copy-done((bf16[224,8192]{1,0:T(8,128)(2,1)S(1)}, bf16[224,8192]{1,0:T(8,128)(2,1)}, u32[]{:S(2)}) %copy-start.3) | copy-done | bytes 3670040
  83.3 2.0 %copy-done.6 = bf16[224,8192]{1,0:T(8,128)(2,1)S(1)} copy-done((bf16[224,8192]{1,0:T(8,128)(2,1)S(1)}, bf16[224,8192]{1,0:T(8,128)(2,1)}, u32[]{:S(2)}) %copy-start.6) | copy-done | bytes 3670040
  85.4 7.2 %shard_map.94 = (f32[224,512]{1,0:T(8,128)S(1)}, f32[224,512]{1,0:T(8,128)S(1)}, f32[224,512]{1,0:T(8,128)S(1)}) custom-call(s32[40]{0:T(128)S(1)} %pad_add_fusion.tab, bf16[224,8192]{1,0:T(8,128)(2,1)S(1)} %copy-done.1, bf16[224,8192]{1,0:T(8,128)(2,1)S(1)} %copy-done.3, bf16[224,8192]{1,0:T(8,128)(2,1)S(1)} %copy-done.6, ...), custom_call_target="tpu_custom_call" | custom-call | flops 2818572288 | bytes 16777216 | tf_op jit(solution)/shard_map/pallas_call | solution.py:135
  92.6 0.9 collective-permute-done.18.refs_0_.refs_4_
  94.1 2.1 %collective-permute-done.24.refs_1_.refs_5_ = bf16[4,256,512]{2,1,0:T(8,128)(2,1)S(1)} collective-permute-done((bf16[4,256,512]{2,1,0:T(8,128)(2,1)S(1)}, bf16[4,256,512]{2,1,0:T(8,128)(2,1)S(1)}, u32[]{:S(2)}, u32[]{:S(2)}) %collective-permute-start.24) | collective-permute-done | bytes 1048608 | tf_op jit(solution)/shard_map/ppermute | solution.py:48
  96.2 1.5 collective-permute-done.25.refs_3_.refs_5_
  97.7 3.6 %shard_map.95 = (bf16[224,512]{1,0:T(8,128)(2,1)S(1)}, bf16[224,512]{1,0:T(8,128)(2,1)S(1)}, bf16[224,512]{1,0:T(8,128)(2,1)S(1)}, bf16[2,2,128,224]{3,2,1,0:T(8,128)(2,1)S(1)}, bf16[2,2,128,224]{3,2,1,0:T(8,128)(2,1)S(1)}) custom-call(s32[40]{0:T(128)S(1)} %pad_add_fusion.tab, bf16[224,8192]{1,0:T(8,128)(2,1)S(1)} %copy-done.1, ...), custom_call_target="tpu_custom_call" | custom-call | flops 1409286144 | bytes 8388608 | tf_op jit(solution)/shard_map/pallas_call | solution.py:135
  101.5 1.4 collective-permute-done.26.far_ref
  102.9 7.0 %shard_map.96 = (bf16[4,128,512]{2,1,0:T(8,128)(2,1)S(1)}, bf16[4,128,512]{2,1,0:T(8,128)(2,1)S(1)}, bf16[4,128,512]{2,1,0:T(8,128)(2,1)S(1)}, bf16[4,128,512]{2...) custom-call(s32[40]{0:T(128)S(1)} %pad_add_fusion.tab, ...), custom_call_target="tpu_custom_call" | custom-call | flops 3758096384 | bytes 18874368 | tf_op jit(solution)/shard_map/pallas_call | solution.py:218
  110.0 3.2 %collective-permute-start.28 = (bf16[4,128,512]{2,1,0:T(8,128)(2,1)S(1)}, bf16[4,128,512]{2,1,0:T(8,128)(2,1)S(1)}, u32[]{:S(2)}, u32[]{:S(2)}) collective-permute-start(bf16[4,128,512]{2,1,0:T(8,128)(2,1)S(1)} %get-tuple-element.122), channel_id=1, source_target_pairs={{0,3},{1,0},{2,1},{3,2},{4,7},{5,4},{6,5},{7,6},{8,11},{9,8},{10,9... | collective-permute-start | bytes 1572872 | tf_op jit(solution)/shard_map/ppermute | solution.py:48
  113.3 3.7 %collective-permute-start.30 = (bf16[4,128,512]{2,1,0:T(8,128)(2,1)S(1)}, bf16[4,128,512]{2,1,0:T(8,128)(2,1)S(1)}, u32[]{:S(2)}, u32[]{:S(2)}) collective-permute-start(bf16[4,128,512]{2,1,0:T(8,128)(2,1)S(1)} %get-tuple-element.124), channel_id=1, source_target_pairs={{0,12},{1,13},{2,14},{3,15},{4,0},{5,1},{6,2},{7,3},{8,4},{9,5},{1... | collective-permute-start | bytes 1572872 | tf_op jit(solution)/shard_map/ppermute | solution.py:48
  116.9 9.0 %shard_map.97 = (bf16[224,8192]{1,0:T(8,128)(2,1)}, bf16[224,8192]{1,0:T(8,128)(2,1)}) custom-call(s32[40]{0:T(128)S(1)} %pad_add_fusion.tab, bf16[224,512]{1,0:T(8,128)(2,1)S(1)} %get-tuple-element.125.dgt_ref, bf16[224,512]{1,0:T(8,128)(2,1)S(1)} %get-tuple-element.126.dut_ref, bf16[4,256,512]{2,1,0:T(8,128)(2,1)} %pad_maximum_fusion.refs_0_, ...), custom_call_target="tpu_custom_call" | custom-call | flops 3758096384 | bytes 12582912 | tf_op jit(solution)/shard_map/pallas_call | solution.py:173
  125.9 2.7 %collective-permute-done.29.b = bf16[4,128,512]{2,1,0:T(8,128)(2,1)S(1)} collective-permute-done((bf16[4,128,512]{2,1,0:T(8,128)(2,1)S(1)}, bf16[4,128,512]{2,1,0:T(8,128)(2,1)S(1)}, u32[]{:S(2)}, u32[]{:S(2)}) %collective-permute-start.29) | collective-permute-done | bytes 524320 | tf_op jit(solution)/shard_map/ppermute | solution.py:48
  129.0 2.9 %collective-permute-start.32 = (bf16[4,128,512]{2,1,0:T(8,128)(2,1)S(1)}, bf16[4,128,512]{2,1,0:T(8,128)(2,1)S(1)}, u32[]{:S(2)}, u32[]{:S(2)}) collective-permute-start(bf16[4,128,512]{2,1,0:T(8,128)(2,1)S(1)} %get-tuple-element.136), channel_id=1, source_target_pairs={{0,8},{1,9},{2,10},{3,11},{4,12},{5,13},{6,14},{7,15},{8,0},{9,1},... | collective-permute-start | bytes 1572872 | tf_op jit(solution)/shard_map/ppermute | solution.py:48
  131.9 4.4 %shard_map.98 = bf16[224,8192]{1,0:T(8,128)(2,1)} custom-call(s32[40]{0:T(128)S(1)} %pad_add_fusion.tab, bf16[224,512]{1,0:T(8,128)(2,1)S(1)} %get-tuple-element.137.ht_ref, bf16[4,256,512]{2,1,0:T(8,128)(2,1)S(1)} %pad_maximum_fusion.1.refs_2_.refs_0_, bf16[4,256,512]{2,1,0:T(8,128)(2,1)S(1)} %copy-done.10, ...), custom_call_target="tpu_custom_call" | custom-call | flops 1879048192 | bytes 6291456 | tf_op jit(solution)/shard_map/pallas_call | solution.py:173
  136.3 6.6 %collective-permute-done.31.d = bf16[4,128,512]{2,1,0:T(8,128)(2,1)S(1)} collective-permute-done((bf16[4,128,512]{2,1,0:T(8,128)(2,1)S(1)}, bf16[4,128,512]{2,1,0:T(8,128)(2,1)S(1)}, u32[]{:S(2)}, u32[]{:S(2)}) %collective-permute-start.31) | collective-permute-done | bytes 524320 | tf_op jit(solution)/shard_map/ppermute | solution.py:48
  143.3 1.1 collective-permute-start.36
  144.4 2.2 %collective-permute-start.37 = (bf16[128,512]{1,0:T(8,128)(2,1)S(1)}, bf16[128,512]{1,0:T(8,128)(2,1)S(1)}, u32[]{:S(2)}, u32[]{:S(2)}) collective-permute-start(bf16[128,512]{1,0:T(8,128)(2,1)S(1)} %get-tuple-element.149), channel_id=1, source_target_pairs={{0,3},{1,0},{2,1},{3,2},{4,7},{5,4},{6,5},{7,6},{8,11},{9,8},{10,9... | collective-permute-start | bytes 393224 | tf_op jit(solution)/shard_map/ppermute | solution.py:48
  146.6 1.9 %collective-permute-start.38 = (bf16[128,512]{1,0:T(8,128)(2,1)S(1)}, bf16[128,512]{1,0:T(8,128)(2,1)S(1)}, u32[]{:S(2)}, u32[]{:S(2)}) collective-permute-start(bf16[128,512]{1,0:T(8,128)(2,1)S(1)} %get-tuple-element.150), channel_id=1, source_target_pairs={{0,2},{1,3},{2,0},{3,1},{4,6},{5,7},{6,4},{7,5},{8,10},{9,11},{10,... | collective-permute-start | bytes 393224 | tf_op jit(solution)/shard_map/ppermute | solution.py:48
  148.8 0.9 collective-permute-start.33
  149.7 2.4 %collective-permute-start.34 = (bf16[128,512]{1,0:T(8,128)(2,1)S(1)}, bf16[128,512]{1,0:T(8,128)(2,1)S(1)}, u32[]{:S(2)}, u32[]{:S(2)}) collective-permute-start(bf16[128,512]{1,0:T(8,128)(2,1)S(1)} %get-tuple-element.141), channel_id=1, source_target_pairs={{0,12},{1,13},{2,14},{3,15},{4,0},{5,1},{6,2},{7,3},{8,4},{9,5},{1... | collective-permute-start | bytes 393224 | tf_op jit(solution)/shard_map/ppermute | solution.py:48
  152.1 1.1 collective-permute-start.35
  153.2 2.2 %collective-permute-done.33.refs_1_ = bf16[128,512]{1,0:T(8,128)(2,1)S(1)} collective-permute-done((bf16[128,512]{1,0:T(8,128)(2,1)S(1)}, bf16[128,512]{1,0:T(8,128)(2,1)S(1)}, u32[]{:S(2)}, u32[]{:S(2)}) %collective-permute-start.33) | collective-permute-done | bytes 131104 | tf_op jit(solution)/shard_map/ppermute | solution.py:48
  155.4 3.2 %collective-permute-done.35.refs_3_ = bf16[128,512]{1,0:T(8,128)(2,1)S(1)} collective-permute-done((bf16[128,512]{1,0:T(8,128)(2,1)S(1)}, bf16[128,512]{1,0:T(8,128)(2,1)S(1)}, u32[]{:S(2)}, u32[]{:S(2)}) %collective-permute-start.35) | collective-permute-done | bytes 131104 | tf_op jit(solution)/shard_map/ppermute | solution.py:48
  158.7 1.3 collective-permute-start.39
  160.0 2.0 %collective-permute-start.40 = (bf16[64,512]{1,0:T(8,128)(2,1)S(1)}, bf16[64,512]{1,0:T(8,128)(2,1)S(1)}, u32[]{:S(2)}, u32[]{:S(2)}) collective-permute-start(bf16[64,512]{1,0:T(8,128)(2,1)S(1)} %get-tuple-element.153), channel_id=1, source_target_pairs={{0,96},{16,112},{32,0},{48,16},{64,32},{80,48},{96,64},{112,80},{1... | collective-permute-start | bytes 196616 | tf_op jit(solution)/shard_map/ppermute | solution.py:48
  162.0 1.1 collective-permute-start.41
  163.1 1.2 collective-permute-done.39
  164.3 3.5 %collective-permute-done.41 = bf16[64,512]{1,0:T(8,128)(2,1)S(1)} collective-permute-done((bf16[64,512]{1,0:T(8,128)(2,1)S(1)}, bf16[64,512]{1,0:T(8,128)(2,1)S(1)}, u32[]{:S(2)}, u32[]{:S(2)}) %collective-permute-start.41) | collective-permute-done | bytes 65568 | tf_op jit(solution)/shard_map/ppermute | solution.py:48
  167.8 0.7 add_convert_fusion
  (95 shorter events, 6.2 us)
Async XLA Ops:
  0.6 13.8 %collective-permute-start.3 = (bf16[224,8192]{1,0:T(8,128)(2,1)}, bf16[224,8192]{1,0:T(8,128)(2,1)S(1)}, u32[]{:S(2)}, u32[]{:S(2)}) collective-permute-start(bf16[224,8192]{1,0:T(8,128)(2,1)} %refs_0_.1), channel_id=1, source_target_pairs={{0,16},{16,0},{32,48},{48,32},{64,80},{80,64},{96,112},{112,96},{1... | collective-permute-start | bytes 11010056 | tf_op jit(solution)/shard_map/ppermute | solution.py:48
  0.7 15.5 %collective-permute-start.4 = (bf16[224,8192]{1,0:T(8,128)(2,1)}, bf16[224,8192]{1,0:T(8,128)(2,1)S(1)}, u32[]{:S(2)}, u32[]{:S(2)}) collective-permute-start(bf16[224,8192]{1,0:T(8,128)(2,1)} %refs_1_.1), channel_id=1, source_target_pairs={{0,16},{16,0},{32,48},{48,32},{64,80},{80,64},{96,112},{112,96},{1... | collective-permute-start | bytes 11010056 | tf_op jit(solution)/shard_map/ppermute | solution.py:48
  2.8 7.3 %collective-permute-start.2 = (bf16[144,512]{1,0:T(8,128)(2,1)S(1)}, bf16[144,512]{1,0:T(8,128)(2,1)S(1)}, u32[]{:S(2)}, u32[]{:S(2)}) collective-permute-start(bf16[144,512]{1,0:T(8,128)(2,1)S(1)} %fusion.1), channel_id=1, source_target_pairs={{0,32},{16,48},{32,64},{48,80},{64,96},{80,112},{96,0},{112,16},{1... | collective-permute-start | bytes 442376 | tf_op jit(solution)/shard_map/ppermute | solution.py:48
  4.5 9.9 %collective-permute-start.1 = (bf16[144,512]{1,0:T(8,128)(2,1)S(1)}, bf16[144,512]{1,0:T(8,128)(2,1)S(1)}, u32[]{:S(2)}, u32[]{:S(2)}) collective-permute-start(bf16[144,512]{1,0:T(8,128)(2,1)S(1)} %fusion.1), channel_id=1, source_target_pairs={{0,64},{16,80},{32,96},{48,112},{64,0},{80,16},{96,32},{112,48},{1... | collective-permute-start | bytes 442376 | tf_op jit(solution)/shard_map/ppermute | solution.py:48
  7.4 7.0 %collective-permute-start = (bf16[144,512]{1,0:T(8,128)(2,1)S(1)}, bf16[144,512]{1,0:T(8,128)(2,1)S(1)}, u32[]{:S(2)}, u32[]{:S(2)}) collective-permute-start(bf16[144,512]{1,0:T(8,128)(2,1)S(1)} %fusion.1), channel_id=1, source_target_pairs={{0,96},{16,112},{32,0},{48,16},{64,32},{80,48},{96,64},{112,80},{1... | collective-permute-start | bytes 442376 | tf_op jit(solution)/shard_map/ppermute | solution.py:48
  14.4 1.8 %copy-start.11 = (bf16[224,8192]{1,0:T(8,128)(2,1)}, bf16[224,8192]{1,0:T(8,128)(2,1)S(1)}, u32[]{:S(2)}) copy-start(bf16[224,8192]{1,0:T(8,128)(2,1)S(1)} %collective-permute-done.3.refs_2_) | copy-start | bytes 11010052
  16.2 1.8 %copy-start.13 = (bf16[224,8192]{1,0:T(8,128)(2,1)}, bf16[224,8192]{1,0:T(8,128)(2,1)S(1)}, u32[]{:S(2)}) copy-start(bf16[224,8192]{1,0:T(8,128)(2,1)S(1)} %collective-permute-done.4.refs_3_) | copy-start | bytes 11010052
  18.1 13.5 %collective-permute-start.5 = (bf16[256,512]{1,0:T(8,128)(2,1)S(1)}, bf16[256,512]{1,0:T(8,128)(2,1)S(1)}, u32[]{:S(2)}, u32[]{:S(2)}) collective-permute-start(bf16[256,512]{1,0:T(8,128)(2,1)S(1)} %pad_maximum_fusion.2), channel_id=1, source_target_pairs={{0,3},{1,0},{2,1},{3,2},{4,7},{5,4},{6,5},{7,6},{8,11},{9,8},{10,9... | collective-permute-start | bytes 786440 | tf_op jit(solution)/shard_map/ppermute | solution.py:48
  21.0 14.0 %collective-permute-start.7 = (bf16[256,512]{1,0:T(8,128)(2,1)S(1)}, bf16[256,512]{1,0:T(8,128)(2,1)S(1)}, u32[]{:S(2)}, u32[]{:S(2)}) collective-permute-start(bf16[256,512]{1,0:T(8,128)(2,1)S(1)} %pad_maximum_fusion.2), channel_id=1, source_target_pairs={{0,1},{1,2},{2,3},{3,0},{4,5},{5,6},{6,7},{7,4},{8,9},{9,10},{10,1... | collective-permute-start | bytes 786440 | tf_op jit(solution)/shard_map/ppermute | solution.py:48
  21.0 14.0 %collective-permute-start.6 = (bf16[256,512]{1,0:T(8,128)(2,1)S(1)}, bf16[256,512]{1,0:T(8,128)(2,1)S(1)}, u32[]{:S(2)}, u32[]{:S(2)}) collective-permute-start(bf16[256,512]{1,0:T(8,128)(2,1)S(1)} %pad_maximum_fusion.2), channel_id=1, source_target_pairs={{0,2},{1,3},{2,0},{3,1},{4,6},{5,7},{6,4},{7,5},{8,10},{9,11},{10,... | collective-permute-start | bytes 786440 | tf_op jit(solution)/shard_map/ppermute | solution.py:48
  23.3 11.7 %collective-permute-start.9 = (bf16[256,512]{1,0:T(8,128)(2,1)S(1)}, bf16[256,512]{1,0:T(8,128)(2,1)S(1)}, u32[]{:S(2)}, u32[]{:S(2)}) collective-permute-start(bf16[256,512]{1,0:T(8,128)(2,1)S(1)} %pad_maximum_fusion.3), channel_id=1, source_target_pairs={{0,8},{1,9},{2,10},{3,11},{4,12},{5,13},{6,14},{7,15},{8,0},{9,1},... | collective-permute-start | bytes 786440 | tf_op jit(solution)/shard_map/ppermute | solution.py:48
  27.2 11.3 %collective-permute-start.8 = (bf16[256,512]{1,0:T(8,128)(2,1)S(1)}, bf16[256,512]{1,0:T(8,128)(2,1)S(1)}, u32[]{:S(2)}, u32[]{:S(2)}) collective-permute-start(bf16[256,512]{1,0:T(8,128)(2,1)S(1)} %pad_maximum_fusion.3), channel_id=1, source_target_pairs={{0,12},{1,13},{2,14},{3,15},{4,0},{5,1},{6,2},{7,3},{8,4},{9,5},{1... | collective-permute-start | bytes 786440 | tf_op jit(solution)/shard_map/ppermute | solution.py:48
  31.6 8.4 %collective-permute-start.10 = (bf16[256,512]{1,0:T(8,128)(2,1)S(1)}, bf16[256,512]{1,0:T(8,128)(2,1)S(1)}, u32[]{:S(2)}, u32[]{:S(2)}) collective-permute-start(bf16[256,512]{1,0:T(8,128)(2,1)S(1)} %pad_maximum_fusion.3), channel_id=1, source_target_pairs={{0,4},{1,5},{2,6},{3,7},{4,8},{5,9},{6,10},{7,11},{8,12},{9,13},{1... | collective-permute-start | bytes 786440 | tf_op jit(solution)/shard_map/ppermute | solution.py:48
  40.1 5.7 %collective-permute-start.16 = (bf16[4,256,512]{2,1,0:T(8,128)(2,1)S(1)}, bf16[4,256,512]{2,1,0:T(8,128)(2,1)S(1)}, u32[]{:S(2)}, u32[]{:S(2)}) collective-permute-start(bf16[4,256,512]{2,1,0:T(8,128)(2,1)S(1)} %pad_maximum_fusion.1.refs_2_.refs_0_), channel_id=1, source_target_pairs={{0,16},{16,0},{32,48},{48,32},{64,80},{80,64},{96,112},{112,96},{1... | collective-permute-start | bytes 3145736 | tf_op jit(solution)/shard_map/ppermute | solution.py:48
  41.3 9.1 %collective-permute-start.15 = (bf16[4,256,512]{2,1,0:T(8,128)(2,1)}, bf16[4,256,512]{2,1,0:T(8,128)(2,1)}, u32[]{:S(2)}, u32[]{:S(2)}) collective-permute-start(bf16[4,256,512]{2,1,0:T(8,128)(2,1)} %pad_maximum_fusion.refs_0_), channel_id=1, source_target_pairs={{0,16},{16,0},{32,48},{48,32},{64,80},{80,64},{96,112},{112,96},{1... | collective-permute-start | bytes 3145736 | tf_op jit(solution)/shard_map/ppermute | solution.py:48
  41.9 3.8 %collective-permute-start.17 = (bf16[1,256]{1,0:T(2,128)(2,1)S(1)}, bf16[1,256]{1,0:T(2,128)(2,1)S(1)}, u32[]{:S(2)}, u32[]{:S(2)}) collective-permute-start(bf16[1,256]{1,0:T(2,128)(2,1)S(1)} %pad_maximum_fusion.4), channel_id=1, source_target_pairs={{0,16},{16,0},{32,48},{48,32},{64,80},{80,64},{96,112},{112,96},{1... | collective-permute-start | bytes 1544 | tf_op jit(solution)/shard_map/ppermute | solution.py:48
  42.0 27.5 %collective-permute-start.14 = (bf16[4,256,512]{2,1,0:T(8,128)(2,1)S(1)}, bf16[4,256,512]{2,1,0:T(8,128)(2,1)S(1)}, u32[]{:S(2)}, u32[]{:S(2)}) collective-permute-start(bf16[4,256,512]{2,1,0:T(8,128)(2,1)S(1)} %pad_maximum_fusion.1.refs_2_.refs_0_), channel_id=1, source_target_pairs={{0,1},{1,2},{2,3},{3,0},{4,5},{5,6},{6,7},{7,4},{8,9},{9,10},{10,1... | collective-permute-start | bytes 3145736 | tf_op jit(solution)/shard_map/ppermute | solution.py:48
  42.4 27.1 %collective-permute-start.13 = (bf16[4,256,512]{2,1,0:T(8,128)(2,1)S(1)}, bf16[4,256,512]{2,1,0:T(8,128)(2,1)S(1)}, u32[]{:S(2)}, u32[]{:S(2)}) collective-permute-start(bf16[4,256,512]{2,1,0:T(8,128)(2,1)S(1)} %pad_maximum_fusion.1.refs_2_.refs_0_), channel_id=1, source_target_pairs={{0,3},{1,0},{2,1},{3,2},{4,7},{5,4},{6,5},{7,6},{8,11},{9,8},{10,9... | collective-permute-start | bytes 3145736 | tf_op jit(solution)/shard_map/ppermute | solution.py:48
  45.8 26.7 %collective-permute-start.12 = (bf16[4,256,512]{2,1,0:T(8,128)(2,1)}, bf16[4,256,512]{2,1,0:T(8,128)(2,1)}, u32[]{:S(2)}, u32[]{:S(2)}) collective-permute-start(bf16[4,256,512]{2,1,0:T(8,128)(2,1)} %pad_maximum_fusion.refs_0_), channel_id=1, source_target_pairs={{0,4},{1,5},{2,6},{3,7},{4,8},{5,9},{6,10},{7,11},{8,12},{9,13},{1... | collective-permute-start | bytes 3145736 | tf_op jit(solution)/shard_map/ppermute | solution.py:48
  45.8 1.0 copy-start.8
  46.8 25.9 %collective-permute-start.11 = (bf16[4,256,512]{2,1,0:T(8,128)(2,1)}, bf16[4,256,512]{2,1,0:T(8,128)(2,1)}, u32[]{:S(2)}, u32[]{:S(2)}) collective-permute-start(bf16[4,256,512]{2,1,0:T(8,128)(2,1)} %pad_maximum_fusion.refs_0_), channel_id=1, source_target_pairs={{0,12},{1,13},{2,14},{3,15},{4,0},{5,1},{6,2},{7,3},{8,4},{9,5},{1... | collective-permute-start | bytes 3145736 | tf_op jit(solution)/shard_map/ppermute | solution.py:48
  50.5 2.0 %copy-start = (bf16[224,8192]{1,0:T(8,128)(2,1)S(1)}, bf16[224,8192]{1,0:T(8,128)(2,1)}, u32[]{:S(2)}) copy-start(bf16[224,8192]{1,0:T(8,128)(2,1)} %refs_0_.1) | copy-start | bytes 11010052
  52.5 2.0 %copy-start.2 = (bf16[224,8192]{1,0:T(8,128)(2,1)S(1)}, bf16[224,8192]{1,0:T(8,128)(2,1)}, u32[]{:S(2)}) copy-start(bf16[224,8192]{1,0:T(8,128)(2,1)} %refs_1_.1) | copy-start | bytes 11010052
  54.6 2.0 %copy-start.5 = (bf16[224,8192]{1,0:T(8,128)(2,1)S(1)}, bf16[224,8192]{1,0:T(8,128)(2,1)}, u32[]{:S(2)}) copy-start(bf16[224,8192]{1,0:T(8,128)(2,1)} %wd.5) | copy-start | bytes 11010052
  56.6 1.2 copy-start.9
  62.1 0.8 copy-start.15
  62.9 0.8 copy-start.17
  63.6 0.8 copy-start.19
  72.7 4.5 %collective-permute-start.20 = (bf16[4,256,512]{2,1,0:T(8,128)(2,1)}, bf16[4,256,512]{2,1,0:T(8,128)(2,1)}, u32[]{:S(2)}, u32[]{:S(2)}) collective-permute-start(bf16[4,256,512]{2,1,0:T(8,128)(2,1)} %collective-permute-done.11.refs_0_.refs_2_), channel_id=1, source_target_pairs={{0,16},{16,0},{32,48},{48,32},{64,80},{80,64},{96,112},{112,96},{1... | collective-permute-start | bytes 3145736 | tf_op jit(solution)/shard_map/ppermute | solution.py:48
  72.7 8.5 %copy-start.1 = (bf16[224,8192]{1,0:T(8,128)(2,1)S(1)}, bf16[224,8192]{1,0:T(8,128)(2,1)}, u32[]{:S(2)}) copy-start(bf16[224,8192]{1,0:T(8,128)(2,1)} %refs_0_.1) | copy-start | bytes 11010052
  72.7 8.5 %copy-start.16 = (f32[224,512]{1,0:T(8,128)S(1)}, f32[224,512]{1,0:T(8,128)}, u32[]{:S(2)}) copy-start(f32[224,512]{1,0:T(8,128)} %copy-done.15) | copy-start | bytes 1376260
  72.7 8.5 %copy-start.18 = (f32[224,512]{1,0:T(8,128)S(1)}, f32[224,512]{1,0:T(8,128)}, u32[]{:S(2)}) copy-start(f32[224,512]{1,0:T(8,128)} %copy-done.17) | copy-start | bytes 1376260
  72.7 8.5 %copy-start.20 = (f32[224,512]{1,0:T(8,128)S(1)}, f32[224,512]{1,0:T(8,128)}, u32[]{:S(2)}) copy-start(f32[224,512]{1,0:T(8,128)} %copy-done.19) | copy-start | bytes 1376260
  72.8 8.5 %collective-permute-start.21 = (bf16[4,256,512]{2,1,0:T(8,128)(2,1)S(1)}, bf16[4,256,512]{2,1,0:T(8,128)(2,1)S(1)}, u32[]{:S(2)}, u32[]{:S(2)}) collective-permute-start(bf16[4,256,512]{2,1,0:T(8,128)(2,1)S(1)} %collective-permute-done.13.refs_2_), channel_id=1, source_target_pairs={{0,16},{16,0},{32,48},{48,32},{64,80},{80,64},{96,112},{112,96},{1... | collective-permute-start | bytes 3145736 | tf_op jit(solution)/shard_map/ppermute | solution.py:48
  73.3 7.9 %collective-permute-start.23 = (bf16[4,256,512]{2,1,0:T(8,128)(2,1)S(1)}, bf16[4,256,512]{2,1,0:T(8,128)(2,1)S(1)}, u32[]{:S(2)}, u32[]{:S(2)}) collective-permute-start(bf16[4,256,512]{2,1,0:T(8,128)(2,1)S(1)} %collective-permute-done.14.refs_6_), channel_id=1, source_target_pairs={{0,16},{16,0},{32,48},{48,32},{64,80},{80,64},{96,112},{112,96},{1... | collective-permute-start | bytes 3145736 | tf_op jit(solution)/shard_map/ppermute | solution.py:48
  73.5 19.0 %collective-permute-start.19 = (bf16[4,256,512]{2,1,0:T(8,128)(2,1)S(1)}, bf16[4,256,512]{2,1,0:T(8,128)(2,1)S(1)}, u32[]{:S(2)}, u32[]{:S(2)}) collective-permute-start(bf16[4,256,512]{2,1,0:T(8,128)(2,1)S(1)} %broadcast_select_fusion), channel_id=1, source_target_pairs={{0,3},{1,0},{2,1},{3,2},{4,7},{5,4},{6,5},{7,6},{8,11},{9,8},{10,9... | collective-permute-start | bytes 3145736 | tf_op jit(solution)/shard_map/ppermute | solution.py:43
  75.9 5.3 %collective-permute-start.22 = (bf16[4,256,512]{2,1,0:T(8,128)(2,1)}, bf16[4,256,512]{2,1,0:T(8,128)(2,1)S(1)}, u32[]{:S(2)}, u32[]{:S(2)}) collective-permute-start(bf16[4,256,512]{2,1,0:T(8,128)(2,1)} %collective-permute-done.12.refs_4_.refs_6_), channel_id=1, source_target_pairs={{0,16},{16,0},{32,48},{48,32},{64,80},{80,64},{96,112},{112,96},{1... | collective-permute-start | bytes 3145736 | tf_op jit(solution)/shard_map/ppermute | solution.py:48
  77.3 16.3 %collective-permute-start.18 = (bf16[4,256,512]{2,1,0:T(8,128)(2,1)S(1)}, bf16[4,256,512]{2,1,0:T(8,128)(2,1)S(1)}, u32[]{:S(2)}, u32[]{:S(2)}) collective-permute-start(bf16[4,256,512]{2,1,0:T(8,128)(2,1)S(1)} %broadcast_select_fusion.1), channel_id=1, source_target_pairs={{0,12},{1,13},{2,14},{3,15},{4,0},{5,1},{6,2},{7,3},{8,4},{9,5},{1... | collective-permute-start | bytes 3145736 | tf_op jit(solution)/shard_map/ppermute | solution.py:43
  81.3 2.0 %copy-start.3 = (bf16[224,8192]{1,0:T(8,128)(2,1)S(1)}, bf16[224,8192]{1,0:T(8,128)(2,1)}, u32[]{:S(2)}) copy-start(bf16[224,8192]{1,0:T(8,128)(2,1)} %refs_1_.1) | copy-start | bytes 11010052
  83.3 2.0 %copy-start.6 = (bf16[224,8192]{1,0:T(8,128)(2,1)S(1)}, bf16[224,8192]{1,0:T(8,128)(2,1)}, u32[]{:S(2)}) copy-start(bf16[224,8192]{1,0:T(8,128)(2,1)} %wd.5) | copy-start | bytes 11010052
  85.4 12.4 %copy-start.4 = (bf16[224,8192]{1,0:T(8,128)(2,1)S(1)}, bf16[224,8192]{1,0:T(8,128)(2,1)}, u32[]{:S(2)}) copy-start(bf16[224,8192]{1,0:T(8,128)(2,1)} %refs_1_.1) | copy-start | bytes 11010052
  85.4 12.4 %copy-start.7 = (bf16[224,8192]{1,0:T(8,128)(2,1)S(1)}, bf16[224,8192]{1,0:T(8,128)(2,1)}, u32[]{:S(2)}) copy-start(bf16[224,8192]{1,0:T(8,128)(2,1)} %wd.5) | copy-start | bytes 11010052
  93.5 9.4 %copy-start.12 = (bf16[224,8192]{1,0:T(8,128)(2,1)S(1)}, bf16[224,8192]{1,0:T(8,128)(2,1)}, u32[]{:S(2)}) copy-start(bf16[224,8192]{1,0:T(8,128)(2,1)} %copy-done.11) | copy-start | bytes 11010052
  93.5 9.4 %copy-start.14 = (bf16[224,8192]{1,0:T(8,128)(2,1)S(1)}, bf16[224,8192]{1,0:T(8,128)(2,1)}, u32[]{:S(2)}) copy-start(bf16[224,8192]{1,0:T(8,128)(2,1)} %copy-done.13) | copy-start | bytes 11010052
  93.5 2.7 %collective-permute-start.24 = (bf16[4,256,512]{2,1,0:T(8,128)(2,1)S(1)}, bf16[4,256,512]{2,1,0:T(8,128)(2,1)S(1)}, u32[]{:S(2)}, u32[]{:S(2)}) collective-permute-start(bf16[4,256,512]{2,1,0:T(8,128)(2,1)S(1)} %collective-permute-done.18.refs_0_.refs_4_), channel_id=1, source_target_pairs={{0,16},{16,0},{32,48},{48,32},{64,80},{80,64},{96,112},{112,96},{1... | collective-permute-start | bytes 3145736 | tf_op jit(solution)/shard_map/ppermute | solution.py:48
  93.6 4.1 %collective-permute-start.25 = (bf16[4,256,512]{2,1,0:T(8,128)(2,1)S(1)}, bf16[4,256,512]{2,1,0:T(8,128)(2,1)S(1)}, u32[]{:S(2)}, u32[]{:S(2)}) collective-permute-start(bf16[4,256,512]{2,1,0:T(8,128)(2,1)S(1)} %collective-permute-done.19.refs_2_.refs_4_), channel_id=1, source_target_pairs={{0,16},{16,0},{32,48},{48,32},{64,80},{80,64},{96,112},{112,96},{1... | collective-permute-start | bytes 3145736 | tf_op jit(solution)/shard_map/ppermute | solution.py:48
  101.3 1.6 collective-permute-start.26
  109.9 16.0 %collective-permute-start.27 = (bf16[4,128,512]{2,1,0:T(8,128)(2,1)S(1)}, bf16[4,128,512]{2,1,0:T(8,128)(2,1)S(1)}, u32[]{:S(2)}, u32[]{:S(2)}) collective-permute-start(bf16[4,128,512]{2,1,0:T(8,128)(2,1)S(1)} %get-tuple-element.121), channel_id=1, source_target_pairs={{0,1},{1,2},{2,3},{3,0},{4,5},{5,6},{6,7},{7,4},{8,9},{9,10},{10,1... | collective-permute-start | bytes 1572872 | tf_op jit(solution)/shard_map/ppermute | solution.py:48
  110.0 15.9 %collective-permute-start.28 = (bf16[4,128,512]{2,1,0:T(8,128)(2,1)S(1)}, bf16[4,128,512]{2,1,0:T(8,128)(2,1)S(1)}, u32[]{:S(2)}, u32[]{:S(2)}) collective-permute-start(bf16[4,128,512]{2,1,0:T(8,128)(2,1)S(1)} %get-tuple-element.122), channel_id=1, source_target_pairs={{0,3},{1,0},{2,1},{3,2},{4,7},{5,4},{6,5},{7,6},{8,11},{9,8},{10,9... | collective-permute-start | bytes 1572872 | tf_op jit(solution)/shard_map/ppermute | solution.py:48
  113.3 15.4 %collective-permute-start.29 = (bf16[4,128,512]{2,1,0:T(8,128)(2,1)S(1)}, bf16[4,128,512]{2,1,0:T(8,128)(2,1)S(1)}, u32[]{:S(2)}, u32[]{:S(2)}) collective-permute-start(bf16[4,128,512]{2,1,0:T(8,128)(2,1)S(1)} %get-tuple-element.123), channel_id=1, source_target_pairs={{0,4},{1,5},{2,6},{3,7},{4,8},{5,9},{6,10},{7,11},{8,12},{9,13},{1... | collective-permute-start | bytes 1572872 | tf_op jit(solution)/shard_map/ppermute | solution.py:48
  113.3 15.4 %collective-permute-start.30 = (bf16[4,128,512]{2,1,0:T(8,128)(2,1)S(1)}, bf16[4,128,512]{2,1,0:T(8,128)(2,1)S(1)}, u32[]{:S(2)}, u32[]{:S(2)}) collective-permute-start(bf16[4,128,512]{2,1,0:T(8,128)(2,1)S(1)} %get-tuple-element.124), channel_id=1, source_target_pairs={{0,12},{1,13},{2,14},{3,15},{4,0},{5,1},{6,2},{7,3},{8,4},{9,5},{1... | collective-permute-start | bytes 1572872 | tf_op jit(solution)/shard_map/ppermute | solution.py:48
  116.9 15.0 %copy-start.10 = (bf16[4,256,512]{2,1,0:T(8,128)(2,1)S(1)}, bf16[4,256,512]{2,1,0:T(8,128)(2,1)}, u32[]{:S(2)}) copy-start(bf16[4,256,512]{2,1,0:T(8,128)(2,1)} %copy-done.8) | copy-start | bytes 3145732
  128.6 14.3 %collective-permute-start.31 = (bf16[4,128,512]{2,1,0:T(8,128)(2,1)S(1)}, bf16[4,128,512]{2,1,0:T(8,128)(2,1)S(1)}, u32[]{:S(2)}, u32[]{:S(2)}) collective-permute-start(bf16[4,128,512]{2,1,0:T(8,128)(2,1)S(1)} %get-tuple-element.135), channel_id=1, source_target_pairs={{0,2},{1,3},{2,0},{3,1},{4,6},{5,7},{6,4},{7,5},{8,10},{9,11},{10,... | collective-permute-start | bytes 1572872 | tf_op jit(solution)/shard_map/ppermute | solution.py:48
  129.0 14.0 %collective-permute-start.32 = (bf16[4,128,512]{2,1,0:T(8,128)(2,1)S(1)}, bf16[4,128,512]{2,1,0:T(8,128)(2,1)S(1)}, u32[]{:S(2)}, u32[]{:S(2)}) collective-permute-start(bf16[4,128,512]{2,1,0:T(8,128)(2,1)S(1)} %get-tuple-element.136), channel_id=1, source_target_pairs={{0,8},{1,9},{2,10},{3,11},{4,12},{5,13},{6,14},{7,15},{8,0},{9,1},... | collective-permute-start | bytes 1572872 | tf_op jit(solution)/shard_map/ppermute | solution.py:48
  143.3 8.8 %collective-permute-start.36 = (bf16[128,512]{1,0:T(8,128)(2,1)S(1)}, bf16[128,512]{1,0:T(8,128)(2,1)S(1)}, u32[]{:S(2)}, u32[]{:S(2)}) collective-permute-start(bf16[128,512]{1,0:T(8,128)(2,1)S(1)} %get-tuple-element.148), channel_id=1, source_target_pairs={{0,1},{1,2},{2,3},{3,0},{4,5},{5,6},{6,7},{7,4},{8,9},{9,10},{10,1... | collective-permute-start | bytes 393224 | tf_op jit(solution)/shard_map/ppermute | solution.py:48
  144.4 8.8 %collective-permute-start.37 = (bf16[128,512]{1,0:T(8,128)(2,1)S(1)}, bf16[128,512]{1,0:T(8,128)(2,1)S(1)}, u32[]{:S(2)}, u32[]{:S(2)}) collective-permute-start(bf16[128,512]{1,0:T(8,128)(2,1)S(1)} %get-tuple-element.149), channel_id=1, source_target_pairs={{0,3},{1,0},{2,1},{3,2},{4,7},{5,4},{6,5},{7,6},{8,11},{9,8},{10,9... | collective-permute-start | bytes 393224 | tf_op jit(solution)/shard_map/ppermute | solution.py:48
  146.6 6.6 %collective-permute-start.38 = (bf16[128,512]{1,0:T(8,128)(2,1)S(1)}, bf16[128,512]{1,0:T(8,128)(2,1)S(1)}, u32[]{:S(2)}, u32[]{:S(2)}) collective-permute-start(bf16[128,512]{1,0:T(8,128)(2,1)S(1)} %get-tuple-element.150), channel_id=1, source_target_pairs={{0,2},{1,3},{2,0},{3,1},{4,6},{5,7},{6,4},{7,5},{8,10},{9,11},{10,... | collective-permute-start | bytes 393224 | tf_op jit(solution)/shard_map/ppermute | solution.py:48
  148.8 6.6 %collective-permute-start.33 = (bf16[128,512]{1,0:T(8,128)(2,1)S(1)}, bf16[128,512]{1,0:T(8,128)(2,1)S(1)}, u32[]{:S(2)}, u32[]{:S(2)}) collective-permute-start(bf16[128,512]{1,0:T(8,128)(2,1)S(1)} %get-tuple-element.140), channel_id=1, source_target_pairs={{0,4},{1,5},{2,6},{3,7},{4,8},{5,9},{6,10},{7,11},{8,12},{9,13},{1... | collective-permute-start | bytes 393224 | tf_op jit(solution)/shard_map/ppermute | solution.py:48
  149.7 5.7 %collective-permute-start.34 = (bf16[128,512]{1,0:T(8,128)(2,1)S(1)}, bf16[128,512]{1,0:T(8,128)(2,1)S(1)}, u32[]{:S(2)}, u32[]{:S(2)}) collective-permute-start(bf16[128,512]{1,0:T(8,128)(2,1)S(1)} %get-tuple-element.141), channel_id=1, source_target_pairs={{0,12},{1,13},{2,14},{3,15},{4,0},{5,1},{6,2},{7,3},{8,4},{9,5},{1... | collective-permute-start | bytes 393224 | tf_op jit(solution)/shard_map/ppermute | solution.py:48
  152.1 6.5 %collective-permute-start.35 = (bf16[128,512]{1,0:T(8,128)(2,1)S(1)}, bf16[128,512]{1,0:T(8,128)(2,1)S(1)}, u32[]{:S(2)}, u32[]{:S(2)}) collective-permute-start(bf16[128,512]{1,0:T(8,128)(2,1)S(1)} %get-tuple-element.142), channel_id=1, source_target_pairs={{0,8},{1,9},{2,10},{3,11},{4,12},{5,13},{6,14},{7,15},{8,0},{9,1},... | collective-permute-start | bytes 393224 | tf_op jit(solution)/shard_map/ppermute | solution.py:48
  158.7 5.5 %collective-permute-start.39 = (bf16[64,512]{1,0:T(8,128)(2,1)S(1)}, bf16[64,512]{1,0:T(8,128)(2,1)S(1)}, u32[]{:S(2)}, u32[]{:S(2)}) collective-permute-start(bf16[64,512]{1,0:T(8,128)(2,1)S(1)} %get-tuple-element.152), channel_id=1, source_target_pairs={{0,32},{16,48},{32,64},{48,80},{64,96},{80,112},{96,0},{112,16},{1... | collective-permute-start | bytes 196616 | tf_op jit(solution)/shard_map/ppermute | solution.py:48
  160.0 4.3 %collective-permute-start.40 = (bf16[64,512]{1,0:T(8,128)(2,1)S(1)}, bf16[64,512]{1,0:T(8,128)(2,1)S(1)}, u32[]{:S(2)}, u32[]{:S(2)}) collective-permute-start(bf16[64,512]{1,0:T(8,128)(2,1)S(1)} %get-tuple-element.153), channel_id=1, source_target_pairs={{0,96},{16,112},{32,0},{48,16},{64,32},{80,48},{96,64},{112,80},{1... | collective-permute-start | bytes 196616 | tf_op jit(solution)/shard_map/ppermute | solution.py:48
  162.0 5.8 %collective-permute-start.41 = (bf16[64,512]{1,0:T(8,128)(2,1)S(1)}, bf16[64,512]{1,0:T(8,128)(2,1)S(1)}, u32[]{:S(2)}, u32[]{:S(2)}) collective-permute-start(bf16[64,512]{1,0:T(8,128)(2,1)S(1)} %get-tuple-element.154), channel_id=1, source_target_pairs={{0,64},{16,80},{32,96},{48,112},{64,0},{80,16},{96,32},{112,48},{1... | collective-permute-start | bytes 196616 | tf_op jit(solution)/shard_map/ppermute | solution.py:48

commit v3 on v2

v3 whole, which is shorter than its diff:
```python
import functools

import jax
import jax.numpy as jnp
from jax import lax
from jax.experimental import pallas as pl
from jax.experimental.pallas import tpu as pltpu
from jax.sharding import PartitionSpec as P

F32 = jnp.float32
BF16 = jnp.bfloat16
NT = (((1,), (1,)), ((), ()))
NN = (((1,), (0,)), ((), ()))
SIDE = 4
wait = lax.optimization_barrier
BLOCK = 512
MIB = 2**20


def dot(a, b, dims):
    return lax.dot_general(a, b, dims, preferred_element_type=F32)


def moves(axis, step):
    if axis == "x":
        return "shard", [(z * 4 + x, z * 4 + (x + step) % 4) for z in range(4) for x in range(4)]
    if axis == "z":
        return "shard", [(z * 4 + x, (z + step) % 4 * 4 + x) for z in range(4) for x in range(4)]
    if axis == "y":
        return "cuts", [(y * 2 + c, (y + step) % 4 * 2 + c) for y in range(4) for c in range(2)]
    return "cuts", [(y * 2 + c, y * 2 + 1 - c) for y in range(4) for c in range(2)]


def hop(value, axis, way):
    pairs = []
    for y in range(4):
        for c in range(2):
            for z in range(4):
                for x in range(4):
                    step = way * (2 * c - 1)
                    to_z, to_x = (z, (x + step) % 4) if axis == "x" else ((z + step) % 4, x)
                    pairs.append(((y * 2 + c) * 16 + z * 4 + x, (y * 2 + c) * 16 + to_z * 4 + to_x))
    return lax.ppermute(value, ("cuts", "shard"), pairs)


def shift(value, axis, step=1):
    name, pairs = moves(axis, step)
    return lax.ppermute(value, name, pairs)


VMEM = pl.BlockSpec(memory_space=pltpu.VMEM)
ANY = pl.BlockSpec(memory_space=pl.ANY)
SMEM = pl.BlockSpec(memory_space=pltpu.SMEM)


def lanes(tab, at):
    return pl.ds(pl.multiple_of(tab[at] * BLOCK, BLOCK), BLOCK)


def wide(tab, at):
    return pl.ds(pl.multiple_of(tab[at] * 4 * BLOCK, 4 * BLOCK), 4 * BLOCK)


def sigmoid(v):
    return 1.0 / (1.0 + jnp.exp(-v))


def copies_of(e, tab, wg, wu, wd, bg, bu, bd, sems):
    cols = wide(tab, 32 + e)
    return [
        [pltpu.make_async_copy(wg.at[:, cols], bg, sems.at[0])],
        [pltpu.make_async_copy(wu.at[:, cols], bu, sems.at[1])],
        [pltpu.make_async_copy(wd.at[:, lanes(tab, 16 + 4 * e + d)], bd.at[d], sems.at[2 + d]) for d in range(SIDE)],
    ]


def product(total, w, data):
    for d in range(SIDE):
        term = dot(w(d), data[d], NT)
        total = term if total is None else total + term
    return total


def forward_kernel(es, first, tab, wg, wu, wd, *refs):
    refs, (bg, bu, bd, sems) = refs[:-4], refs[-4:]
    pieces, refs = refs[:4 * len(es)], refs[4 * len(es):]
    before, outs = refs[:-2], refs[-2:]
    copies = [copies_of(e, tab, wg, wu, wd, bg.at[n], bu.at[n], bd.at[n], sems.at[n]) for n, e in enumerate(es)]
    for group in copies:
        for copy in sum(group, []):
            copy.start()
    for n in range(len(es)):
        for m in range(3):
            for copy in copies[n][m]:
                copy.wait()
            w = (lambda d: bd[n, d]) if m == 2 else (lambda d: (bg, bu)[m][n, :, lanes(tab, 36 + d)])
            for side in range(2):
                total = outs[side][m] if n else None if first else before[side][m]
                outs[side][m] = product(total, w, pieces[4 * n + 2 * (m // 2) + side])


def forward(es, tab, weights, pieces, before):
    count = len(es)
    operands = [tab, *weights, *pieces, *before]
    return pl.pallas_call(
        functools.partial(forward_kernel, es, not before),
        in_specs=[SMEM] + [ANY] * 3 + [VMEM] * (len(operands) - 4),
        out_specs=[VMEM] * 2,
        out_shape=[jax.ShapeDtypeStruct((3, 224, 256), F32)] * 2,
        scratch_shapes=[
            pltpu.VMEM((count, 224, 4 * BLOCK), BF16),
            pltpu.VMEM((count, 224, 4 * BLOCK), BF16),
            pltpu.VMEM((count, 4, 224, BLOCK), BF16),
            pltpu.SemaphoreType.DMA((count, 6)),
        ],
        compiler_params=pltpu.CompilerParams(vmem_limit_bytes=(6 + 7 * count) * MIB),
        cost_estimate=pl.CostEstimate(flops=count * 6 * 512 * 224 * 2048, bytes_accessed=count * 8 * MIB, transcendentals=0),
    )(*operands)


def finish_kernel(tab, wg, wu, wd, far_wg, far_wu, far_wd, x, g, own_sums, far_sums, keep_ref, *refs):
    (own_t, far_t, own_rows, far_rows), (bg, bu, bd, sems) = refs[:4], refs[4:]
    copies = copies_of(2, tab, wg, wu, wd, bg.at[0], bu.at[0], bd, sems.at[0])
    cols = wide(tab, 34)
    far_copies = [
        [pltpu.make_async_copy(far_wg.at[:, cols], bg.at[1], sems.at[1, 0])],
        [pltpu.make_async_copy(far_wu.at[:, cols], bu.at[1], sems.at[1, 1])],
        [],
    ]
    for group in (copies, far_copies):
        for copy in sum(group, []):
            copy.start()
    for side, (group, before, out_t, out_rows) in enumerate(
        ((copies, own_sums, own_t, own_rows), (far_copies, far_sums, far_t, far_rows))
    ):
        sums = []
        for m in range(3):
            for copy in group[m]:
                copy.wait()
            down = far_wd if side else bd
            w = (lambda d: down[d]) if m == 2 else (lambda d: (bg, bu)[m][side, :, lanes(tab, 36 + d)])
            sums.append(product(before[m], w, g if m == 2 else x))
        keep = keep_ref[side:side + 1]
        gv, uv, dhv = sums[0], sums[1], sums[2] * keep
        sig = sigmoid(gv)
        silu = gv * sig
        out_t[2] = (silu * uv * keep).astype(BF16)
        dg = dhv * uv * sig * (1.0 + gv * (1.0 - sig))
        du = dhv * silu
        for k, value in enumerate((dg, du)):
            out_t[k] = value.astype(BF16)
            turned = value.T.astype(BF16)
            for b in range(SIDE):
                for half in range(2):
                    low = b * 64 + half * 32
                    out_rows[k, half, b * 32:b * 32 + 32] = turned[low:low + 32]


def finish(tab, weights, far_weights, x, g, own_sums, far_sums, keep):
    return pl.pallas_call(
        finish_kernel,
        in_specs=[SMEM] + [ANY] * 5 + [VMEM] * 6,
        out_specs=[VMEM] * 4,
        out_shape=[jax.ShapeDtypeStruct((3, 224, 256), BF16)] * 2 + [jax.ShapeDtypeStruct((2, 2, 128, 224), BF16)] * 2,
        scratch_shapes=[
            pltpu.VMEM((2, 224, 4 * BLOCK), BF16),
            pltpu.VMEM((2, 224, 4 * BLOCK), BF16),
            pltpu.VMEM((4, 224, BLOCK), BF16),
            pltpu.SemaphoreType.DMA((2, 6)),
        ],
        compiler_params=pltpu.CompilerParams(vmem_limit_bytes=16 * MIB),
        cost_estimate=pl.CostEstimate(flops=6 * 512 * 224 * 2048, bytes_accessed=8 * MIB, transcendentals=2**17),
    )(tab, *weights, *far_weights, x, g, own_sums, far_sums, keep)


def cut_down(tab, wd):
    return pl.pallas_call(
        lambda tab, w, out: out.__setitem__(0, w[...]),
        grid_spec=pltpu.PrefetchScalarGridSpec(
            num_scalar_prefetch=1,
            grid=(SIDE,),
            in_specs=[pl.BlockSpec((224, BLOCK), lambda d, tab: (0, tab[24 + d]))],
            out_specs=pl.BlockSpec((1, 224, BLOCK), lambda d, tab: (d, 0, 0)),
        ),
        out_shape=jax.ShapeDtypeStruct((4, 224, BLOCK), BF16),
        compiler_params=pltpu.CompilerParams(vmem_limit_bytes=4 * MIB),
        cost_estimate=pl.CostEstimate(flops=0, bytes_accessed=2 * MIB, transcendentals=0),
    )(tab, wd)


def token_grad_kernel(tab, own_t, far_t, *refs):
    pieces, outs = refs[:8], refs[8:]
    for e in range(SIDE):
        @pl.when(pl.program_id(0) == e)
        def _(e=e):
            for d in range(SIDE):
                x0, x1 = pieces[2 * e][d], pieces[2 * e + 1][d]
                for k, out in enumerate(outs):
                    out[:, lanes(tab, 36 + d)] = (dot(own_t[k], x0, NN) + dot(far_t[k], x1, NN)).astype(BF16)


def down_grad_kernel(tab, own_t, far_t, *refs):
    pieces, out = refs[:8], refs[8]
    d = pl.program_id(0)
    for e in range(SIDE):
        g0, g1 = pieces[2 * e][d], pieces[2 * e + 1][d]
        out[:, lanes(tab, 44 + e)] = (dot(own_t[2], g0, NN) + dot(far_t[2], g1, NN)).astype(BF16)


def weight_grads(kernel, at, count, tab, rows, own, far):
    pieces = [p for e in range(SIDE) for p in (own[e], far[e])]
    return pl.pallas_call(
        kernel,
        grid_spec=pltpu.PrefetchScalarGridSpec(
            num_scalar_prefetch=1,
            grid=(SIDE,),
            in_specs=[VMEM] * (2 + len(pieces)),
            out_specs=[pl.BlockSpec((224, 4 * BLOCK), lambda k, tab: (0, tab[at + k]))] * count,
        ),
        out_shape=[jax.ShapeDtypeStruct((224, 8192), BF16)] * count,
        compiler_params=pltpu.CompilerParams(vmem_limit_bytes=14 * MIB),
        cost_estimate=pl.CostEstimate(flops=count * 2 * 512 * 224 * 8192, bytes_accessed=count * 6 * MIB, transcendentals=0),
    )(tab, *rows, *pieces)


def input_grad_kernel(tab, own_ref, far_ref, *refs):
    weights, outs, (held, sems) = refs[:4], refs[4:12], refs[12:]
    rows = [ref[k].reshape(256, 224) for ref in (own_ref, far_ref) for k in range(2)]

    def fetch(dz):
        return [
            pltpu.make_async_copy(w.at[:, wide(tab, 32 + dz)], held.at[dz % 2, n], sems.at[dz % 2, n])
            for n, w in enumerate(weights)
        ]

    copies = fetch(0)
    for copy in copies:
        copy.start()
    for dz in range(SIDE):
        current = copies
        if dz < SIDE - 1:
            copies = fetch(dz + 1)
            for copy in copies:
                copy.start()
        for copy in current:
            copy.wait()
        for dx in range(SIDE):
            cols = lanes(tab, 44 + dx)
            w = [held[dz % 2, n, :, cols] for n in range(4)]
            total = (dot(rows[0], w[0], NN) + dot(rows[1], w[1], NN)) + (dot(rows[2], w[2], NN) + dot(rows[3], w[3], NN))
            done = total.astype(BF16)
            outs[dx][dz] = done[:128]
            outs[4 + dz][dx] = done[128:]


def input_grads(tab, own, far, weights):
    return pl.pallas_call(
        input_grad_kernel,
        in_specs=[SMEM] + [VMEM] * 2 + [ANY] * 4,
        out_specs=[VMEM] * 8,
        out_shape=[jax.ShapeDtypeStruct((4, 128, BLOCK), BF16)] * 8,
        scratch_shapes=[pltpu.VMEM((2, 4, 224, 4 * BLOCK), BF16), pltpu.SemaphoreType.DMA((2, 4))],
        compiler_params=pltpu.CompilerParams(vmem_limit_bytes=16 * MIB),
        cost_estimate=pl.CostEstimate(flops=8 * 256 * 224 * 8192, bytes_accessed=18 * MIB, transcendentals=0),
    )(tab, own, far, *weights)


def add_kernel(a, b, out):
    out[...] = (a[...].astype(F32) + b[...].astype(F32)).astype(BF16)


def add_two(a, b):
    return pl.pallas_call(
        add_kernel,
        out_shape=jax.ShapeDtypeStruct(a.shape, BF16),
        compiler_params=pltpu.CompilerParams(vmem_limit_bytes=4 * MIB),
        cost_estimate=pl.CostEstimate(flops=4 * 128 * 512, bytes_accessed=3 * 2**19, transcendentals=0),
    )(a, b)


def sum_kernel(a, b, c, *outs):
    for k in range(SIDE):
        outs[k][...] = (a[k].astype(F32) + (b[k].astype(F32) + c[k].astype(F32))).astype(BF16)


def sum_apart(parts):
    return pl.pallas_call(
        sum_kernel,
        out_shape=[jax.ShapeDtypeStruct((128, BLOCK), BF16)] * 4,
        compiler_params=pltpu.CompilerParams(vmem_limit_bytes=4 * MIB),
        cost_estimate=pl.CostEstimate(flops=3 * 4 * 128 * 512, bytes_accessed=5 * 2**19, transcendentals=0),
    )(*parts)


def join_kernel(*refs):
    ins, outs = refs[:8], refs[8:]
    for h in range(2):
        total = (ins[4 * h][...].astype(F32) + ins[4 * h + 1][...].astype(F32)) + (
            ins[4 * h + 2][...].astype(F32) + ins[4 * h + 3][...].astype(F32)
        )
        for k in range(SIDE):
            outs[k][h * 32:(h + 1) * 32] = total[k * 32:(k + 1) * 32].astype(BF16)


def join_apart(first, second):
    return pl.pallas_call(
        join_kernel,
        out_shape=[jax.ShapeDtypeStruct((64, BLOCK), BF16)] * 4,
        compiler_params=pltpu.CompilerParams(vmem_limit_bytes=4 * MIB),
        cost_estimate=pl.CostEstimate(flops=2**19, bytes_accessed=5 * 2**18, transcendentals=0),
    )(*first, *second)


def exchange(pieces, axis):
    return [pieces[0]] + [shift(pieces[d], axis, d) for d in (1, 3, 2)]


def exchange_hops(pieces, axis):
    return [pieces[0], hop(pieces[1], axis, -1), hop(pieces[3], axis, 1), shift(pieces[2], axis, 2)]


def sum_in_two(first, second, fill):
    (p, p_axis), (q, q_axis) = first, second
    sent = [hop(p[2], p_axis, -1), hop(q[2], q_axis, -1), hop(p[3], p_axis, 1), hop(q[3], q_axis, 1)]
    sent, done0 = wait((sent, fill[0]()))
    ends = [hop(add_two(p[1], sent[0]), p_axis, -1), hop(add_two(q[1], sent[1]), q_axis, -1)]
    ends, done1 = wait((ends, fill[1]()))
    return (p[0], sent[2], ends[0]), (q[0], sent[3], ends[1]), done0, done1


def around(value, axis):
    return [value] + [shift(value, axis, -e % SIDE) for e in (1, 2, 3)]


def body(tokens, grad_out, counts, gate_weight, up_weight, down_weight):
    c = lax.axis_index("cuts")
    s = lax.axis_index("shard")
    core, z, x = c % 2, s // 4, s % 4
    step = jnp.arange(SIDE, dtype=jnp.int32)
    zs, xs = (z + step) % 4, (x + step) % 4
    way = step * (1 - 2 * core)
    hop_zs, hop_xs = (z + way) % 4, (x + way) % 4
    tokens_at = hop_zs[:, None] * 4 + xs[None, :]
    grads_at = zs[None, :] * 4 + hop_xs[:, None]
    tab = jnp.concatenate([tokens_at.reshape(16), grads_at.reshape(16), hop_zs, xs, zs, hop_xs]).astype(jnp.int32)
    weights = (gate_weight, up_weight, down_weight)

    row = jnp.pad(counts.astype(BF16)[None, :], ((0, 15), (0, BLOCK - 64)))
    blocks = around(jnp.concatenate([tokens, grad_out, row], 0), "y")
    blocks, far_gate, far_up = wait((blocks, shift(gate_weight, "core"), shift(up_weight, "core")))

    x0 = jnp.concatenate([b[:64] for b in blocks], 0)
    g0 = jnp.concatenate([b[64:128] for b in blocks], 0)
    x0, g0 = wait((around(x0, "x"), around(g0, "z")))
    x0, g0 = jnp.stack(x0), jnp.stack(g0)

    own_x, own_g, far_x, far_g = {0: x0}, {0: g0}, {}, {}

    def swap(e):
        far_x[-e % SIDE], far_g[-e % SIDE] = shift(own_x[e], "core"), shift(own_g[e], "core")

    def add(es, before):
        pieces = [p[e] for e in es for p in (own_x, far_x, own_g, far_g)]
        return forward(es, tab, weights, pieces, before)

    near = [hop(x0, "z", 1), hop(x0, "z", -1), hop(g0, "x", 1), hop(g0, "x", -1)]
    swap(0)
    sums = add((0,), ())
    counts = jnp.concatenate([b[128:129, :64] for b in blocks], 1).astype(F32)
    levels = jnp.stack([c, c + 1 - 2 * core]).astype(F32)
    keep = (counts > levels[:, None]).astype(F32)
    far_down = cut_down(tab, down_weight)
    near, sums, keep, far_down = wait((near, sums, keep, far_down))
    own_x[1], own_x[3], own_g[1], own_g[3] = near
    ends = [hop(own_x[1], "z", 1), hop(own_g[1], "x", 1)]
    swap(1)
    swap(3)
    own_sums, far_sums = add((1, 3), sums)
    far_sums, far_down = shift(far_sums, "core"), shift(far_down, "core")
    ends, own_sums, far_sums, far_down = wait((ends, own_sums, far_sums, far_down))
    own_x[2], own_g[2] = ends
    swap(2)
    far_weights = (far_gate, far_up, far_down)
    own_t, far_t, own_rows, far_rows = finish(tab, weights, far_weights, own_x[2], own_g[2], own_sums, far_sums, keep)
    far_t = shift(far_t, "core")
    terms = input_grads(tab, own_rows, far_rows, (gate_weight, up_weight, far_gate, far_up))
    first, second, grads, down = sum_in_two(
        (terms[:4], "x"),
        (terms[4:], "z"),
        (
            lambda: weight_grads(token_grad_kernel, 32, 2, tab, (own_t, far_t), own_x, far_x),
            lambda: weight_grads(down_grad_kernel, 40, 1, tab, (own_t, far_t), own_g, far_g),
        ),
    )
    first = exchange_hops(sum_apart(first), "z")
    second = exchange_hops(sum_apart(second), "x")
    parts = exchange(join_apart(first, second), "y")
    total = (parts[0].astype(F32) + parts[1].astype(F32)) + (parts[2].astype(F32) + parts[3].astype(F32))
    return (total.astype(BF16), *grads, *down)


def solution(mesh):
    return jax.shard_map(
        body,
        mesh=mesh,
        in_specs=(
            P("cuts", "shard"),
            P("cuts", "shard"),
            P("cuts"),
            P(("cuts", "shard"), None),
            P(("cuts", "shard"), None),
            P(("cuts", "shard"), None),
        ),
        out_specs=(
            P("cuts", "shard"),
            P(("cuts", "shard"), None),
            P(("cuts", "shard"), None),
            P(("cuts", "shard"), None),
        ),
        check_vma=False,
    )
```

time: 169 us -> 155 us (0.917)
  local copies, waits for them, and re-layouts: 18.8 us -> 11.7 us
  starting transfers between devices: 58 us -> 51 us
  Pallas kernels: 36.1 us -> 39.4 us
    ppermute x40 -> x27, waiting for transfers between devices: 48.6 us -> 27.2 us  [shift(): return lax.ppermute(value, name, pairs)]
    ppermute x40 -> x27, starting transfers between devices: 51.7 us -> 30.2 us  [shift(): return lax.ppermute(value, name, pairs)]
    ppermute x2 -> x16, waiting for transfers between devices: 0.95 us -> 21 us  [hop(): return lax.ppermute(value, ('cuts', 'shard'), pairs)]
    ppermute x2 -> x16, starting transfers between devices: 6.33 us -> 20.8 us  [hop(): return lax.ppermute(value, ('cuts', 'shard'), pairs)]
    unnamed x42 -> x24, local copies, waits for them, and re-layouts: 18.4 us -> 9.84 us
    pallas_call x3 -> x6, Pallas kernels: 15.1 us -> 17.7 us  [the longest x2 11.5 us: forward(): pl.pallas_call(functools.partial(forward_kernel, es, not before), in_spec...]
  transfers between devices with their start and end apart: 42 -> 43, of which waited for: 20 -> 21; matrix products, arithmetic and copies ran while one was open for 3% -> 3% of each run, Pallas kernels for 15% -> 25%
where the time goes in v3:
time: 155 us
  starting transfers between devices  51 us (33%)
  waiting for transfers between devices  48.2 us (31%)
  Pallas kernels  39.4 us (25%)
  local copies, waits for them, and re-layouts  11.7 us (8%)
  other arithmetic  3.91 us (3%)
    ppermute x27, starting transfers between devices, shift(): return lax.ppermute(value, name, pairs)  30.2 us
    ppermute x27, waiting for transfers between devices, shift(): return lax.ppermute(value, name, pairs)  27.2 us
    ppermute x16, waiting for transfers between devices, hop(): return lax.ppermute(value, ('cuts', 'shard'), pairs)  21 us
    ppermute x16, starting transfers between devices, hop(): return lax.ppermute(value, ('cuts', 'shard'), pairs)  20.8 us
    pallas_call x2, Pallas kernels, weight_grads(): pl.pallas_call(kernel, grid_spec=pltpu.PrefetchScalarGridSpec(num_scalar_...  14.2 us
    pallas_call x2, Pallas kernels, forward(): pl.pallas_call(functools.partial(forward_kernel, es, not before), in_spec...  11.5 us
    unnamed x24, local copies, waits for them, and re-layouts  9.84 us
    pallas_call x1, Pallas kernels, input_grads(): pl.pallas_call(input_grad_kernel, in_specs=[SMEM] + [VMEM] * 2 + [ANY] *...  7 us
  transfers between devices with their start and end apart: 43, of which 21 were waited for; matrix products, arithmetic and copies ran while one was open for 3% of the time, Pallas kernels for 25%

profile of v3, /device:TPU:0, one launch (start us, length us, event | category | flops | bytes accessed | tf_op | source)
XLA Modules:
  0.0 155.0 jit_solution(3053756661110716665)
XLA Ops:
  0.7 0.5 collective-permute-start.4
  1.2 0.7 convert_bitcast_fusion
  1.9 0.9 fusion.1
  2.8 1.7 %collective-permute-start.2 = (bf16[144,512]{1,0:T(8,128)(2,1)S(1)}, bf16[144,512]{1,0:T(8,128)(2,1)S(1)}, u32[]{:S(2)}, u32[]{:S(2)}) collective-permute-start(bf16[144,512]{1,0:T(8,128)(2,1)S(1)} %fusion.1), channel_id=1, source_target_pairs={{0,32},{16,48},{32,64},{48,80},{64,96},{80,112},{96,0},{112,16},{1... | collective-permute-start | bytes 442376 | tf_op jit(solution)/shard_map/ppermute | solution.py:48
  4.5 2.9 %collective-permute-start.1 = (bf16[144,512]{1,0:T(8,128)(2,1)S(1)}, bf16[144,512]{1,0:T(8,128)(2,1)S(1)}, u32[]{:S(2)}, u32[]{:S(2)}) collective-permute-start(bf16[144,512]{1,0:T(8,128)(2,1)S(1)} %fusion.1), channel_id=1, source_target_pairs={{0,64},{16,80},{32,96},{48,112},{64,0},{80,16},{96,32},{112,48},{1... | collective-permute-start | bytes 442376 | tf_op jit(solution)/shard_map/ppermute | solution.py:48
  7.4 1.3 collective-permute-start
  8.7 1.3 collective-permute-done.2
  10.0 4.3 %collective-permute-done.1 = bf16[144,512]{1,0:T(8,128)(2,1)S(1)} collective-permute-done((bf16[144,512]{1,0:T(8,128)(2,1)S(1)}, bf16[144,512]{1,0:T(8,128)(2,1)S(1)}, u32[]{:S(2)}, u32[]{:S(2)}) %collective-permute-start.1) | collective-permute-done | bytes 147488 | tf_op jit(solution)/shard_map/ppermute | solution.py:48
  14.4 1.9 %copy-done.6 = bf16[224,8192]{1,0:T(8,128)(2,1)} copy-done((bf16[224,8192]{1,0:T(8,128)(2,1)}, bf16[224,8192]{1,0:T(8,128)(2,1)S(1)}, u32[]{:S(2)}) %copy-start.6) | copy-done | bytes 3670040
  16.3 1.8 %copy-done.8 = bf16[224,8192]{1,0:T(8,128)(2,1)} copy-done((bf16[224,8192]{1,0:T(8,128)(2,1)}, bf16[224,8192]{1,0:T(8,128)(2,1)S(1)}, u32[]{:S(2)}) %copy-start.8) | copy-done | bytes 3670040
  18.2 1.6 %collective-permute-start.7 = (bf16[256,512]{1,0:T(8,128)(2,1)S(1)}, bf16[256,512]{1,0:T(8,128)(2,1)S(1)}, u32[]{:S(2)}, u32[]{:S(2)}) collective-permute-start(bf16[256,512]{1,0:T(8,128)(2,1)S(1)} %pad_maximum_fusion.2), channel_id=1, source_target_pairs={{0,1},{1,2},{2,3},{3,0},{4,5},{5,6},{6,7},{7,4},{8,9},{9,10},{10,1... | collective-permute-start | bytes 786440 | tf_op jit(solution)/shard_map/ppermute | solution.py:48
  19.7 2.7 %collective-permute-start.6 = (bf16[256,512]{1,0:T(8,128)(2,1)S(1)}, bf16[256,512]{1,0:T(8,128)(2,1)S(1)}, u32[]{:S(2)}, u32[]{:S(2)}) collective-permute-start(bf16[256,512]{1,0:T(8,128)(2,1)S(1)} %pad_maximum_fusion.2), channel_id=1, source_target_pairs={{0,2},{1,3},{2,0},{3,1},{4,6},{5,7},{6,4},{7,5},{8,10},{9,11},{10,... | collective-permute-start | bytes 786440 | tf_op jit(solution)/shard_map/ppermute | solution.py:48
  22.5 1.4 collective-permute-start.5
  23.9 2.0 %collective-permute-start.10 = (bf16[256,512]{1,0:T(8,128)(2,1)S(1)}, bf16[256,512]{1,0:T(8,128)(2,1)S(1)}, u32[]{:S(2)}, u32[]{:S(2)}) collective-permute-start(bf16[256,512]{1,0:T(8,128)(2,1)S(1)} %pad_maximum_fusion.3), channel_id=1, source_target_pairs={{0,4},{1,5},{2,6},{3,7},{4,8},{5,9},{6,10},{7,11},{8,12},{9,13},{1... | collective-permute-start | bytes 786440 | tf_op jit(solution)/shard_map/ppermute | solution.py:48
  25.9 3.6 %collective-permute-start.9 = (bf16[256,512]{1,0:T(8,128)(2,1)S(1)}, bf16[256,512]{1,0:T(8,128)(2,1)S(1)}, u32[]{:S(2)}, u32[]{:S(2)}) collective-permute-start(bf16[256,512]{1,0:T(8,128)(2,1)S(1)} %pad_maximum_fusion.3), channel_id=1, source_target_pairs={{0,8},{1,9},{2,10},{3,11},{4,12},{5,13},{6,14},{7,15},{8,0},{9,1},... | collective-permute-start | bytes 786440 | tf_op jit(solution)/shard_map/ppermute | solution.py:48
  29.5 2.3 %collective-permute-start.8 = (bf16[256,512]{1,0:T(8,128)(2,1)S(1)}, bf16[256,512]{1,0:T(8,128)(2,1)S(1)}, u32[]{:S(2)}, u32[]{:S(2)}) collective-permute-start(bf16[256,512]{1,0:T(8,128)(2,1)S(1)} %pad_maximum_fusion.3), channel_id=1, source_target_pairs={{0,12},{1,13},{2,14},{3,15},{4,0},{5,1},{6,2},{7,3},{8,4},{9,5},{1... | collective-permute-start | bytes 786440 | tf_op jit(solution)/shard_map/ppermute | solution.py:48
  31.8 1.8 %collective-permute-done.6 = bf16[256,512]{1,0:T(8,128)(2,1)S(1)} collective-permute-done((bf16[256,512]{1,0:T(8,128)(2,1)S(1)}, bf16[256,512]{1,0:T(8,128)(2,1)S(1)}, u32[]{:S(2)}, u32[]{:S(2)}) %collective-permute-start.6) | collective-permute-done | bytes 262176 | tf_op jit(solution)/shard_map/ppermute | solution.py:48
  33.5 0.8 collective-permute-done.10
  34.4 5.4 %collective-permute-done.9 = bf16[256,512]{1,0:T(8,128)(2,1)S(1)} collective-permute-done((bf16[256,512]{1,0:T(8,128)(2,1)S(1)}, bf16[256,512]{1,0:T(8,128)(2,1)S(1)}, u32[]{:S(2)}, u32[]{:S(2)}) %collective-permute-start.9) | collective-permute-done | bytes 262176 | tf_op jit(solution)/shard_map/ppermute | solution.py:48
  40.1 1.1 pad_maximum_fusion.refs_0_
  41.2 0.5 collective-permute-start.15
  41.7 0.6 collective-permute-start.14
  42.3 2.6 %collective-permute-start.13 = (bf16[4,256,512]{2,1,0:T(8,128)(2,1)S(1)}, bf16[4,256,512]{2,1,0:T(8,128)(2,1)}, u32[]{:S(2)}, u32[]{:S(2)}) collective-permute-start(bf16[4,256,512]{2,1,0:T(8,128)(2,1)S(1)} %pad_maximum_fusion.1.refs_2_.refs_0_), channel_id=1, source_target_pairs={{0,3},{1,0},{2,1},{3,2},{4,7},{5,4},{6,5},{7,6},{8,11},{9,8},{10,9... | collective-permute-start | bytes 3145736 | tf_op jit(solution)/shard_map/ppermute | solution.py:43
  45.0 1.5 collective-permute-start.12
  46.5 1.8 %collective-permute-start.11 = (bf16[4,256,512]{2,1,0:T(8,128)(2,1)}, bf16[4,256,512]{2,1,0:T(8,128)(2,1)}, u32[]{:S(2)}, u32[]{:S(2)}) collective-permute-start(bf16[4,256,512]{2,1,0:T(8,128)(2,1)} %pad_maximum_fusion.refs_0_), channel_id=1, source_target_pairs={{0,12},{1,13},{2,14},{3,15},{4,0},{5,1},{6,2},{7,3},{8,4},{9,5},{1... | collective-permute-start | bytes 3145736 | tf_op jit(solution)/shard_map/ppermute | solution.py:43
  48.5 2.0 %copy-done = bf16[224,8192]{1,0:T(8,128)(2,1)S(1)} copy-done((bf16[224,8192]{1,0:T(8,128)(2,1)S(1)}, bf16[224,8192]{1,0:T(8,128)(2,1)}, u32[]{:S(2)}) %copy-start) | copy-done | bytes 3670040
  50.5 0.8 shard_map.94
  51.4 0.9 slice_bitcast_fusion.2
  52.3 0.7 slice_bitcast_fusion
  53.2 2.0 %copy-done.2 = bf16[224,8192]{1,0:T(8,128)(2,1)S(1)} copy-done((bf16[224,8192]{1,0:T(8,128)(2,1)S(1)}, bf16[224,8192]{1,0:T(8,128)(2,1)}, u32[]{:S(2)}) %copy-start.2) | copy-done | bytes 3670040
  55.2 2.0 %copy-done.4 = bf16[224,8192]{1,0:T(8,128)(2,1)S(1)} copy-done((bf16[224,8192]{1,0:T(8,128)(2,1)S(1)}, bf16[224,8192]{1,0:T(8,128)(2,1)}, u32[]{:S(2)}) %copy-start.4) | copy-done | bytes 3670040
  57.2 4.4 %shard_map.93 = (f32[3,224,256]{2,1,0:T(8,128)S(1)}, f32[3,224,256]{2,1,0:T(8,128)S(1)}) custom-call(s32[48]{0:T(128)S(1)} %concatenate.32.tab, bf16[224,8192]{1,0:T(8,128)(2,1)S(1)} %copy-done.2, bf16[224,8192]{1,0:T(8,128)(2,1)S(1)} %copy-done.4, bf16[224,8192]{1,0:T(8,128)(2,1)S(1)} %copy-done.1, bf16[4,256,512]{2,1,0:T(8,128)(2,1)} %pad_maximum_fusion.refs_0_, ...), custom_call_target="tpu_custom_call" | custom-call | flops 1409286144 | bytes 8388608 | tf_op jit(solution)/shard_map/pallas_call | solution.py:105
  61.7 6.4 %collective-permute-done.14.refs_6_ = bf16[4,256,512]{2,1,0:T(8,128)(2,1)S(1)} collective-permute-done((bf16[4,256,512]{2,1,0:T(8,128)(2,1)S(1)}, bf16[4,256,512]{2,1,0:T(8,128)(2,1)S(1)}, u32[]{:S(2)}, u32[]{:S(2)}) %collective-permute-start.14) | collective-permute-done | bytes 1048608 | tf_op jit(solution)/shard_map/ppermute | solution.py:43
  68.1 3.7 %collective-permute-done.12.refs_4_.refs_6_ = bf16[4,256,512]{2,1,0:T(8,128)(2,1)} collective-permute-done((bf16[4,256,512]{2,1,0:T(8,128)(2,1)}, bf16[4,256,512]{2,1,0:T(8,128)(2,1)}, u32[]{:S(2)}, u32[]{:S(2)}) %collective-permute-start.12) | collective-permute-done | bytes 1048608 | tf_op jit(solution)/shard_map/ppermute | solution.py:43
  71.8 0.5 collective-permute-start.20
  73.0 2.2 %collective-permute-done.19.refs_1_.refs_3_ = bf16[4,256,512]{2,1,0:T(8,128)(2,1)S(1)} collective-permute-done((bf16[4,256,512]{2,1,0:T(8,128)(2,1)}, bf16[4,256,512]{2,1,0:T(8,128)(2,1)S(1)}, u32[]{:S(2)}, u32[]{:S(2)}) %collective-permute-start.19) | collective-permute-done | bytes 1048608 | tf_op jit(solution)/shard_map/ppermute | solution.py:48
  75.6 1.5 collective-permute-done.20.refs_3_
  77.7 1.5 collective-permute-done.22.refs_7_
  79.2 7.1 %shard_map.95 = (f32[3,224,256]{2,1,0:T(8,128)S(1)}, f32[3,224,256]{2,1,0:T(8,128)S(1)}) custom-call(s32[48]{0:T(128)S(1)} %concatenate.32.tab, bf16[224,8192]{1,0:T(8,128)(2,1)S(1)} %copy-done.3, bf16[224,8192]{1,0:T(8,128)(2,1)S(1)} %copy-done.5, bf16[224,8192]{1,0:T(8,128)(2,1)S(1)} %copy-done.1, ...), custom_call_target="tpu_custom_call" | custom-call | flops 2818572288 | bytes 16777216 | tf_op jit(solution)/shard_map/pallas_call | solution.py:105
  86.5 1.4 collective-permute-done.17.x.refs_4_
  87.9 2.4 %collective-permute-done.18.g.refs_4_ = bf16[4,256,512]{2,1,0:T(8,128)(2,1)S(1)} collective-permute-done((bf16[4,256,512]{2,1,0:T(8,128)(2,1)}, bf16[4,256,512]{2,1,0:T(8,128)(2,1)S(1)}, u32[]{:S(2)}, u32[]{:S(2)}) %collective-permute-start.18) | collective-permute-done | bytes 1048608 | tf_op jit(solution)/shard_map/ppermute | solution.py:43
  90.8 5.1 %shard_map.96 = (bf16[3,224,256]{2,1,0:T(8,128)(2,1)S(1)}, bf16[3,224,256]{2,1,0:T(8,128)(2,1)S(1)}, bf16[2,2,128,224]{3,2,1,0:T(8,128)(2,1)S(1)}, bf16[2,2,128,224]{3,2,1,0:T(8,128)(2,1)S(1)}) custom-call(s32[48]{0:T(128)S(1)} %concatenate.32.tab, bf16[224,8192]{1,0:T(8,128)(2,1)S(1)} %copy-done.3, bf16[224,8192]{1,0:T(8,128)(2,1)S(1)} %copy-done.5, ...), custom_call_target="tpu_custom_call" | custom-call | flops 1409286144 | bytes 8388608 | tf_op jit(solution)/shard_map/pallas_call | solution.py:160
  96.2 7.0 %shard_map.97 = (bf16[4,128,512]{2,1,0:T(8,128)(2,1)S(1)}, bf16[4,128,512]{2,1,0:T(8,128)(2,1)S(1)}, bf16[4,128,512]{2,1,0:T(8,128)(2,1)S(1)}, bf16[4,128,512]{2...) custom-call(s32[48]{0:T(128)S(1)} %concatenate.32.tab, ...), custom_call_target="tpu_custom_call" | custom-call | flops 3758096384 | bytes 18874368 | tf_op jit(solution)/shard_map/pallas_call | solution.py:257
  103.4 3.1 %collective-permute-start.27 = (bf16[4,128,512]{2,1,0:T(8,128)(2,1)S(1)}, bf16[4,128,512]{2,1,0:T(8,128)(2,1)S(1)}, u32[]{:S(2)}, u32[]{:S(2)}) collective-permute-start(bf16[4,128,512]{2,1,0:T(8,128)(2,1)S(1)} %get-tuple-element.106), channel_id=1, source_target_pairs={{0,3},{1,0},{2,1},{3,2},{4,7},{5,4},{6,5},{7,6},{8,11},{9,8},{10,9... | collective-permute-start | bytes 1572872 | tf_op jit(solution)/shard_map/ppermute | solution.py:43
  106.5 3.2 %collective-permute-start.28 = (bf16[4,128,512]{2,1,0:T(8,128)(2,1)S(1)}, bf16[4,128,512]{2,1,0:T(8,128)(2,1)S(1)}, u32[]{:S(2)}, u32[]{:S(2)}) collective-permute-start(bf16[4,128,512]{2,1,0:T(8,128)(2,1)S(1)} %get-tuple-element.107), channel_id=1, source_target_pairs={{0,12},{1,13},{2,14},{3,15},{4,0},{5,1},{6,2},{7,3},{8,4},{9,5},{1... | collective-permute-start | bytes 1572872 | tf_op jit(solution)/shard_map/ppermute | solution.py:43
  109.8 8.6 %shard_map.98 = (bf16[224,8192]{1,0:T(8,128)(2,1)}, bf16[224,8192]{1,0:T(8,128)(2,1)}) custom-call(s32[48]{0:T(128)S(1)} %concatenate.32.tab, bf16[3,224,256]{2,1,0:T(8,128)(2,1)S(1)} %get-tuple-element.108.own_t, bf16[3,224,256]{2,1,0:T(8,128)(2,1)S(1)} %collective-permute-done.29.far_t, bf16[4,256,512]{2,1,0:T(8,128)(2,1)} %pad_maximum_fusion.refs_0_, ...), custom_call_target="tpu_custom_call" | custom-call | flops 3758096384 | bytes 12582912 | tf_op jit(solution)/shard_map/pallas_call | solution.py:212
  118.8 0.5 collective-permute-start.31
  119.6 5.6 %shard_map.101 = bf16[224,8192]{1,0:T(8,128)(2,1)} custom-call(s32[48]{0:T(128)S(1)} %concatenate.32.tab, bf16[3,224,256]{2,1,0:T(8,128)(2,1)S(1)} %get-tuple-element.108.own_t, bf16[3,224,256]{2,1,0:T(8,128)(2,1)S(1)} %collective-permute-done.29.far_t, bf16[4,256,512]{2,1,0:T(8,128)(2,1)S(1)} %pad_maximum_fusion.1.refs_2_.refs_0_, ...), custom_call_target="tpu_custom_call" | custom-call | flops 1879048192 | bytes 6291456 | tf_op jit(solution)/shard_map/pallas_call | solution.py:212
  125.2 4.1 %collective-permute-done.31.c = bf16[4,128,512]{2,1,0:T(8,128)(2,1)S(1)} collective-permute-done((bf16[4,128,512]{2,1,0:T(8,128)(2,1)S(1)}, bf16[4,128,512]{2,1,0:T(8,128)(2,1)S(1)}, u32[]{:S(2)}, u32[]{:S(2)}) %collective-permute-start.31) | collective-permute-done | bytes 524320 | tf_op jit(solution)/shard_map/ppermute | solution.py:43
  129.3 0.7 collective-permute-done.32.c
  130.1 2.3 %collective-permute-start.37 = (bf16[128,512]{1,0:T(8,128)(2,1)S(1)}, bf16[128,512]{1,0:T(8,128)(2,1)S(1)}, u32[]{:S(2)}, u32[]{:S(2)}) collective-permute-start(bf16[128,512]{1,0:T(8,128)(2,1)S(1)} %get-tuple-element.126), channel_id=1, source_target_pairs={{0,1},{1,2},{2,3},{3,0},{4,5},{5,6},{6,7},{7,4},{8,9},{9,10},{10,1... | collective-permute-start | bytes 393224 | tf_op jit(solution)/shard_map/ppermute | solution.py:43
  132.4 1.1 collective-permute-start.38
  133.4 1.8 %collective-permute-start.39 = (bf16[128,512]{1,0:T(8,128)(2,1)S(1)}, bf16[128,512]{1,0:T(8,128)(2,1)S(1)}, u32[]{:S(2)}, u32[]{:S(2)}) collective-permute-start(bf16[128,512]{1,0:T(8,128)(2,1)S(1)} %get-tuple-element.128), channel_id=1, source_target_pairs={{0,2},{1,3},{2,0},{3,1},{4,6},{5,7},{6,4},{7,5},{8,10},{9,11},{10,... | collective-permute-start | bytes 393224 | tf_op jit(solution)/shard_map/ppermute | solution.py:48
  135.5 3.2 %collective-permute-start.35 = (bf16[128,512]{1,0:T(8,128)(2,1)S(1)}, bf16[128,512]{1,0:T(8,128)(2,1)S(1)}, u32[]{:S(2)}, u32[]{:S(2)}) collective-permute-start(bf16[128,512]{1,0:T(8,128)(2,1)S(1)} %get-tuple-element.120), channel_id=1, source_target_pairs={{0,12},{1,13},{2,14},{3,15},{4,0},{5,1},{6,2},{7,3},{8,4},{9,5},{1... | collective-permute-start | bytes 393224 | tf_op jit(solution)/shard_map/ppermute | solution.py:43
  138.7 1.0 collective-permute-start.36
  139.7 0.6 collective-permute-done.39.refs_7_
  140.3 2.1 %collective-permute-done.34.refs_1_ = bf16[128,512]{1,0:T(8,128)(2,1)S(1)} collective-permute-done((bf16[128,512]{1,0:T(8,128)(2,1)S(1)}, bf16[128,512]{1,0:T(8,128)(2,1)S(1)}, u32[]{:S(2)}, u32[]{:S(2)}) %collective-permute-start.34) | collective-permute-done | bytes 131104 | tf_op jit(solution)/shard_map/ppermute | solution.py:43
  142.4 2.8 %collective-permute-done.36.refs_3_ = bf16[128,512]{1,0:T(8,128)(2,1)S(1)} collective-permute-done((bf16[128,512]{1,0:T(8,128)(2,1)S(1)}, bf16[128,512]{1,0:T(8,128)(2,1)S(1)}, u32[]{:S(2)}, u32[]{:S(2)}) %collective-permute-start.36) | collective-permute-done | bytes 131104 | tf_op jit(solution)/shard_map/ppermute | solution.py:48
  145.3 1.3 collective-permute-start.40
  146.6 2.0 %collective-permute-start.41 = (bf16[64,512]{1,0:T(8,128)(2,1)S(1)}, bf16[64,512]{1,0:T(8,128)(2,1)S(1)}, u32[]{:S(2)}, u32[]{:S(2)}) collective-permute-start(bf16[64,512]{1,0:T(8,128)(2,1)S(1)} %get-tuple-element.131), channel_id=1, source_target_pairs={{0,96},{16,112},{32,0},{48,16},{64,32},{80,48},{96,64},{112,80},{1... | collective-permute-start | bytes 196616 | tf_op jit(solution)/shard_map/ppermute | solution.py:48
  148.6 1.1 collective-permute-start.42
  149.7 1.2 collective-permute-done.40
  150.9 3.5 %collective-permute-done.42 = bf16[64,512]{1,0:T(8,128)(2,1)S(1)} collective-permute-done((bf16[64,512]{1,0:T(8,128)(2,1)S(1)}, bf16[64,512]{1,0:T(8,128)(2,1)S(1)}, u32[]{:S(2)}, u32[]{:S(2)}) %collective-permute-start.42) | collective-permute-done | bytes 65568 | tf_op jit(solution)/shard_map/ppermute | solution.py:48
  154.4 0.7 add_convert_fusion
  (80 shorter events, 5.2 us)
Async XLA Ops:
  0.6 13.8 %collective-permute-start.3 = (bf16[224,8192]{1,0:T(8,128)(2,1)}, bf16[224,8192]{1,0:T(8,128)(2,1)S(1)}, u32[]{:S(2)}, u32[]{:S(2)}) collective-permute-start(bf16[224,8192]{1,0:T(8,128)(2,1)} %refs_0_.1), channel_id=1, source_target_pairs={{0,16},{16,0},{32,48},{48,32},{64,80},{80,64},{96,112},{112,96},{1... | collective-permute-start | bytes 11010056 | tf_op jit(solution)/shard_map/ppermute | solution.py:48
  0.7 15.5 %collective-permute-start.4 = (bf16[224,8192]{1,0:T(8,128)(2,1)}, bf16[224,8192]{1,0:T(8,128)(2,1)S(1)}, u32[]{:S(2)}, u32[]{:S(2)}) collective-permute-start(bf16[224,8192]{1,0:T(8,128)(2,1)} %refs_1_.1), channel_id=1, source_target_pairs={{0,16},{16,0},{32,48},{48,32},{64,80},{80,64},{96,112},{112,96},{1... | collective-permute-start | bytes 11010056 | tf_op jit(solution)/shard_map/ppermute | solution.py:48
  2.8 7.3 %collective-permute-start.2 = (bf16[144,512]{1,0:T(8,128)(2,1)S(1)}, bf16[144,512]{1,0:T(8,128)(2,1)S(1)}, u32[]{:S(2)}, u32[]{:S(2)}) collective-permute-start(bf16[144,512]{1,0:T(8,128)(2,1)S(1)} %fusion.1), channel_id=1, source_target_pairs={{0,32},{16,48},{32,64},{48,80},{64,96},{80,112},{96,0},{112,16},{1... | collective-permute-start | bytes 442376 | tf_op jit(solution)/shard_map/ppermute | solution.py:48
  4.5 9.9 %collective-permute-start.1 = (bf16[144,512]{1,0:T(8,128)(2,1)S(1)}, bf16[144,512]{1,0:T(8,128)(2,1)S(1)}, u32[]{:S(2)}, u32[]{:S(2)}) collective-permute-start(bf16[144,512]{1,0:T(8,128)(2,1)S(1)} %fusion.1), channel_id=1, source_target_pairs={{0,64},{16,80},{32,96},{48,112},{64,0},{80,16},{96,32},{112,48},{1... | collective-permute-start | bytes 442376 | tf_op jit(solution)/shard_map/ppermute | solution.py:48
  7.4 7.0 %collective-permute-start = (bf16[144,512]{1,0:T(8,128)(2,1)S(1)}, bf16[144,512]{1,0:T(8,128)(2,1)S(1)}, u32[]{:S(2)}, u32[]{:S(2)}) collective-permute-start(bf16[144,512]{1,0:T(8,128)(2,1)S(1)} %fusion.1), channel_id=1, source_target_pairs={{0,96},{16,112},{32,0},{48,16},{64,32},{80,48},{96,64},{112,80},{1... | collective-permute-start | bytes 442376 | tf_op jit(solution)/shard_map/ppermute | solution.py:48
  14.4 15.1 %copy-start.10 = (bf16[144,512]{1,0:T(8,128)(2,1)}, bf16[144,512]{1,0:T(8,128)(2,1)S(1)}, u32[]{:S(2)}) copy-start(bf16[144,512]{1,0:T(8,128)(2,1)S(1)} %collective-permute-done.1) | copy-start | bytes 442372
  14.4 3.8 %copy-start.11 = (bf16[144,512]{1,0:T(8,128)(2,1)}, bf16[144,512]{1,0:T(8,128)(2,1)S(1)}, u32[]{:S(2)}) copy-start(bf16[144,512]{1,0:T(8,128)(2,1)S(1)} %collective-permute-done) | copy-start | bytes 442372
  14.4 1.9 %copy-start.6 = (bf16[224,8192]{1,0:T(8,128)(2,1)}, bf16[224,8192]{1,0:T(8,128)(2,1)S(1)}, u32[]{:S(2)}) copy-start(bf16[224,8192]{1,0:T(8,128)(2,1)S(1)} %collective-permute-done.3.far_wg.refs_2_) | copy-start | bytes 11010052
  16.3 1.8 %copy-start.8 = (bf16[224,8192]{1,0:T(8,128)(2,1)}, bf16[224,8192]{1,0:T(8,128)(2,1)S(1)}, u32[]{:S(2)}) copy-start(bf16[224,8192]{1,0:T(8,128)(2,1)S(1)} %collective-permute-done.4.far_wu.refs_3_) | copy-start | bytes 11010052
  18.2 11.3 %collective-permute-start.7 = (bf16[256,512]{1,0:T(8,128)(2,1)S(1)}, bf16[256,512]{1,0:T(8,128)(2,1)S(1)}, u32[]{:S(2)}, u32[]{:S(2)}) collective-permute-start(bf16[256,512]{1,0:T(8,128)(2,1)S(1)} %pad_maximum_fusion.2), channel_id=1, source_target_pairs={{0,1},{1,2},{2,3},{3,0},{4,5},{5,6},{6,7},{7,4},{8,9},{9,10},{10,1... | collective-permute-start | bytes 786440 | tf_op jit(solution)/shard_map/ppermute | solution.py:48
  19.7 13.8 %collective-permute-start.6 = (bf16[256,512]{1,0:T(8,128)(2,1)S(1)}, bf16[256,512]{1,0:T(8,128)(2,1)S(1)}, u32[]{:S(2)}, u32[]{:S(2)}) collective-permute-start(bf16[256,512]{1,0:T(8,128)(2,1)S(1)} %pad_maximum_fusion.2), channel_id=1, source_target_pairs={{0,2},{1,3},{2,0},{3,1},{4,6},{5,7},{6,4},{7,5},{8,10},{9,11},{10,... | collective-permute-start | bytes 786440 | tf_op jit(solution)/shard_map/ppermute | solution.py:48
  22.5 11.1 %collective-permute-start.5 = (bf16[256,512]{1,0:T(8,128)(2,1)S(1)}, bf16[256,512]{1,0:T(8,128)(2,1)S(1)}, u32[]{:S(2)}, u32[]{:S(2)}) collective-permute-start(bf16[256,512]{1,0:T(8,128)(2,1)S(1)} %pad_maximum_fusion.2), channel_id=1, source_target_pairs={{0,3},{1,0},{2,1},{3,2},{4,7},{5,4},{6,5},{7,6},{8,11},{9,8},{10,9... | collective-permute-start | bytes 786440 | tf_op jit(solution)/shard_map/ppermute | solution.py:48
  23.9 10.4 %collective-permute-start.10 = (bf16[256,512]{1,0:T(8,128)(2,1)S(1)}, bf16[256,512]{1,0:T(8,128)(2,1)S(1)}, u32[]{:S(2)}, u32[]{:S(2)}) collective-permute-start(bf16[256,512]{1,0:T(8,128)(2,1)S(1)} %pad_maximum_fusion.3), channel_id=1, source_target_pairs={{0,4},{1,5},{2,6},{3,7},{4,8},{5,9},{6,10},{7,11},{8,12},{9,13},{1... | collective-permute-start | bytes 786440 | tf_op jit(solution)/shard_map/ppermute | solution.py:48
  25.9 13.8 %collective-permute-start.9 = (bf16[256,512]{1,0:T(8,128)(2,1)S(1)}, bf16[256,512]{1,0:T(8,128)(2,1)S(1)}, u32[]{:S(2)}, u32[]{:S(2)}) collective-permute-start(bf16[256,512]{1,0:T(8,128)(2,1)S(1)} %pad_maximum_fusion.3), channel_id=1, source_target_pairs={{0,8},{1,9},{2,10},{3,11},{4,12},{5,13},{6,14},{7,15},{8,0},{9,1},... | collective-permute-start | bytes 786440 | tf_op jit(solution)/shard_map/ppermute | solution.py:48
  29.5 10.2 %collective-permute-start.8 = (bf16[256,512]{1,0:T(8,128)(2,1)S(1)}, bf16[256,512]{1,0:T(8,128)(2,1)S(1)}, u32[]{:S(2)}, u32[]{:S(2)}) collective-permute-start(bf16[256,512]{1,0:T(8,128)(2,1)S(1)} %pad_maximum_fusion.3), channel_id=1, source_target_pairs={{0,12},{1,13},{2,14},{3,15},{4,0},{5,1},{6,2},{7,3},{8,4},{9,5},{1... | collective-permute-start | bytes 786440 | tf_op jit(solution)/shard_map/ppermute | solution.py:48
  39.9 6.6 %collective-permute-start.16 = (bf16[4,256,512]{2,1,0:T(8,128)(2,1)S(1)}, bf16[4,256,512]{2,1,0:T(8,128)(2,1)S(1)}, u32[]{:S(2)}, u32[]{:S(2)}) collective-permute-start(bf16[4,256,512]{2,1,0:T(8,128)(2,1)S(1)} %pad_maximum_fusion.1.refs_2_.refs_0_), channel_id=1, source_target_pairs={{0,16},{16,0},{32,48},{48,32},{64,80},{80,64},{96,112},{112,96},{1... | collective-permute-start | bytes 3145736 | tf_op jit(solution)/shard_map/ppermute | solution.py:48
  41.2 11.9 %collective-permute-start.15 = (bf16[4,256,512]{2,1,0:T(8,128)(2,1)}, bf16[4,256,512]{2,1,0:T(8,128)(2,1)}, u32[]{:S(2)}, u32[]{:S(2)}) collective-permute-start(bf16[4,256,512]{2,1,0:T(8,128)(2,1)} %pad_maximum_fusion.refs_0_), channel_id=1, source_target_pairs={{0,16},{16,0},{32,48},{48,32},{64,80},{80,64},{96,112},{112,96},{1... | collective-permute-start | bytes 3145736 | tf_op jit(solution)/shard_map/ppermute | solution.py:48
  41.7 26.3 %collective-permute-start.14 = (bf16[4,256,512]{2,1,0:T(8,128)(2,1)S(1)}, bf16[4,256,512]{2,1,0:T(8,128)(2,1)S(1)}, u32[]{:S(2)}, u32[]{:S(2)}) collective-permute-start(bf16[4,256,512]{2,1,0:T(8,128)(2,1)S(1)} %pad_maximum_fusion.1.refs_2_.refs_0_), channel_id=1, source_target_pairs={{0,1},{1,2},{2,3},{3,0},{4,5},{5,6},{6,7},{7,4},{8,9},{9,10},{10,1... | collective-permute-start | bytes 3145736 | tf_op jit(solution)/shard_map/ppermute | solution.py:43
  42.3 25.7 %collective-permute-start.13 = (bf16[4,256,512]{2,1,0:T(8,128)(2,1)S(1)}, bf16[4,256,512]{2,1,0:T(8,128)(2,1)}, u32[]{:S(2)}, u32[]{:S(2)}) collective-permute-start(bf16[4,256,512]{2,1,0:T(8,128)(2,1)S(1)} %pad_maximum_fusion.1.refs_2_.refs_0_), channel_id=1, source_target_pairs={{0,3},{1,0},{2,1},{3,2},{4,7},{5,4},{6,5},{7,6},{8,11},{9,8},{10,9... | collective-permute-start | bytes 3145736 | tf_op jit(solution)/shard_map/ppermute | solution.py:43
  45.0 26.8 %collective-permute-start.12 = (bf16[4,256,512]{2,1,0:T(8,128)(2,1)}, bf16[4,256,512]{2,1,0:T(8,128)(2,1)}, u32[]{:S(2)}, u32[]{:S(2)}) collective-permute-start(bf16[4,256,512]{2,1,0:T(8,128)(2,1)} %pad_maximum_fusion.refs_0_), channel_id=1, source_target_pairs={{0,4},{1,5},{2,6},{3,7},{4,8},{5,9},{6,10},{7,11},{8,12},{9,13},{1... | collective-permute-start | bytes 3145736 | tf_op jit(solution)/shard_map/ppermute | solution.py:43
  46.5 25.3 %collective-permute-start.11 = (bf16[4,256,512]{2,1,0:T(8,128)(2,1)}, bf16[4,256,512]{2,1,0:T(8,128)(2,1)}, u32[]{:S(2)}, u32[]{:S(2)}) collective-permute-start(bf16[4,256,512]{2,1,0:T(8,128)(2,1)} %pad_maximum_fusion.refs_0_), channel_id=1, source_target_pairs={{0,12},{1,13},{2,14},{3,15},{4,0},{5,1},{6,2},{7,3},{8,4},{9,5},{1... | collective-permute-start | bytes 3145736 | tf_op jit(solution)/shard_map/ppermute | solution.py:43
  48.5 2.0 %copy-start = (bf16[224,8192]{1,0:T(8,128)(2,1)S(1)}, bf16[224,8192]{1,0:T(8,128)(2,1)}, u32[]{:S(2)}) copy-start(bf16[224,8192]{1,0:T(8,128)(2,1)} %wd.5) | copy-start | bytes 11010052
  50.5 2.6 %copy-start.1 = (bf16[224,8192]{1,0:T(8,128)(2,1)S(1)}, bf16[224,8192]{1,0:T(8,128)(2,1)}, u32[]{:S(2)}) copy-start(bf16[224,8192]{1,0:T(8,128)(2,1)} %wd.5) | copy-start | bytes 11010052
  53.1 2.0 %copy-start.2 = (bf16[224,8192]{1,0:T(8,128)(2,1)S(1)}, bf16[224,8192]{1,0:T(8,128)(2,1)}, u32[]{:S(2)}) copy-start(bf16[224,8192]{1,0:T(8,128)(2,1)} %refs_0_.1) | copy-start | bytes 11010052
  55.2 2.0 %copy-start.4 = (bf16[224,8192]{1,0:T(8,128)(2,1)S(1)}, bf16[224,8192]{1,0:T(8,128)(2,1)}, u32[]{:S(2)}) copy-start(bf16[224,8192]{1,0:T(8,128)(2,1)} %refs_1_.1) | copy-start | bytes 11010052
  57.2 22.0 %copy-start.3 = (bf16[224,8192]{1,0:T(8,128)(2,1)S(1)}, bf16[224,8192]{1,0:T(8,128)(2,1)}, u32[]{:S(2)}) copy-start(bf16[224,8192]{1,0:T(8,128)(2,1)} %refs_0_.1) | copy-start | bytes 11010052
  57.2 22.0 %copy-start.5 = (bf16[224,8192]{1,0:T(8,128)(2,1)S(1)}, bf16[224,8192]{1,0:T(8,128)(2,1)}, u32[]{:S(2)}) copy-start(bf16[224,8192]{1,0:T(8,128)(2,1)} %refs_1_.1) | copy-start | bytes 11010052
  71.7 19.1 %copy-start.7 = (bf16[224,8192]{1,0:T(8,128)(2,1)S(1)}, bf16[224,8192]{1,0:T(8,128)(2,1)}, u32[]{:S(2)}) copy-start(bf16[224,8192]{1,0:T(8,128)(2,1)} %copy-done.6) | copy-start | bytes 11010052
  71.7 19.1 %copy-start.9 = (bf16[224,8192]{1,0:T(8,128)(2,1)S(1)}, bf16[224,8192]{1,0:T(8,128)(2,1)}, u32[]{:S(2)}) copy-start(bf16[224,8192]{1,0:T(8,128)(2,1)} %copy-done.8) | copy-start | bytes 11010052
  71.7 3.5 %collective-permute-start.19 = (bf16[4,256,512]{2,1,0:T(8,128)(2,1)}, bf16[4,256,512]{2,1,0:T(8,128)(2,1)S(1)}, u32[]{:S(2)}, u32[]{:S(2)}) collective-permute-start(bf16[4,256,512]{2,1,0:T(8,128)(2,1)} %collective-permute-done.12.refs_4_.refs_6_), channel_id=1, source_target_pairs={{0,16},{16,0},{32,48},{48,32},{64,80},{80,64},{96,112},{112,96},{1... | collective-permute-start | bytes 3145736 | tf_op jit(solution)/shard_map/ppermute | solution.py:48
  71.8 5.3 %collective-permute-start.20 = (bf16[4,256,512]{2,1,0:T(8,128)(2,1)S(1)}, bf16[4,256,512]{2,1,0:T(8,128)(2,1)S(1)}, u32[]{:S(2)}, u32[]{:S(2)}) collective-permute-start(bf16[4,256,512]{2,1,0:T(8,128)(2,1)S(1)} %collective-permute-done.14.refs_6_), channel_id=1, source_target_pairs={{0,16},{16,0},{32,48},{48,32},{64,80},{80,64},{96,112},{112,96},{1... | collective-permute-start | bytes 3145736 | tf_op jit(solution)/shard_map/ppermute | solution.py:48
  72.3 5.4 %collective-permute-start.21 = (bf16[4,256,512]{2,1,0:T(8,128)(2,1)}, bf16[4,256,512]{2,1,0:T(8,128)(2,1)S(1)}, u32[]{:S(2)}, u32[]{:S(2)}) collective-permute-start(bf16[4,256,512]{2,1,0:T(8,128)(2,1)} %collective-permute-done.11.refs_0_.refs_2_), channel_id=1, source_target_pairs={{0,16},{16,0},{32,48},{48,32},{64,80},{80,64},{96,112},{112,96},{1... | collective-permute-start | bytes 3145736 | tf_op jit(solution)/shard_map/ppermute | solution.py:48
  72.4 6.8 %collective-permute-start.22 = (bf16[4,256,512]{2,1,0:T(8,128)(2,1)}, bf16[4,256,512]{2,1,0:T(8,128)(2,1)S(1)}, u32[]{:S(2)}, u32[]{:S(2)}) collective-permute-start(bf16[4,256,512]{2,1,0:T(8,128)(2,1)} %collective-permute-done.13.refs_2_), channel_id=1, source_target_pairs={{0,16},{16,0},{32,48},{48,32},{64,80},{80,64},{96,112},{112,96},{1... | collective-permute-start | bytes 3145736 | tf_op jit(solution)/shard_map/ppermute | solution.py:48
  72.8 15.0 %collective-permute-start.17 = (bf16[4,256,512]{2,1,0:T(8,128)(2,1)}, bf16[4,256,512]{2,1,0:T(8,128)(2,1)S(1)}, u32[]{:S(2)}, u32[]{:S(2)}) collective-permute-start(bf16[4,256,512]{2,1,0:T(8,128)(2,1)} %collective-permute-done.11.refs_0_.refs_2_), channel_id=1, source_target_pairs={{0,12},{1,13},{2,14},{3,15},{4,0},{5,1},{6,2},{7,3},{8,4},{9,5},{1... | collective-permute-start | bytes 3145736 | tf_op jit(solution)/shard_map/ppermute | solution.py:43
  75.3 15.0 %collective-permute-start.18 = (bf16[4,256,512]{2,1,0:T(8,128)(2,1)}, bf16[4,256,512]{2,1,0:T(8,128)(2,1)S(1)}, u32[]{:S(2)}, u32[]{:S(2)}) collective-permute-start(bf16[4,256,512]{2,1,0:T(8,128)(2,1)} %collective-permute-done.13.refs_2_), channel_id=1, source_target_pairs={{0,3},{1,0},{2,1},{3,2},{4,7},{5,4},{6,5},{7,6},{8,11},{9,8},{10,9... | collective-permute-start | bytes 3145736 | tf_op jit(solution)/shard_map/ppermute | solution.py:43
  77.1 9.4 %collective-permute-start.24 = (bf16[4,224,512]{2,1,0:T(8,128)(2,1)S(1)}, bf16[4,224,512]{2,1,0:T(8,128)(2,1)S(1)}, u32[]{:S(2)}, u32[]{:S(2)}) collective-permute-start(bf16[4,224,512]{2,1,0:T(8,128)(2,1)S(1)} %shard_map.94), channel_id=1, source_target_pairs={{0,16},{16,0},{32,48},{48,32},{64,80},{80,64},{96,112},{112,96},{1... | collective-permute-start | bytes 2752520 | tf_op jit(solution)/shard_map/ppermute | solution.py:48
  86.3 4.0 %collective-permute-start.23 = (f32[3,224,256]{2,1,0:T(8,128)S(1)}, f32[3,224,256]{2,1,0:T(8,128)S(1)}, u32[]{:S(2)}, u32[]{:S(2)}) collective-permute-start(f32[3,224,256]{2,1,0:T(8,128)S(1)} %get-tuple-element.93), channel_id=1, source_target_pairs={{0,16},{16,0},{32,48},{48,32},{64,80},{80,64},{96,112},{112,96},{1... | collective-permute-start | bytes 2064392 | tf_op jit(solution)/shard_map/ppermute | solution.py:48
  90.3 16.2 %collective-permute-start.30 = (bf16[4,256,512]{2,1,0:T(8,128)(2,1)S(1)}, bf16[4,256,512]{2,1,0:T(8,128)(2,1)S(1)}, u32[]{:S(2)}, u32[]{:S(2)}) collective-permute-start(bf16[4,256,512]{2,1,0:T(8,128)(2,1)S(1)} %collective-permute-done.17.x.refs_4_), channel_id=1, source_target_pairs={{0,16},{16,0},{32,48},{48,32},{64,80},{80,64},{96,112},{112,96},{1... | collective-permute-start | bytes 3145736 | tf_op jit(solution)/shard_map/ppermute | solution.py:48
  90.5 29.1 %collective-permute-start.33 = (bf16[4,256,512]{2,1,0:T(8,128)(2,1)S(1)}, bf16[4,256,512]{2,1,0:T(8,128)(2,1)S(1)}, u32[]{:S(2)}, u32[]{:S(2)}) collective-permute-start(bf16[4,256,512]{2,1,0:T(8,128)(2,1)S(1)} %collective-permute-done.18.g.refs_4_), channel_id=1, source_target_pairs={{0,16},{16,0},{32,48},{48,32},{64,80},{80,64},{96,112},{112,96},{1... | collective-permute-start | bytes 3145736 | tf_op jit(solution)/shard_map/ppermute | solution.py:48
  95.9 7.5 %collective-permute-start.29 = (bf16[3,224,256]{2,1,0:T(8,128)(2,1)S(1)}, bf16[3,224,256]{2,1,0:T(8,128)(2,1)S(1)}, u32[]{:S(2)}, u32[]{:S(2)}) collective-permute-start(bf16[3,224,256]{2,1,0:T(8,128)(2,1)S(1)} %get-tuple-element.109), channel_id=1, source_target_pairs={{0,16},{16,0},{32,48},{48,32},{64,80},{80,64},{96,112},{112,96},{1... | collective-permute-start | bytes 1032200 | tf_op jit(solution)/shard_map/ppermute | solution.py:48
  103.2 15.2 %collective-permute-start.25 = (bf16[4,128,512]{2,1,0:T(8,128)(2,1)S(1)}, bf16[4,128,512]{2,1,0:T(8,128)(2,1)S(1)}, u32[]{:S(2)}, u32[]{:S(2)}) collective-permute-start(bf16[4,128,512]{2,1,0:T(8,128)(2,1)S(1)} %get-tuple-element.104), channel_id=1, source_target_pairs={{0,1},{1,2},{2,3},{3,0},{4,5},{5,6},{6,7},{7,4},{8,9},{9,10},{10,1... | collective-permute-start | bytes 1572872 | tf_op jit(solution)/shard_map/ppermute | solution.py:43
  103.3 15.1 %collective-permute-start.26 = (bf16[4,128,512]{2,1,0:T(8,128)(2,1)S(1)}, bf16[4,128,512]{2,1,0:T(8,128)(2,1)S(1)}, u32[]{:S(2)}, u32[]{:S(2)}) collective-permute-start(bf16[4,128,512]{2,1,0:T(8,128)(2,1)S(1)} %get-tuple-element.105), channel_id=1, source_target_pairs={{0,4},{1,5},{2,6},{3,7},{4,8},{5,9},{6,10},{7,11},{8,12},{9,13},{1... | collective-permute-start | bytes 1572872 | tf_op jit(solution)/shard_map/ppermute | solution.py:43
  103.4 15.0 %collective-permute-start.27 = (bf16[4,128,512]{2,1,0:T(8,128)(2,1)S(1)}, bf16[4,128,512]{2,1,0:T(8,128)(2,1)S(1)}, u32[]{:S(2)}, u32[]{:S(2)}) collective-permute-start(bf16[4,128,512]{2,1,0:T(8,128)(2,1)S(1)} %get-tuple-element.106), channel_id=1, source_target_pairs={{0,3},{1,0},{2,1},{3,2},{4,7},{5,4},{6,5},{7,6},{8,11},{9,8},{10,9... | collective-permute-start | bytes 1572872 | tf_op jit(solution)/shard_map/ppermute | solution.py:43
  106.5 12.2 %collective-permute-start.28 = (bf16[4,128,512]{2,1,0:T(8,128)(2,1)S(1)}, bf16[4,128,512]{2,1,0:T(8,128)(2,1)S(1)}, u32[]{:S(2)}, u32[]{:S(2)}) collective-permute-start(bf16[4,128,512]{2,1,0:T(8,128)(2,1)S(1)} %get-tuple-element.107), channel_id=1, source_target_pairs={{0,12},{1,13},{2,14},{3,15},{4,0},{5,1},{6,2},{7,3},{8,4},{9,5},{1... | collective-permute-start | bytes 1572872 | tf_op jit(solution)/shard_map/ppermute | solution.py:43
  118.8 10.5 %collective-permute-start.31 = (bf16[4,128,512]{2,1,0:T(8,128)(2,1)S(1)}, bf16[4,128,512]{2,1,0:T(8,128)(2,1)S(1)}, u32[]{:S(2)}, u32[]{:S(2)}) collective-permute-start(bf16[4,128,512]{2,1,0:T(8,128)(2,1)S(1)} %shard_map.99), channel_id=1, source_target_pairs={{0,1},{1,2},{2,3},{3,0},{4,5},{5,6},{6,7},{7,4},{8,9},{9,10},{10,1... | collective-permute-start | bytes 1572872 | tf_op jit(solution)/shard_map/ppermute | solution.py:43
  119.5 10.5 %collective-permute-start.32 = (bf16[4,128,512]{2,1,0:T(8,128)(2,1)S(1)}, bf16[4,128,512]{2,1,0:T(8,128)(2,1)S(1)}, u32[]{:S(2)}, u32[]{:S(2)}) collective-permute-start(bf16[4,128,512]{2,1,0:T(8,128)(2,1)S(1)} %shard_map.100), channel_id=1, source_target_pairs={{0,4},{1,5},{2,6},{3,7},{4,8},{5,9},{6,10},{7,11},{8,12},{9,13},{1... | collective-permute-start | bytes 1572872 | tf_op jit(solution)/shard_map/ppermute | solution.py:43
  130.1 8.6 %collective-permute-start.37 = (bf16[128,512]{1,0:T(8,128)(2,1)S(1)}, bf16[128,512]{1,0:T(8,128)(2,1)S(1)}, u32[]{:S(2)}, u32[]{:S(2)}) collective-permute-start(bf16[128,512]{1,0:T(8,128)(2,1)S(1)} %get-tuple-element.126), channel_id=1, source_target_pairs={{0,1},{1,2},{2,3},{3,0},{4,5},{5,6},{6,7},{7,4},{8,9},{9,10},{10,1... | collective-permute-start | bytes 393224 | tf_op jit(solution)/shard_map/ppermute | solution.py:43
  132.4 7.3 %collective-permute-start.38 = (bf16[128,512]{1,0:T(8,128)(2,1)S(1)}, bf16[128,512]{1,0:T(8,128)(2,1)S(1)}, u32[]{:S(2)}, u32[]{:S(2)}) collective-permute-start(bf16[128,512]{1,0:T(8,128)(2,1)S(1)} %get-tuple-element.127), channel_id=1, source_target_pairs={{0,3},{1,0},{2,1},{3,2},{4,7},{5,4},{6,5},{7,6},{8,11},{9,8},{10,9... | collective-permute-start | bytes 393224 | tf_op jit(solution)/shard_map/ppermute | solution.py:43
  133.4 6.8 %collective-permute-start.39 = (bf16[128,512]{1,0:T(8,128)(2,1)S(1)}, bf16[128,512]{1,0:T(8,128)(2,1)S(1)}, u32[]{:S(2)}, u32[]{:S(2)}) collective-permute-start(bf16[128,512]{1,0:T(8,128)(2,1)S(1)} %get-tuple-element.128), channel_id=1, source_target_pairs={{0,2},{1,3},{2,0},{3,1},{4,6},{5,7},{6,4},{7,5},{8,10},{9,11},{10,... | collective-permute-start | bytes 393224 | tf_op jit(solution)/shard_map/ppermute | solution.py:48
  135.4 7.0 %collective-permute-start.34 = (bf16[128,512]{1,0:T(8,128)(2,1)S(1)}, bf16[128,512]{1,0:T(8,128)(2,1)S(1)}, u32[]{:S(2)}, u32[]{:S(2)}) collective-permute-start(bf16[128,512]{1,0:T(8,128)(2,1)S(1)} %get-tuple-element.119), channel_id=1, source_target_pairs={{0,4},{1,5},{2,6},{3,7},{4,8},{5,9},{6,10},{7,11},{8,12},{9,13},{1... | collective-permute-start | bytes 393224 | tf_op jit(solution)/shard_map/ppermute | solution.py:43
  135.5 6.9 %collective-permute-start.35 = (bf16[128,512]{1,0:T(8,128)(2,1)S(1)}, bf16[128,512]{1,0:T(8,128)(2,1)S(1)}, u32[]{:S(2)}, u32[]{:S(2)}) collective-permute-start(bf16[128,512]{1,0:T(8,128)(2,1)S(1)} %get-tuple-element.120), channel_id=1, source_target_pairs={{0,12},{1,13},{2,14},{3,15},{4,0},{5,1},{6,2},{7,3},{8,4},{9,5},{1... | collective-permute-start | bytes 393224 | tf_op jit(solution)/shard_map/ppermute | solution.py:43
  138.7 6.5 %collective-permute-start.36 = (bf16[128,512]{1,0:T(8,128)(2,1)S(1)}, bf16[128,512]{1,0:T(8,128)(2,1)S(1)}, u32[]{:S(2)}, u32[]{:S(2)}) collective-permute-start(bf16[128,512]{1,0:T(8,128)(2,1)S(1)} %get-tuple-element.121), channel_id=1, source_target_pairs={{0,8},{1,9},{2,10},{3,11},{4,12},{5,13},{6,14},{7,15},{8,0},{9,1},... | collective-permute-start | bytes 393224 | tf_op jit(solution)/shard_map/ppermute | solution.py:48
  145.3 5.5 %collective-permute-start.40 = (bf16[64,512]{1,0:T(8,128)(2,1)S(1)}, bf16[64,512]{1,0:T(8,128)(2,1)S(1)}, u32[]{:S(2)}, u32[]{:S(2)}) collective-permute-start(bf16[64,512]{1,0:T(8,128)(2,1)S(1)} %get-tuple-element.130), channel_id=1, source_target_pairs={{0,32},{16,48},{32,64},{48,80},{64,96},{80,112},{96,0},{112,16},{1... | collective-permute-start | bytes 196616 | tf_op jit(solution)/shard_map/ppermute | solution.py:48
  146.6 4.3 %collective-permute-start.41 = (bf16[64,512]{1,0:T(8,128)(2,1)S(1)}, bf16[64,512]{1,0:T(8,128)(2,1)S(1)}, u32[]{:S(2)}, u32[]{:S(2)}) collective-permute-start(bf16[64,512]{1,0:T(8,128)(2,1)S(1)} %get-tuple-element.131), channel_id=1, source_target_pairs={{0,96},{16,112},{32,0},{48,16},{64,32},{80,48},{96,64},{112,80},{1... | collective-permute-start | bytes 196616 | tf_op jit(solution)/shard_map/ppermute | solution.py:48
  148.6 5.8 %collective-permute-start.42 = (bf16[64,512]{1,0:T(8,128)(2,1)S(1)}, bf16[64,512]{1,0:T(8,128)(2,1)S(1)}, u32[]{:S(2)}, u32[]{:S(2)}) collective-permute-start(bf16[64,512]{1,0:T(8,128)(2,1)S(1)} %get-tuple-element.132), channel_id=1, source_target_pairs={{0,64},{16,80},{32,96},{48,112},{64,0},{80,16},{96,32},{112,48},{1... | collective-permute-start | bytes 196616 | tf_op jit(solution)/shard_map/ppermute | solution.py:48

commit v4 on v3

--- a/solution.py
+++ b/solution.py
@@ -312,11 +312,13 @@
 
 
 def exchange(pieces, axis):
-    return [pieces[0]] + [shift(pieces[d], axis, d) for d in (1, 3, 2)]
+    far = shift(pieces[2], axis, 2)
+    return [pieces[0], far, shift(pieces[1], axis, 1), shift(pieces[3], axis, 3)]
 
 
 def exchange_hops(pieces, axis):
-    return [pieces[0], hop(pieces[1], axis, -1), hop(pieces[3], axis, 1), shift(pieces[2], axis, 2)]
+    far = shift(pieces[2], axis, 2)
+    return [pieces[0], far, hop(pieces[1], axis, -1), hop(pieces[3], axis, 1)]
 
 
 def sum_in_two(first, second, fill):
@@ -329,7 +331,8 @@
 
 
 def around(value, axis):
-    return [value] + [shift(value, axis, -e % SIDE) for e in (1, 2, 3)]
+    near = shift(value, axis, 3), shift(value, axis, 1)
+    return [value, near[0], shift(value, axis, 2), near[1]]
 
 
 def body(tokens, grad_out, counts, gate_weight, up_weight, down_weight):
@@ -347,11 +350,12 @@
 
     row = jnp.pad(counts.astype(BF16)[None, :], ((0, 15), (0, BLOCK - 64)))
     blocks = around(jnp.concatenate([tokens, grad_out, row], 0), "y")
-    blocks, far_gate, far_up = wait((blocks, shift(gate_weight, "core"), shift(up_weight, "core")))
+    blocks, far_gate = wait((blocks, shift(gate_weight, "core")))
 
     x0 = jnp.concatenate([b[:64] for b in blocks], 0)
     g0 = jnp.concatenate([b[64:128] for b in blocks], 0)
-    x0, g0 = wait((around(x0, "x"), around(g0, "z")))
+    g0, far_up = wait((g0, shift(up_weight, "core")))
+    g0, x0 = wait((around(g0, "z"), around(x0, "x")))
     x0, g0 = jnp.stack(x0), jnp.stack(g0)
 
     own_x, own_g, far_x, far_g = {0: x0}, {0: g0}, {}, {}
@@ -372,9 +376,9 @@
     far_down = cut_down(tab, down_weight)
     near, sums, keep, far_down = wait((near, sums, keep, far_down))
     own_x[1], own_x[3], own_g[1], own_g[3] = near
-    ends = [hop(own_x[1], "z", 1), hop(own_g[1], "x", 1)]
     swap(1)
     swap(3)
+    ends = [hop(own_x[1], "z", 1), hop(own_g[1], "x", 1)]
     own_sums, far_sums = add((1, 3), sums)
     far_sums, far_down = shift(far_sums, "core"), shift(far_down, "core")
     ends, own_sums, far_sums, far_down = wait((ends, own_sums, far_sums, far_down))

time: 155 us -> 154 us (level)
  no operation moved by 1% of the time
where the time goes in v4:
time: 154 us
  starting transfers between devices  50.8 us (33%)
  waiting for transfers between devices  47.2 us (31%)
  Pallas kernels  39.4 us (26%)
  local copies, waits for them, and re-layouts  11.7 us (8%)
  other arithmetic  3.91 us (3%)
    ppermute x27, starting transfers between devices, shift(): return lax.ppermute(value, name, pairs)  30.8 us
    ppermute x27, waiting for transfers between devices, shift(): return lax.ppermute(value, name, pairs)  26.5 us
    ppermute x16, waiting for transfers between devices, hop(): return lax.ppermute(value, ('cuts', 'shard'), pairs)  20.7 us
    ppermute x16, starting transfers between devices, hop(): return lax.ppermute(value, ('cuts', 'shard'), pairs)  20 us
    pallas_call x2, Pallas kernels, weight_grads(): pl.pallas_call(kernel, grid_spec=pltpu.PrefetchScalarGridSpec(num_scalar_...  14.2 us
    pallas_call x2, Pallas kernels, forward(): pl.pallas_call(functools.partial(forward_kernel, es, not before), in_spec...  11.5 us
    unnamed x24, local copies, waits for them, and re-layouts  9.83 us
    pallas_call x1, Pallas kernels, input_grads(): pl.pallas_call(input_grad_kernel, in_specs=[SMEM] + [VMEM] * 2 + [ANY] *...  7 us
  transfers between devices with their start and end apart: 43, of which 21 were waited for; matrix products, arithmetic and copies ran while one was open for 3% of the time, Pallas kernels for 25%

profile of v4, /device:TPU:0, one launch (start us, length us, event | category | flops | bytes accessed | tf_op | source)
XLA Modules:
  0.0 154.0 jit_solution(12093610634036060328)
XLA Ops:
  0.7 0.5 collective-permute-start.4
  1.2 0.7 convert_bitcast_fusion
  1.9 0.9 fusion.1
  2.8 1.7 %collective-permute-start.2 = (bf16[144,512]{1,0:T(8,128)(2,1)S(1)}, bf16[144,512]{1,0:T(8,128)(2,1)S(1)}, u32[]{:S(2)}, u32[]{:S(2)}) collective-permute-start(bf16[144,512]{1,0:T(8,128)(2,1)S(1)} %fusion.1), channel_id=1, source_target_pairs={{0,32},{16,48},{32,64},{48,80},{64,96},{80,112},{96,0},{112,16},{1... | collective-permute-start | bytes 442376 | tf_op jit(solution)/shard_map/ppermute | solution.py:48
  4.5 2.9 %collective-permute-start.1 = (bf16[144,512]{1,0:T(8,128)(2,1)S(1)}, bf16[144,512]{1,0:T(8,128)(2,1)S(1)}, u32[]{:S(2)}, u32[]{:S(2)}) collective-permute-start(bf16[144,512]{1,0:T(8,128)(2,1)S(1)} %fusion.1), channel_id=1, source_target_pairs={{0,64},{16,80},{32,96},{48,112},{64,0},{80,16},{96,32},{112,48},{1... | collective-permute-start | bytes 442376 | tf_op jit(solution)/shard_map/ppermute | solution.py:48
  7.4 1.3 collective-permute-start
  8.7 1.3 collective-permute-done.2
  10.0 4.3 %collective-permute-done.1 = bf16[144,512]{1,0:T(8,128)(2,1)S(1)} collective-permute-done((bf16[144,512]{1,0:T(8,128)(2,1)S(1)}, bf16[144,512]{1,0:T(8,128)(2,1)S(1)}, u32[]{:S(2)}, u32[]{:S(2)}) %collective-permute-start.1) | collective-permute-done | bytes 147488 | tf_op jit(solution)/shard_map/ppermute | solution.py:48
  14.4 1.9 %copy-done.6 = bf16[224,8192]{1,0:T(8,128)(2,1)} copy-done((bf16[224,8192]{1,0:T(8,128)(2,1)}, bf16[224,8192]{1,0:T(8,128)(2,1)S(1)}, u32[]{:S(2)}) %copy-start.6) | copy-done | bytes 3670040
  16.3 1.6 %collective-permute-start.10 = (bf16[256,512]{1,0:T(8,128)(2,1)S(1)}, bf16[256,512]{1,0:T(8,128)(2,1)S(1)}, u32[]{:S(2)}, u32[]{:S(2)}) collective-permute-start(bf16[256,512]{1,0:T(8,128)(2,1)S(1)} %pad_maximum_fusion.3), channel_id=1, source_target_pairs={{0,1},{1,2},{2,3},{3,0},{4,5},{5,6},{6,7},{7,4},{8,9},{9,10},{10,1... | collective-permute-start | bytes 786440 | tf_op jit(solution)/shard_map/ppermute | solution.py:48
  17.9 2.7 %collective-permute-start.9 = (bf16[256,512]{1,0:T(8,128)(2,1)S(1)}, bf16[256,512]{1,0:T(8,128)(2,1)S(1)}, u32[]{:S(2)}, u32[]{:S(2)}) collective-permute-start(bf16[256,512]{1,0:T(8,128)(2,1)S(1)} %pad_maximum_fusion.3), channel_id=1, source_target_pairs={{0,2},{1,3},{2,0},{3,1},{4,6},{5,7},{6,4},{7,5},{8,10},{9,11},{10,... | collective-permute-start | bytes 786440 | tf_op jit(solution)/shard_map/ppermute | solution.py:48
  20.6 1.4 collective-permute-start.8
  22.1 1.8 %copy-done.8 = bf16[224,8192]{1,0:T(8,128)(2,1)} copy-done((bf16[224,8192]{1,0:T(8,128)(2,1)}, bf16[224,8192]{1,0:T(8,128)(2,1)S(1)}, u32[]{:S(2)}) %copy-start.8) | copy-done | bytes 3670040
  23.9 1.9 %collective-permute-start.7 = (bf16[256,512]{1,0:T(8,128)(2,1)S(1)}, bf16[256,512]{1,0:T(8,128)(2,1)S(1)}, u32[]{:S(2)}, u32[]{:S(2)}) collective-permute-start(bf16[256,512]{1,0:T(8,128)(2,1)S(1)} %pad_maximum_fusion.2), channel_id=1, source_target_pairs={{0,4},{1,5},{2,6},{3,7},{4,8},{5,9},{6,10},{7,11},{8,12},{9,13},{1... | collective-permute-start | bytes 786440 | tf_op jit(solution)/shard_map/ppermute | solution.py:48
  25.9 3.6 %collective-permute-start.6 = (bf16[256,512]{1,0:T(8,128)(2,1)S(1)}, bf16[256,512]{1,0:T(8,128)(2,1)S(1)}, u32[]{:S(2)}, u32[]{:S(2)}) collective-permute-start(bf16[256,512]{1,0:T(8,128)(2,1)S(1)} %pad_maximum_fusion.2), channel_id=1, source_target_pairs={{0,8},{1,9},{2,10},{3,11},{4,12},{5,13},{6,14},{7,15},{8,0},{9,1},... | collective-permute-start | bytes 786440 | tf_op jit(solution)/shard_map/ppermute | solution.py:48
  29.4 1.0 collective-permute-start.5
  30.5 1.2 collective-permute-done.9
  31.7 2.6 %collective-permute-done.7 = bf16[256,512]{1,0:T(8,128)(2,1)S(1)} collective-permute-done((bf16[256,512]{1,0:T(8,128)(2,1)S(1)}, bf16[256,512]{1,0:T(8,128)(2,1)S(1)}, u32[]{:S(2)}, u32[]{:S(2)}) %collective-permute-start.7) | collective-permute-done | bytes 262176 | tf_op jit(solution)/shard_map/ppermute | solution.py:48
  34.3 5.4 %collective-permute-done.6 = bf16[256,512]{1,0:T(8,128)(2,1)S(1)} collective-permute-done((bf16[256,512]{1,0:T(8,128)(2,1)S(1)}, bf16[256,512]{1,0:T(8,128)(2,1)S(1)}, u32[]{:S(2)}, u32[]{:S(2)}) %collective-permute-start.6) | collective-permute-done | bytes 262176 | tf_op jit(solution)/shard_map/ppermute | solution.py:48
  40.0 1.1 pad_maximum_fusion.refs_0_
  41.2 0.5 collective-permute-start.15
  41.7 0.6 collective-permute-start.14
  42.3 2.6 %collective-permute-start.13 = (bf16[4,256,512]{2,1,0:T(8,128)(2,1)S(1)}, bf16[4,256,512]{2,1,0:T(8,128)(2,1)}, u32[]{:S(2)}, u32[]{:S(2)}) collective-permute-start(bf16[4,256,512]{2,1,0:T(8,128)(2,1)S(1)} %pad_maximum_fusion.1.refs_2_.refs_0_), channel_id=1, source_target_pairs={{0,3},{1,0},{2,1},{3,2},{4,7},{5,4},{6,5},{7,6},{8,11},{9,8},{10,9... | collective-permute-start | bytes 3145736 | tf_op jit(solution)/shard_map/ppermute | solution.py:43
  44.9 1.1 collective-permute-start.12
  46.1 2.1 %collective-permute-start.11 = (bf16[4,256,512]{2,1,0:T(8,128)(2,1)}, bf16[4,256,512]{2,1,0:T(8,128)(2,1)}, u32[]{:S(2)}, u32[]{:S(2)}) collective-permute-start(bf16[4,256,512]{2,1,0:T(8,128)(2,1)} %pad_maximum_fusion.refs_0_), channel_id=1, source_target_pairs={{0,12},{1,13},{2,14},{3,15},{4,0},{5,1},{6,2},{7,3},{8,4},{9,5},{1... | collective-permute-start | bytes 3145736 | tf_op jit(solution)/shard_map/ppermute | solution.py:43
  48.4 2.0 %copy-done = bf16[224,8192]{1,0:T(8,128)(2,1)S(1)} copy-done((bf16[224,8192]{1,0:T(8,128)(2,1)S(1)}, bf16[224,8192]{1,0:T(8,128)(2,1)}, u32[]{:S(2)}) %copy-start) | copy-done | bytes 3670040
  50.5 0.8 shard_map.94
  51.4 0.9 slice_bitcast_fusion.2
  52.2 0.7 slice_bitcast_fusion
  53.1 2.0 %copy-done.2 = bf16[224,8192]{1,0:T(8,128)(2,1)S(1)} copy-done((bf16[224,8192]{1,0:T(8,128)(2,1)S(1)}, bf16[224,8192]{1,0:T(8,128)(2,1)}, u32[]{:S(2)}) %copy-start.2) | copy-done | bytes 3670040
  55.1 2.0 %copy-done.4 = bf16[224,8192]{1,0:T(8,128)(2,1)S(1)} copy-done((bf16[224,8192]{1,0:T(8,128)(2,1)S(1)}, bf16[224,8192]{1,0:T(8,128)(2,1)}, u32[]{:S(2)}) %copy-start.4) | copy-done | bytes 3670040
  57.2 4.4 %shard_map.93 = (f32[3,224,256]{2,1,0:T(8,128)S(1)}, f32[3,224,256]{2,1,0:T(8,128)S(1)}) custom-call(s32[48]{0:T(128)S(1)} %concatenate.32.tab, bf16[224,8192]{1,0:T(8,128)(2,1)S(1)} %copy-done.2, bf16[224,8192]{1,0:T(8,128)(2,1)S(1)} %copy-done.4, bf16[224,8192]{1,0:T(8,128)(2,1)S(1)} %copy-done.1, bf16[4,256,512]{2,1,0:T(8,128)(2,1)} %pad_maximum_fusion.refs_0_, ...), custom_call_target="tpu_custom_call" | custom-call | flops 1409286144 | bytes 8388608 | tf_op jit(solution)/shard_map/pallas_call | solution.py:105
  61.6 6.4 %collective-permute-done.14.refs_6_ = bf16[4,256,512]{2,1,0:T(8,128)(2,1)S(1)} collective-permute-done((bf16[4,256,512]{2,1,0:T(8,128)(2,1)S(1)}, bf16[4,256,512]{2,1,0:T(8,128)(2,1)S(1)}, u32[]{:S(2)}, u32[]{:S(2)}) %collective-permute-start.14) | collective-permute-done | bytes 1048608 | tf_op jit(solution)/shard_map/ppermute | solution.py:43
  68.0 3.6 %collective-permute-done.12.refs_4_.refs_6_ = bf16[4,256,512]{2,1,0:T(8,128)(2,1)} collective-permute-done((bf16[4,256,512]{2,1,0:T(8,128)(2,1)}, bf16[4,256,512]{2,1,0:T(8,128)(2,1)}, u32[]{:S(2)}, u32[]{:S(2)}) %collective-permute-start.12) | collective-permute-done | bytes 1048608 | tf_op jit(solution)/shard_map/ppermute | solution.py:43
  71.7 0.5 collective-permute-start.20
  72.3 0.4 collective-permute-start.22
  72.9 2.2 %collective-permute-done.19.refs_1_.refs_3_ = bf16[4,256,512]{2,1,0:T(8,128)(2,1)S(1)} collective-permute-done((bf16[4,256,512]{2,1,0:T(8,128)(2,1)}, bf16[4,256,512]{2,1,0:T(8,128)(2,1)S(1)}, u32[]{:S(2)}, u32[]{:S(2)}) %collective-permute-start.19) | collective-permute-done | bytes 1048608 | tf_op jit(solution)/shard_map/ppermute | solution.py:48
  75.1 1.8 %collective-permute-done.20.refs_3_ = bf16[4,256,512]{2,1,0:T(8,128)(2,1)S(1)} collective-permute-done((bf16[4,256,512]{2,1,0:T(8,128)(2,1)S(1)}, bf16[4,256,512]{2,1,0:T(8,128)(2,1)S(1)}, u32[]{:S(2)}, u32[]{:S(2)}) %collective-permute-start.20) | collective-permute-done | bytes 1048608 | tf_op jit(solution)/shard_map/ppermute | solution.py:48
  77.5 1.5 collective-permute-done.22.refs_7_
  79.0 7.1 %shard_map.95 = (f32[3,224,256]{2,1,0:T(8,128)S(1)}, f32[3,224,256]{2,1,0:T(8,128)S(1)}) custom-call(s32[48]{0:T(128)S(1)} %concatenate.32.tab, bf16[224,8192]{1,0:T(8,128)(2,1)S(1)} %copy-done.3, bf16[224,8192]{1,0:T(8,128)(2,1)S(1)} %copy-done.5, bf16[224,8192]{1,0:T(8,128)(2,1)S(1)} %copy-done.1, ...), custom_call_target="tpu_custom_call" | custom-call | flops 2818572288 | bytes 16777216 | tf_op jit(solution)/shard_map/pallas_call | solution.py:105
  86.4 1.3 collective-permute-done.17.x.refs_4_
  87.7 2.4 %collective-permute-done.18.g.refs_4_ = bf16[4,256,512]{2,1,0:T(8,128)(2,1)S(1)} collective-permute-done((bf16[4,256,512]{2,1,0:T(8,128)(2,1)}, bf16[4,256,512]{2,1,0:T(8,128)(2,1)S(1)}, u32[]{:S(2)}, u32[]{:S(2)}) %collective-permute-start.18) | collective-permute-done | bytes 1048608 | tf_op jit(solution)/shard_map/ppermute | solution.py:43
  90.6 5.1 %shard_map.96 = (bf16[3,224,256]{2,1,0:T(8,128)(2,1)S(1)}, bf16[3,224,256]{2,1,0:T(8,128)(2,1)S(1)}, bf16[2,2,128,224]{3,2,1,0:T(8,128)(2,1)S(1)}, bf16[2,2,128,224]{3,2,1,0:T(8,128)(2,1)S(1)}) custom-call(s32[48]{0:T(128)S(1)} %concatenate.32.tab, bf16[224,8192]{1,0:T(8,128)(2,1)S(1)} %copy-done.3, bf16[224,8192]{1,0:T(8,128)(2,1)S(1)} %copy-done.5, ...), custom_call_target="tpu_custom_call" | custom-call | flops 1409286144 | bytes 8388608 | tf_op jit(solution)/shard_map/pallas_call | solution.py:160
  96.0 7.0 %shard_map.97 = (bf16[4,128,512]{2,1,0:T(8,128)(2,1)S(1)}, bf16[4,128,512]{2,1,0:T(8,128)(2,1)S(1)}, bf16[4,128,512]{2,1,0:T(8,128)(2,1)S(1)}, bf16[4,128,512]{2...) custom-call(s32[48]{0:T(128)S(1)} %concatenate.32.tab, ...), custom_call_target="tpu_custom_call" | custom-call | flops 3758096384 | bytes 18874368 | tf_op jit(solution)/shard_map/pallas_call | solution.py:257
  103.2 3.1 %collective-permute-start.27 = (bf16[4,128,512]{2,1,0:T(8,128)(2,1)S(1)}, bf16[4,128,512]{2,1,0:T(8,128)(2,1)S(1)}, u32[]{:S(2)}, u32[]{:S(2)}) collective-permute-start(bf16[4,128,512]{2,1,0:T(8,128)(2,1)S(1)} %get-tuple-element.108), channel_id=1, source_target_pairs={{0,3},{1,0},{2,1},{3,2},{4,7},{5,4},{6,5},{7,6},{8,11},{9,8},{10,9... | collective-permute-start | bytes 1572872 | tf_op jit(solution)/shard_map/ppermute | solution.py:43
  106.4 3.2 %collective-permute-start.28 = (bf16[4,128,512]{2,1,0:T(8,128)(2,1)S(1)}, bf16[4,128,512]{2,1,0:T(8,128)(2,1)S(1)}, u32[]{:S(2)}, u32[]{:S(2)}) collective-permute-start(bf16[4,128,512]{2,1,0:T(8,128)(2,1)S(1)} %get-tuple-element.109), channel_id=1, source_target_pairs={{0,12},{1,13},{2,14},{3,15},{4,0},{5,1},{6,2},{7,3},{8,4},{9,5},{1... | collective-permute-start | bytes 1572872 | tf_op jit(solution)/shard_map/ppermute | solution.py:43
  109.6 8.6 %shard_map.98 = (bf16[224,8192]{1,0:T(8,128)(2,1)}, bf16[224,8192]{1,0:T(8,128)(2,1)}) custom-call(s32[48]{0:T(128)S(1)} %concatenate.32.tab, bf16[3,224,256]{2,1,0:T(8,128)(2,1)S(1)} %get-tuple-element.110.own_t, bf16[3,224,256]{2,1,0:T(8,128)(2,1)S(1)} %collective-permute-done.29.far_t, bf16[4,256,512]{2,1,0:T(8,128)(2,1)} %pad_maximum_fusion.refs_0_, ...), custom_call_target="tpu_custom_call" | custom-call | flops 3758096384 | bytes 12582912 | tf_op jit(solution)/shard_map/pallas_call | solution.py:212
  118.4 0.8 collective-permute-start.31
  119.4 5.6 %shard_map.101 = bf16[224,8192]{1,0:T(8,128)(2,1)} custom-call(s32[48]{0:T(128)S(1)} %concatenate.32.tab, bf16[3,224,256]{2,1,0:T(8,128)(2,1)S(1)} %get-tuple-element.110.own_t, bf16[3,224,256]{2,1,0:T(8,128)(2,1)S(1)} %collective-permute-done.29.far_t, bf16[4,256,512]{2,1,0:T(8,128)(2,1)S(1)} %pad_maximum_fusion.1.refs_2_.refs_0_, ...), custom_call_target="tpu_custom_call" | custom-call | flops 1879048192 | bytes 6291456 | tf_op jit(solution)/shard_map/pallas_call | solution.py:212
  125.0 3.9 %collective-permute-done.31.c = bf16[4,128,512]{2,1,0:T(8,128)(2,1)S(1)} collective-permute-done((bf16[4,128,512]{2,1,0:T(8,128)(2,1)S(1)}, bf16[4,128,512]{2,1,0:T(8,128)(2,1)S(1)}, u32[]{:S(2)}, u32[]{:S(2)}) %collective-permute-start.31) | collective-permute-done | bytes 524320 | tf_op jit(solution)/shard_map/ppermute | solution.py:43
  128.9 0.9 collective-permute-done.32.c
  130.0 3.3 %collective-permute-start.37 = (bf16[128,512]{1,0:T(8,128)(2,1)S(1)}, bf16[128,512]{1,0:T(8,128)(2,1)S(1)}, u32[]{:S(2)}, u32[]{:S(2)}) collective-permute-start(bf16[128,512]{1,0:T(8,128)(2,1)S(1)} %get-tuple-element.128), channel_id=1, source_target_pairs={{0,2},{1,3},{2,0},{3,1},{4,6},{5,7},{6,4},{7,5},{8,10},{9,11},{10,... | collective-permute-start | bytes 393224 | tf_op jit(solution)/shard_map/ppermute | solution.py:48
  133.4 3.1 %collective-permute-start.39 = (bf16[128,512]{1,0:T(8,128)(2,1)S(1)}, bf16[128,512]{1,0:T(8,128)(2,1)S(1)}, u32[]{:S(2)}, u32[]{:S(2)}) collective-permute-start(bf16[128,512]{1,0:T(8,128)(2,1)S(1)} %get-tuple-element.130), channel_id=1, source_target_pairs={{0,3},{1,0},{2,1},{3,2},{4,7},{5,4},{6,5},{7,6},{8,11},{9,8},{10,9... | collective-permute-start | bytes 393224 | tf_op jit(solution)/shard_map/ppermute | solution.py:43
  136.8 0.5 collective-permute-start.35
  137.3 0.6 collective-permute-done.37.refs_5_
  137.8 2.3 %collective-permute-start.36 = (bf16[128,512]{1,0:T(8,128)(2,1)S(1)}, bf16[128,512]{1,0:T(8,128)(2,1)S(1)}, u32[]{:S(2)}, u32[]{:S(2)}) collective-permute-start(bf16[128,512]{1,0:T(8,128)(2,1)S(1)} %get-tuple-element.123), channel_id=1, source_target_pairs={{0,12},{1,13},{2,14},{3,15},{4,0},{5,1},{6,2},{7,3},{8,4},{9,5},{1... | collective-permute-start | bytes 393224 | tf_op jit(solution)/shard_map/ppermute | solution.py:43
  140.3 3.0 %collective-permute-done.34.refs_1_ = bf16[128,512]{1,0:T(8,128)(2,1)S(1)} collective-permute-done((bf16[128,512]{1,0:T(8,128)(2,1)S(1)}, bf16[128,512]{1,0:T(8,128)(2,1)S(1)}, u32[]{:S(2)}, u32[]{:S(2)}) %collective-permute-start.34) | collective-permute-done | bytes 131104 | tf_op jit(solution)/shard_map/ppermute | solution.py:48
  143.4 2.0 %collective-permute-done.35.refs_2_ = bf16[128,512]{1,0:T(8,128)(2,1)S(1)} collective-permute-done((bf16[128,512]{1,0:T(8,128)(2,1)S(1)}, bf16[128,512]{1,0:T(8,128)(2,1)S(1)}, u32[]{:S(2)}, u32[]{:S(2)}) %collective-permute-start.35) | collective-permute-done | bytes 131104 | tf_op jit(solution)/shard_map/ppermute | solution.py:43
  145.4 2.4 %collective-permute-start.40 = (bf16[64,512]{1,0:T(8,128)(2,1)S(1)}, bf16[64,512]{1,0:T(8,128)(2,1)S(1)}, u32[]{:S(2)}, u32[]{:S(2)}) collective-permute-start(bf16[64,512]{1,0:T(8,128)(2,1)S(1)} %get-tuple-element.132), channel_id=1, source_target_pairs={{0,64},{16,80},{32,96},{48,112},{64,0},{80,16},{96,32},{112,48},{1... | collective-permute-start | bytes 196616 | tf_op jit(solution)/shard_map/ppermute | solution.py:48
  147.8 0.9 collective-permute-start.41
  148.7 2.3 %collective-permute-start.42 = (bf16[64,512]{1,0:T(8,128)(2,1)S(1)}, bf16[64,512]{1,0:T(8,128)(2,1)S(1)}, u32[]{:S(2)}, u32[]{:S(2)}) collective-permute-start(bf16[64,512]{1,0:T(8,128)(2,1)S(1)} %get-tuple-element.134), channel_id=1, source_target_pairs={{0,96},{16,112},{32,0},{48,16},{64,32},{80,48},{96,64},{112,80},{1... | collective-permute-start | bytes 196616 | tf_op jit(solution)/shard_map/ppermute | solution.py:48
  151.1 0.7 collective-permute-done.40
  151.7 1.6 %collective-permute-done.41 = bf16[64,512]{1,0:T(8,128)(2,1)S(1)} collective-permute-done((bf16[64,512]{1,0:T(8,128)(2,1)S(1)}, bf16[64,512]{1,0:T(8,128)(2,1)S(1)}, u32[]{:S(2)}, u32[]{:S(2)}) %collective-permute-start.41) | collective-permute-done | bytes 65568 | tf_op jit(solution)/shard_map/ppermute | solution.py:48
  153.3 0.7 add_convert_fusion
  (80 shorter events, 4.6 us)
Async XLA Ops:
  0.6 13.8 %collective-permute-start.3 = (bf16[224,8192]{1,0:T(8,128)(2,1)}, bf16[224,8192]{1,0:T(8,128)(2,1)S(1)}, u32[]{:S(2)}, u32[]{:S(2)}) collective-permute-start(bf16[224,8192]{1,0:T(8,128)(2,1)} %refs_0_.1), channel_id=1, source_target_pairs={{0,16},{16,0},{32,48},{48,32},{64,80},{80,64},{96,112},{112,96},{1... | collective-permute-start | bytes 11010056 | tf_op jit(solution)/shard_map/ppermute | solution.py:48
  0.7 21.4 %collective-permute-start.4 = (bf16[224,8192]{1,0:T(8,128)(2,1)}, bf16[224,8192]{1,0:T(8,128)(2,1)S(1)}, u32[]{:S(2)}, u32[]{:S(2)}) collective-permute-start(bf16[224,8192]{1,0:T(8,128)(2,1)} %refs_1_.1), channel_id=1, source_target_pairs={{0,16},{16,0},{32,48},{48,32},{64,80},{80,64},{96,112},{112,96},{1... | collective-permute-start | bytes 11010056 | tf_op jit(solution)/shard_map/ppermute | solution.py:48
  2.8 7.3 %collective-permute-start.2 = (bf16[144,512]{1,0:T(8,128)(2,1)S(1)}, bf16[144,512]{1,0:T(8,128)(2,1)S(1)}, u32[]{:S(2)}, u32[]{:S(2)}) collective-permute-start(bf16[144,512]{1,0:T(8,128)(2,1)S(1)} %fusion.1), channel_id=1, source_target_pairs={{0,32},{16,48},{32,64},{48,80},{64,96},{80,112},{96,0},{112,16},{1... | collective-permute-start | bytes 442376 | tf_op jit(solution)/shard_map/ppermute | solution.py:48
  4.5 9.9 %collective-permute-start.1 = (bf16[144,512]{1,0:T(8,128)(2,1)S(1)}, bf16[144,512]{1,0:T(8,128)(2,1)S(1)}, u32[]{:S(2)}, u32[]{:S(2)}) collective-permute-start(bf16[144,512]{1,0:T(8,128)(2,1)S(1)} %fusion.1), channel_id=1, source_target_pairs={{0,64},{16,80},{32,96},{48,112},{64,0},{80,16},{96,32},{112,48},{1... | collective-permute-start | bytes 442376 | tf_op jit(solution)/shard_map/ppermute | solution.py:48
  7.4 7.0 %collective-permute-start = (bf16[144,512]{1,0:T(8,128)(2,1)S(1)}, bf16[144,512]{1,0:T(8,128)(2,1)S(1)}, u32[]{:S(2)}, u32[]{:S(2)}) collective-permute-start(bf16[144,512]{1,0:T(8,128)(2,1)S(1)} %fusion.1), channel_id=1, source_target_pairs={{0,96},{16,112},{32,0},{48,16},{64,32},{80,48},{96,64},{112,80},{1... | collective-permute-start | bytes 442376 | tf_op jit(solution)/shard_map/ppermute | solution.py:48
  14.4 15.1 %copy-start.10 = (bf16[144,512]{1,0:T(8,128)(2,1)}, bf16[144,512]{1,0:T(8,128)(2,1)S(1)}, u32[]{:S(2)}) copy-start(bf16[144,512]{1,0:T(8,128)(2,1)S(1)} %collective-permute-done.1) | copy-start | bytes 442372
  14.4 1.9 %copy-start.11 = (bf16[144,512]{1,0:T(8,128)(2,1)}, bf16[144,512]{1,0:T(8,128)(2,1)S(1)}, u32[]{:S(2)}) copy-start(bf16[144,512]{1,0:T(8,128)(2,1)S(1)} %collective-permute-done) | copy-start | bytes 442372
  14.4 1.9 %copy-start.6 = (bf16[224,8192]{1,0:T(8,128)(2,1)}, bf16[224,8192]{1,0:T(8,128)(2,1)S(1)}, u32[]{:S(2)}) copy-start(bf16[224,8192]{1,0:T(8,128)(2,1)S(1)} %collective-permute-done.3.far_wg.refs_2_) | copy-start | bytes 11010052
  16.3 13.1 %collective-permute-start.10 = (bf16[256,512]{1,0:T(8,128)(2,1)S(1)}, bf16[256,512]{1,0:T(8,128)(2,1)S(1)}, u32[]{:S(2)}, u32[]{:S(2)}) collective-permute-start(bf16[256,512]{1,0:T(8,128)(2,1)S(1)} %pad_maximum_fusion.3), channel_id=1, source_target_pairs={{0,1},{1,2},{2,3},{3,0},{4,5},{5,6},{6,7},{7,4},{8,9},{9,10},{10,1... | collective-permute-start | bytes 786440 | tf_op jit(solution)/shard_map/ppermute | solution.py:48
  17.9 13.8 %collective-permute-start.9 = (bf16[256,512]{1,0:T(8,128)(2,1)S(1)}, bf16[256,512]{1,0:T(8,128)(2,1)S(1)}, u32[]{:S(2)}, u32[]{:S(2)}) collective-permute-start(bf16[256,512]{1,0:T(8,128)(2,1)S(1)} %pad_maximum_fusion.3), channel_id=1, source_target_pairs={{0,2},{1,3},{2,0},{3,1},{4,6},{5,7},{6,4},{7,5},{8,10},{9,11},{10,... | collective-permute-start | bytes 786440 | tf_op jit(solution)/shard_map/ppermute | solution.py:48
  20.6 11.1 %collective-permute-start.8 = (bf16[256,512]{1,0:T(8,128)(2,1)S(1)}, bf16[256,512]{1,0:T(8,128)(2,1)S(1)}, u32[]{:S(2)}, u32[]{:S(2)}) collective-permute-start(bf16[256,512]{1,0:T(8,128)(2,1)S(1)} %pad_maximum_fusion.3), channel_id=1, source_target_pairs={{0,3},{1,0},{2,1},{3,2},{4,7},{5,4},{6,5},{7,6},{8,11},{9,8},{10,9... | collective-permute-start | bytes 786440 | tf_op jit(solution)/shard_map/ppermute | solution.py:48
  22.1 1.8 %copy-start.8 = (bf16[224,8192]{1,0:T(8,128)(2,1)}, bf16[224,8192]{1,0:T(8,128)(2,1)S(1)}, u32[]{:S(2)}) copy-start(bf16[224,8192]{1,0:T(8,128)(2,1)S(1)} %collective-permute-done.4.far_wu.refs_3_) | copy-start | bytes 11010052
  23.9 10.4 %collective-permute-start.7 = (bf16[256,512]{1,0:T(8,128)(2,1)S(1)}, bf16[256,512]{1,0:T(8,128)(2,1)S(1)}, u32[]{:S(2)}, u32[]{:S(2)}) collective-permute-start(bf16[256,512]{1,0:T(8,128)(2,1)S(1)} %pad_maximum_fusion.2), channel_id=1, source_target_pairs={{0,4},{1,5},{2,6},{3,7},{4,8},{5,9},{6,10},{7,11},{8,12},{9,13},{1... | collective-permute-start | bytes 786440 | tf_op jit(solution)/shard_map/ppermute | solution.py:48
  25.9 13.8 %collective-permute-start.6 = (bf16[256,512]{1,0:T(8,128)(2,1)S(1)}, bf16[256,512]{1,0:T(8,128)(2,1)S(1)}, u32[]{:S(2)}, u32[]{:S(2)}) collective-permute-start(bf16[256,512]{1,0:T(8,128)(2,1)S(1)} %pad_maximum_fusion.2), channel_id=1, source_target_pairs={{0,8},{1,9},{2,10},{3,11},{4,12},{5,13},{6,14},{7,15},{8,0},{9,1},... | collective-permute-start | bytes 786440 | tf_op jit(solution)/shard_map/ppermute | solution.py:48
  29.4 10.2 %collective-permute-start.5 = (bf16[256,512]{1,0:T(8,128)(2,1)S(1)}, bf16[256,512]{1,0:T(8,128)(2,1)S(1)}, u32[]{:S(2)}, u32[]{:S(2)}) collective-permute-start(bf16[256,512]{1,0:T(8,128)(2,1)S(1)} %pad_maximum_fusion.2), channel_id=1, source_target_pairs={{0,12},{1,13},{2,14},{3,15},{4,0},{5,1},{6,2},{7,3},{8,4},{9,5},{1... | collective-permute-start | bytes 786440 | tf_op jit(solution)/shard_map/ppermute | solution.py:48
  39.8 6.3 %collective-permute-start.16 = (bf16[4,256,512]{2,1,0:T(8,128)(2,1)S(1)}, bf16[4,256,512]{2,1,0:T(8,128)(2,1)S(1)}, u32[]{:S(2)}, u32[]{:S(2)}) collective-permute-start(bf16[4,256,512]{2,1,0:T(8,128)(2,1)S(1)} %pad_maximum_fusion.1.refs_2_.refs_0_), channel_id=1, source_target_pairs={{0,16},{16,0},{32,48},{48,32},{64,80},{80,64},{96,112},{112,96},{1... | collective-permute-start | bytes 3145736 | tf_op jit(solution)/shard_map/ppermute | solution.py:48
  41.2 11.9 %collective-permute-start.15 = (bf16[4,256,512]{2,1,0:T(8,128)(2,1)}, bf16[4,256,512]{2,1,0:T(8,128)(2,1)}, u32[]{:S(2)}, u32[]{:S(2)}) collective-permute-start(bf16[4,256,512]{2,1,0:T(8,128)(2,1)} %pad_maximum_fusion.refs_0_), channel_id=1, source_target_pairs={{0,16},{16,0},{32,48},{48,32},{64,80},{80,64},{96,112},{112,96},{1... | collective-permute-start | bytes 3145736 | tf_op jit(solution)/shard_map/ppermute | solution.py:48
  41.7 26.3 %collective-permute-start.14 = (bf16[4,256,512]{2,1,0:T(8,128)(2,1)S(1)}, bf16[4,256,512]{2,1,0:T(8,128)(2,1)S(1)}, u32[]{:S(2)}, u32[]{:S(2)}) collective-permute-start(bf16[4,256,512]{2,1,0:T(8,128)(2,1)S(1)} %pad_maximum_fusion.1.refs_2_.refs_0_), channel_id=1, source_target_pairs={{0,1},{1,2},{2,3},{3,0},{4,5},{5,6},{6,7},{7,4},{8,9},{9,10},{10,1... | collective-permute-start | bytes 3145736 | tf_op jit(solution)/shard_map/ppermute | solution.py:43
  42.3 25.7 %collective-permute-start.13 = (bf16[4,256,512]{2,1,0:T(8,128)(2,1)S(1)}, bf16[4,256,512]{2,1,0:T(8,128)(2,1)}, u32[]{:S(2)}, u32[]{:S(2)}) collective-permute-start(bf16[4,256,512]{2,1,0:T(8,128)(2,1)S(1)} %pad_maximum_fusion.1.refs_2_.refs_0_), channel_id=1, source_target_pairs={{0,3},{1,0},{2,1},{3,2},{4,7},{5,4},{6,5},{7,6},{8,11},{9,8},{10,9... | collective-permute-start | bytes 3145736 | tf_op jit(solution)/shard_map/ppermute | solution.py:43
  44.9 26.7 %collective-permute-start.12 = (bf16[4,256,512]{2,1,0:T(8,128)(2,1)}, bf16[4,256,512]{2,1,0:T(8,128)(2,1)}, u32[]{:S(2)}, u32[]{:S(2)}) collective-permute-start(bf16[4,256,512]{2,1,0:T(8,128)(2,1)} %pad_maximum_fusion.refs_0_), channel_id=1, source_target_pairs={{0,4},{1,5},{2,6},{3,7},{4,8},{5,9},{6,10},{7,11},{8,12},{9,13},{1... | collective-permute-start | bytes 3145736 | tf_op jit(solution)/shard_map/ppermute | solution.py:43
  46.1 25.5 %collective-permute-start.11 = (bf16[4,256,512]{2,1,0:T(8,128)(2,1)}, bf16[4,256,512]{2,1,0:T(8,128)(2,1)}, u32[]{:S(2)}, u32[]{:S(2)}) collective-permute-start(bf16[4,256,512]{2,1,0:T(8,128)(2,1)} %pad_maximum_fusion.refs_0_), channel_id=1, source_target_pairs={{0,12},{1,13},{2,14},{3,15},{4,0},{5,1},{6,2},{7,3},{8,4},{9,5},{1... | collective-permute-start | bytes 3145736 | tf_op jit(solution)/shard_map/ppermute | solution.py:43
  48.4 2.0 %copy-start = (bf16[224,8192]{1,0:T(8,128)(2,1)S(1)}, bf16[224,8192]{1,0:T(8,128)(2,1)}, u32[]{:S(2)}) copy-start(bf16[224,8192]{1,0:T(8,128)(2,1)} %wd.5) | copy-start | bytes 11010052
  50.5 2.6 %copy-start.1 = (bf16[224,8192]{1,0:T(8,128)(2,1)S(1)}, bf16[224,8192]{1,0:T(8,128)(2,1)}, u32[]{:S(2)}) copy-start(bf16[224,8192]{1,0:T(8,128)(2,1)} %wd.5) | copy-start | bytes 11010052
  53.1 2.0 %copy-start.2 = (bf16[224,8192]{1,0:T(8,128)(2,1)S(1)}, bf16[224,8192]{1,0:T(8,128)(2,1)}, u32[]{:S(2)}) copy-start(bf16[224,8192]{1,0:T(8,128)(2,1)} %refs_0_.1) | copy-start | bytes 11010052
  55.1 2.0 %copy-start.4 = (bf16[224,8192]{1,0:T(8,128)(2,1)S(1)}, bf16[224,8192]{1,0:T(8,128)(2,1)}, u32[]{:S(2)}) copy-start(bf16[224,8192]{1,0:T(8,128)(2,1)} %refs_1_.1) | copy-start | bytes 11010052
  57.2 21.9 %copy-start.3 = (bf16[224,8192]{1,0:T(8,128)(2,1)S(1)}, bf16[224,8192]{1,0:T(8,128)(2,1)}, u32[]{:S(2)}) copy-start(bf16[224,8192]{1,0:T(8,128)(2,1)} %refs_0_.1) | copy-start | bytes 11010052
  57.2 21.9 %copy-start.5 = (bf16[224,8192]{1,0:T(8,128)(2,1)S(1)}, bf16[224,8192]{1,0:T(8,128)(2,1)}, u32[]{:S(2)}) copy-start(bf16[224,8192]{1,0:T(8,128)(2,1)} %refs_1_.1) | copy-start | bytes 11010052
  71.6 19.1 %copy-start.7 = (bf16[224,8192]{1,0:T(8,128)(2,1)S(1)}, bf16[224,8192]{1,0:T(8,128)(2,1)}, u32[]{:S(2)}) copy-start(bf16[224,8192]{1,0:T(8,128)(2,1)} %copy-done.6) | copy-start | bytes 11010052
  71.6 19.1 %copy-start.9 = (bf16[224,8192]{1,0:T(8,128)(2,1)S(1)}, bf16[224,8192]{1,0:T(8,128)(2,1)}, u32[]{:S(2)}) copy-start(bf16[224,8192]{1,0:T(8,128)(2,1)} %copy-done.8) | copy-start | bytes 11010052
  71.6 3.5 %collective-permute-start.19 = (bf16[4,256,512]{2,1,0:T(8,128)(2,1)}, bf16[4,256,512]{2,1,0:T(8,128)(2,1)S(1)}, u32[]{:S(2)}, u32[]{:S(2)}) collective-permute-start(bf16[4,256,512]{2,1,0:T(8,128)(2,1)} %collective-permute-done.12.refs_4_.refs_6_), channel_id=1, source_target_pairs={{0,16},{16,0},{32,48},{48,32},{64,80},{80,64},{96,112},{112,96},{1... | collective-permute-start | bytes 3145736 | tf_op jit(solution)/shard_map/ppermute | solution.py:48
  71.7 5.3 %collective-permute-start.20 = (bf16[4,256,512]{2,1,0:T(8,128)(2,1)S(1)}, bf16[4,256,512]{2,1,0:T(8,128)(2,1)S(1)}, u32[]{:S(2)}, u32[]{:S(2)}) collective-permute-start(bf16[4,256,512]{2,1,0:T(8,128)(2,1)S(1)} %collective-permute-done.14.refs_6_), channel_id=1, source_target_pairs={{0,16},{16,0},{32,48},{48,32},{64,80},{80,64},{96,112},{112,96},{1... | collective-permute-start | bytes 3145736 | tf_op jit(solution)/shard_map/ppermute | solution.py:48
  72.2 5.4 %collective-permute-start.21 = (bf16[4,256,512]{2,1,0:T(8,128)(2,1)}, bf16[4,256,512]{2,1,0:T(8,128)(2,1)S(1)}, u32[]{:S(2)}, u32[]{:S(2)}) collective-permute-start(bf16[4,256,512]{2,1,0:T(8,128)(2,1)} %collective-permute-done.11.refs_0_.refs_2_), channel_id=1, source_target_pairs={{0,16},{16,0},{32,48},{48,32},{64,80},{80,64},{96,112},{112,96},{1... | collective-permute-start | bytes 3145736 | tf_op jit(solution)/shard_map/ppermute | solution.py:48
  72.3 6.8 %collective-permute-start.22 = (bf16[4,256,512]{2,1,0:T(8,128)(2,1)}, bf16[4,256,512]{2,1,0:T(8,128)(2,1)S(1)}, u32[]{:S(2)}, u32[]{:S(2)}) collective-permute-start(bf16[4,256,512]{2,1,0:T(8,128)(2,1)} %collective-permute-done.13.refs_2_), channel_id=1, source_target_pairs={{0,16},{16,0},{32,48},{48,32},{64,80},{80,64},{96,112},{112,96},{1... | collective-permute-start | bytes 3145736 | tf_op jit(solution)/shard_map/ppermute | solution.py:48
  72.7 15.0 %collective-permute-start.17 = (bf16[4,256,512]{2,1,0:T(8,128)(2,1)}, bf16[4,256,512]{2,1,0:T(8,128)(2,1)S(1)}, u32[]{:S(2)}, u32[]{:S(2)}) collective-permute-start(bf16[4,256,512]{2,1,0:T(8,128)(2,1)} %collective-permute-done.11.refs_0_.refs_2_), channel_id=1, source_target_pairs={{0,12},{1,13},{2,14},{3,15},{4,0},{5,1},{6,2},{7,3},{8,4},{9,5},{1... | collective-permute-start | bytes 3145736 | tf_op jit(solution)/shard_map/ppermute | solution.py:43
  75.1 15.0 %collective-permute-start.18 = (bf16[4,256,512]{2,1,0:T(8,128)(2,1)}, bf16[4,256,512]{2,1,0:T(8,128)(2,1)S(1)}, u32[]{:S(2)}, u32[]{:S(2)}) collective-permute-start(bf16[4,256,512]{2,1,0:T(8,128)(2,1)} %collective-permute-done.13.refs_2_), channel_id=1, source_target_pairs={{0,3},{1,0},{2,1},{3,2},{4,7},{5,4},{6,5},{7,6},{8,11},{9,8},{10,9... | collective-permute-start | bytes 3145736 | tf_op jit(solution)/shard_map/ppermute | solution.py:43
  77.0 9.4 %collective-permute-start.24 = (bf16[4,224,512]{2,1,0:T(8,128)(2,1)S(1)}, bf16[4,224,512]{2,1,0:T(8,128)(2,1)S(1)}, u32[]{:S(2)}, u32[]{:S(2)}) collective-permute-start(bf16[4,224,512]{2,1,0:T(8,128)(2,1)S(1)} %shard_map.94), channel_id=1, source_target_pairs={{0,16},{16,0},{32,48},{48,32},{64,80},{80,64},{96,112},{112,96},{1... | collective-permute-start | bytes 2752520 | tf_op jit(solution)/shard_map/ppermute | solution.py:48
  86.1 4.0 %collective-permute-start.23 = (f32[3,224,256]{2,1,0:T(8,128)S(1)}, f32[3,224,256]{2,1,0:T(8,128)S(1)}, u32[]{:S(2)}, u32[]{:S(2)}) collective-permute-start(f32[3,224,256]{2,1,0:T(8,128)S(1)} %get-tuple-element.95), channel_id=1, source_target_pairs={{0,16},{16,0},{32,48},{48,32},{64,80},{80,64},{96,112},{112,96},{1... | collective-permute-start | bytes 2064392 | tf_op jit(solution)/shard_map/ppermute | solution.py:48
  90.1 16.2 %collective-permute-start.30 = (bf16[4,256,512]{2,1,0:T(8,128)(2,1)S(1)}, bf16[4,256,512]{2,1,0:T(8,128)(2,1)S(1)}, u32[]{:S(2)}, u32[]{:S(2)}) collective-permute-start(bf16[4,256,512]{2,1,0:T(8,128)(2,1)S(1)} %collective-permute-done.17.x.refs_4_), channel_id=1, source_target_pairs={{0,16},{16,0},{32,48},{48,32},{64,80},{80,64},{96,112},{112,96},{1... | collective-permute-start | bytes 3145736 | tf_op jit(solution)/shard_map/ppermute | solution.py:48
  90.3 29.1 %collective-permute-start.33 = (bf16[4,256,512]{2,1,0:T(8,128)(2,1)S(1)}, bf16[4,256,512]{2,1,0:T(8,128)(2,1)S(1)}, u32[]{:S(2)}, u32[]{:S(2)}) collective-permute-start(bf16[4,256,512]{2,1,0:T(8,128)(2,1)S(1)} %collective-permute-done.18.g.refs_4_), channel_id=1, source_target_pairs={{0,16},{16,0},{32,48},{48,32},{64,80},{80,64},{96,112},{112,96},{1... | collective-permute-start | bytes 3145736 | tf_op jit(solution)/shard_map/ppermute | solution.py:48
  95.8 7.5 %collective-permute-start.29 = (bf16[3,224,256]{2,1,0:T(8,128)(2,1)S(1)}, bf16[3,224,256]{2,1,0:T(8,128)(2,1)S(1)}, u32[]{:S(2)}, u32[]{:S(2)}) collective-permute-start(bf16[3,224,256]{2,1,0:T(8,128)(2,1)S(1)} %get-tuple-element.111), channel_id=1, source_target_pairs={{0,16},{16,0},{32,48},{48,32},{64,80},{80,64},{96,112},{112,96},{1... | collective-permute-start | bytes 1032200 | tf_op jit(solution)/shard_map/ppermute | solution.py:48
  103.0 15.2 %collective-permute-start.25 = (bf16[4,128,512]{2,1,0:T(8,128)(2,1)S(1)}, bf16[4,128,512]{2,1,0:T(8,128)(2,1)S(1)}, u32[]{:S(2)}, u32[]{:S(2)}) collective-permute-start(bf16[4,128,512]{2,1,0:T(8,128)(2,1)S(1)} %get-tuple-element.106), channel_id=1, source_target_pairs={{0,1},{1,2},{2,3},{3,0},{4,5},{5,6},{6,7},{7,4},{8,9},{9,10},{10,1... | collective-permute-start | bytes 1572872 | tf_op jit(solution)/shard_map/ppermute | solution.py:43
  103.1 15.1 %collective-permute-start.26 = (bf16[4,128,512]{2,1,0:T(8,128)(2,1)S(1)}, bf16[4,128,512]{2,1,0:T(8,128)(2,1)S(1)}, u32[]{:S(2)}, u32[]{:S(2)}) collective-permute-start(bf16[4,128,512]{2,1,0:T(8,128)(2,1)S(1)} %get-tuple-element.107), channel_id=1, source_target_pairs={{0,4},{1,5},{2,6},{3,7},{4,8},{5,9},{6,10},{7,11},{8,12},{9,13},{1... | collective-permute-start | bytes 1572872 | tf_op jit(solution)/shard_map/ppermute | solution.py:43
  103.2 15.0 %collective-permute-start.27 = (bf16[4,128,512]{2,1,0:T(8,128)(2,1)S(1)}, bf16[4,128,512]{2,1,0:T(8,128)(2,1)S(1)}, u32[]{:S(2)}, u32[]{:S(2)}) collective-permute-start(bf16[4,128,512]{2,1,0:T(8,128)(2,1)S(1)} %get-tuple-element.108), channel_id=1, source_target_pairs={{0,3},{1,0},{2,1},{3,2},{4,7},{5,4},{6,5},{7,6},{8,11},{9,8},{10,9... | collective-permute-start | bytes 1572872 | tf_op jit(solution)/shard_map/ppermute | solution.py:43
  106.4 11.9 %collective-permute-start.28 = (bf16[4,128,512]{2,1,0:T(8,128)(2,1)S(1)}, bf16[4,128,512]{2,1,0:T(8,128)(2,1)S(1)}, u32[]{:S(2)}, u32[]{:S(2)}) collective-permute-start(bf16[4,128,512]{2,1,0:T(8,128)(2,1)S(1)} %get-tuple-element.109), channel_id=1, source_target_pairs={{0,12},{1,13},{2,14},{3,15},{4,0},{5,1},{6,2},{7,3},{8,4},{9,5},{1... | collective-permute-start | bytes 1572872 | tf_op jit(solution)/shard_map/ppermute | solution.py:43
  118.4 10.5 %collective-permute-start.31 = (bf16[4,128,512]{2,1,0:T(8,128)(2,1)S(1)}, bf16[4,128,512]{2,1,0:T(8,128)(2,1)S(1)}, u32[]{:S(2)}, u32[]{:S(2)}) collective-permute-start(bf16[4,128,512]{2,1,0:T(8,128)(2,1)S(1)} %shard_map.99), channel_id=1, source_target_pairs={{0,1},{1,2},{2,3},{3,0},{4,5},{5,6},{6,7},{7,4},{8,9},{9,10},{10,1... | collective-permute-start | bytes 1572872 | tf_op jit(solution)/shard_map/ppermute | solution.py:43
  119.3 10.5 %collective-permute-start.32 = (bf16[4,128,512]{2,1,0:T(8,128)(2,1)S(1)}, bf16[4,128,512]{2,1,0:T(8,128)(2,1)S(1)}, u32[]{:S(2)}, u32[]{:S(2)}) collective-permute-start(bf16[4,128,512]{2,1,0:T(8,128)(2,1)S(1)} %shard_map.100), channel_id=1, source_target_pairs={{0,4},{1,5},{2,6},{3,7},{4,8},{5,9},{6,10},{7,11},{8,12},{9,13},{1... | collective-permute-start | bytes 1572872 | tf_op jit(solution)/shard_map/ppermute | solution.py:43
  130.0 7.9 %collective-permute-start.37 = (bf16[128,512]{1,0:T(8,128)(2,1)S(1)}, bf16[128,512]{1,0:T(8,128)(2,1)S(1)}, u32[]{:S(2)}, u32[]{:S(2)}) collective-permute-start(bf16[128,512]{1,0:T(8,128)(2,1)S(1)} %get-tuple-element.128), channel_id=1, source_target_pairs={{0,2},{1,3},{2,0},{3,1},{4,6},{5,7},{6,4},{7,5},{8,10},{9,11},{10,... | collective-permute-start | bytes 393224 | tf_op jit(solution)/shard_map/ppermute | solution.py:48
  133.3 7.0 %collective-permute-start.38 = (bf16[128,512]{1,0:T(8,128)(2,1)S(1)}, bf16[128,512]{1,0:T(8,128)(2,1)S(1)}, u32[]{:S(2)}, u32[]{:S(2)}) collective-permute-start(bf16[128,512]{1,0:T(8,128)(2,1)S(1)} %get-tuple-element.129), channel_id=1, source_target_pairs={{0,1},{1,2},{2,3},{3,0},{4,5},{5,6},{6,7},{7,4},{8,9},{9,10},{10,1... | collective-permute-start | bytes 393224 | tf_op jit(solution)/shard_map/ppermute | solution.py:43
  133.4 6.9 %collective-permute-start.39 = (bf16[128,512]{1,0:T(8,128)(2,1)S(1)}, bf16[128,512]{1,0:T(8,128)(2,1)S(1)}, u32[]{:S(2)}, u32[]{:S(2)}) collective-permute-start(bf16[128,512]{1,0:T(8,128)(2,1)S(1)} %get-tuple-element.130), channel_id=1, source_target_pairs={{0,3},{1,0},{2,1},{3,2},{4,7},{5,4},{6,5},{7,6},{8,11},{9,8},{10,9... | collective-permute-start | bytes 393224 | tf_op jit(solution)/shard_map/ppermute | solution.py:43
  136.7 6.7 %collective-permute-start.34 = (bf16[128,512]{1,0:T(8,128)(2,1)S(1)}, bf16[128,512]{1,0:T(8,128)(2,1)S(1)}, u32[]{:S(2)}, u32[]{:S(2)}) collective-permute-start(bf16[128,512]{1,0:T(8,128)(2,1)S(1)} %get-tuple-element.121), channel_id=1, source_target_pairs={{0,8},{1,9},{2,10},{3,11},{4,12},{5,13},{6,14},{7,15},{8,0},{9,1},... | collective-permute-start | bytes 393224 | tf_op jit(solution)/shard_map/ppermute | solution.py:48
  136.8 8.5 %collective-permute-start.35 = (bf16[128,512]{1,0:T(8,128)(2,1)S(1)}, bf16[128,512]{1,0:T(8,128)(2,1)S(1)}, u32[]{:S(2)}, u32[]{:S(2)}) collective-permute-start(bf16[128,512]{1,0:T(8,128)(2,1)S(1)} %get-tuple-element.122), channel_id=1, source_target_pairs={{0,4},{1,5},{2,6},{3,7},{4,8},{5,9},{6,10},{7,11},{8,12},{9,13},{1... | collective-permute-start | bytes 393224 | tf_op jit(solution)/shard_map/ppermute | solution.py:43
  137.8 7.5 %collective-permute-start.36 = (bf16[128,512]{1,0:T(8,128)(2,1)S(1)}, bf16[128,512]{1,0:T(8,128)(2,1)S(1)}, u32[]{:S(2)}, u32[]{:S(2)}) collective-permute-start(bf16[128,512]{1,0:T(8,128)(2,1)S(1)} %get-tuple-element.123), channel_id=1, source_target_pairs={{0,12},{1,13},{2,14},{3,15},{4,0},{5,1},{6,2},{7,3},{8,4},{9,5},{1... | collective-permute-start | bytes 393224 | tf_op jit(solution)/shard_map/ppermute | solution.py:43
  145.4 6.3 %collective-permute-start.40 = (bf16[64,512]{1,0:T(8,128)(2,1)S(1)}, bf16[64,512]{1,0:T(8,128)(2,1)S(1)}, u32[]{:S(2)}, u32[]{:S(2)}) collective-permute-start(bf16[64,512]{1,0:T(8,128)(2,1)S(1)} %get-tuple-element.132), channel_id=1, source_target_pairs={{0,64},{16,80},{32,96},{48,112},{64,0},{80,16},{96,32},{112,48},{1... | collective-permute-start | bytes 196616 | tf_op jit(solution)/shard_map/ppermute | solution.py:48
  147.8 5.5 %collective-permute-start.41 = (bf16[64,512]{1,0:T(8,128)(2,1)S(1)}, bf16[64,512]{1,0:T(8,128)(2,1)S(1)}, u32[]{:S(2)}, u32[]{:S(2)}) collective-permute-start(bf16[64,512]{1,0:T(8,128)(2,1)S(1)} %get-tuple-element.133), channel_id=1, source_target_pairs={{0,32},{16,48},{32,64},{48,80},{64,96},{80,112},{96,0},{112,16},{1... | collective-permute-start | bytes 196616 | tf_op jit(solution)/shard_map/ppermute | solution.py:48
  148.7 4.5 %collective-permute-start.42 = (bf16[64,512]{1,0:T(8,128)(2,1)S(1)}, bf16[64,512]{1,0:T(8,128)(2,1)S(1)}, u32[]{:S(2)}, u32[]{:S(2)}) collective-permute-start(bf16[64,512]{1,0:T(8,128)(2,1)S(1)} %get-tuple-element.134), channel_id=1, source_target_pairs={{0,96},{16,112},{32,0},{48,16},{64,32},{80,48},{96,64},{112,80},{1... | collective-permute-start | bytes 196616 | tf_op jit(solution)/shard_map/ppermute | solution.py:48

commit v5 on v4

--- a/solution.py
+++ b/solution.py
@@ -377,6 +377,7 @@
     near, sums, keep, far_down = wait((near, sums, keep, far_down))
     own_x[1], own_x[3], own_g[1], own_g[3] = near
     swap(1)
+    own_g[3], _ = wait((own_g[3], far_x[3]))
     swap(3)
     ends = [hop(own_x[1], "z", 1), hop(own_g[1], "x", 1)]
     own_sums, far_sums = add((1, 3), sums)

time: 154 us -> 155 us (level)
  starting transfers between devices: 50.8 us -> 53.1 us
  waiting for transfers between devices: 47.2 us -> 45.1 us
    ppermute x16, starting transfers between devices: 20 us -> 22.5 us  [hop(): return lax.ppermute(value, ('cuts', 'shard'), pairs)]
  transfers between devices with their start and end apart: 43 -> 43, of which waited for: 21 -> 18; matrix products, arithmetic and copies ran while one was open for 3% -> 3% of each run, Pallas kernels for 25% -> 25%
where the time goes in v5:
time: 155 us; the launch traced here: 154 us
  starting transfers between devices  53.1 us (34%)
  waiting for transfers between devices  45.1 us (29%)
  Pallas kernels  39.4 us (25%)
  local copies, waits for them, and re-layouts  11.7 us (8%)
  other arithmetic  3.91 us (3%)
    ppermute x27, starting transfers between devices, shift(): return lax.ppermute(value, name, pairs)  30.6 us
    ppermute x27, waiting for transfers between devices, shift(): return lax.ppermute(value, name, pairs)  25.6 us
    ppermute x16, starting transfers between devices, hop(): return lax.ppermute(value, ('cuts', 'shard'), pairs)  22.5 us
    ppermute x16, waiting for transfers between devices, hop(): return lax.ppermute(value, ('cuts', 'shard'), pairs)  19.5 us
    pallas_call x2, Pallas kernels, weight_grads(): pl.pallas_call(kernel, grid_spec=pltpu.PrefetchScalarGridSpec(num_scalar_...  14.2 us
    pallas_call x2, Pallas kernels, forward(): pl.pallas_call(functools.partial(forward_kernel, es, not before), in_spec...  11.5 us
    unnamed x24, local copies, waits for them, and re-layouts  9.83 us
    pallas_call x1, Pallas kernels, input_grads(): pl.pallas_call(input_grad_kernel, in_specs=[SMEM] + [VMEM] * 2 + [ANY] *...  7.01 us
  transfers between devices with their start and end apart: 43, of which 18 were waited for; matrix products, arithmetic and copies ran while one was open for 3% of the time, Pallas kernels for 25%

profile of v5, /device:TPU:0, one launch (start us, length us, event | category | flops | bytes accessed | tf_op | source)
XLA Modules:
  0.0 154.2 jit_solution(1473458233225346716)
XLA Ops:
  0.7 0.5 collective-permute-start.4
  1.2 0.7 convert_bitcast_fusion
  1.9 0.9 fusion.1
  2.8 1.7 %collective-permute-start.2 = (bf16[144,512]{1,0:T(8,128)(2,1)S(1)}, bf16[144,512]{1,0:T(8,128)(2,1)S(1)}, u32[]{:S(2)}, u32[]{:S(2)}) collective-permute-start(bf16[144,512]{1,0:T(8,128)(2,1)S(1)} %fusion.1), channel_id=1, source_target_pairs={{0,32},{16,48},{32,64},{48,80},{64,96},{80,112},{96,0},{112,16},{1... | collective-permute-start | bytes 442376 | tf_op jit(solution)/shard_map/ppermute | solution.py:48
  4.5 2.9 %collective-permute-start.1 = (bf16[144,512]{1,0:T(8,128)(2,1)S(1)}, bf16[144,512]{1,0:T(8,128)(2,1)S(1)}, u32[]{:S(2)}, u32[]{:S(2)}) collective-permute-start(bf16[144,512]{1,0:T(8,128)(2,1)S(1)} %fusion.1), channel_id=1, source_target_pairs={{0,64},{16,80},{32,96},{48,112},{64,0},{80,16},{96,32},{112,48},{1... | collective-permute-start | bytes 442376 | tf_op jit(solution)/shard_map/ppermute | solution.py:48
  7.4 1.3 collective-permute-start
  8.7 1.3 collective-permute-done.2
  10.0 4.3 %collective-permute-done.1 = bf16[144,512]{1,0:T(8,128)(2,1)S(1)} collective-permute-done((bf16[144,512]{1,0:T(8,128)(2,1)S(1)}, bf16[144,512]{1,0:T(8,128)(2,1)S(1)}, u32[]{:S(2)}, u32[]{:S(2)}) %collective-permute-start.1) | collective-permute-done | bytes 147488 | tf_op jit(solution)/shard_map/ppermute | solution.py:48
  14.4 1.9 %copy-done.6 = bf16[224,8192]{1,0:T(8,128)(2,1)} copy-done((bf16[224,8192]{1,0:T(8,128)(2,1)}, bf16[224,8192]{1,0:T(8,128)(2,1)S(1)}, u32[]{:S(2)}) %copy-start.6) | copy-done | bytes 3670040
  16.3 1.6 %collective-permute-start.10 = (bf16[256,512]{1,0:T(8,128)(2,1)S(1)}, bf16[256,512]{1,0:T(8,128)(2,1)S(1)}, u32[]{:S(2)}, u32[]{:S(2)}) collective-permute-start(bf16[256,512]{1,0:T(8,128)(2,1)S(1)} %pad_maximum_fusion.3), channel_id=1, source_target_pairs={{0,1},{1,2},{2,3},{3,0},{4,5},{5,6},{6,7},{7,4},{8,9},{9,10},{10,1... | collective-permute-start | bytes 786440 | tf_op jit(solution)/shard_map/ppermute | solution.py:48
  17.9 2.7 %collective-permute-start.9 = (bf16[256,512]{1,0:T(8,128)(2,1)S(1)}, bf16[256,512]{1,0:T(8,128)(2,1)S(1)}, u32[]{:S(2)}, u32[]{:S(2)}) collective-permute-start(bf16[256,512]{1,0:T(8,128)(2,1)S(1)} %pad_maximum_fusion.3), channel_id=1, source_target_pairs={{0,2},{1,3},{2,0},{3,1},{4,6},{5,7},{6,4},{7,5},{8,10},{9,11},{10,... | collective-permute-start | bytes 786440 | tf_op jit(solution)/shard_map/ppermute | solution.py:48
  20.6 1.4 collective-permute-start.8
  22.1 1.8 %copy-done.8 = bf16[224,8192]{1,0:T(8,128)(2,1)} copy-done((bf16[224,8192]{1,0:T(8,128)(2,1)}, bf16[224,8192]{1,0:T(8,128)(2,1)S(1)}, u32[]{:S(2)}) %copy-start.8) | copy-done | bytes 3670040
  23.9 1.9 %collective-permute-start.7 = (bf16[256,512]{1,0:T(8,128)(2,1)S(1)}, bf16[256,512]{1,0:T(8,128)(2,1)S(1)}, u32[]{:S(2)}, u32[]{:S(2)}) collective-permute-start(bf16[256,512]{1,0:T(8,128)(2,1)S(1)} %pad_maximum_fusion.2), channel_id=1, source_target_pairs={{0,4},{1,5},{2,6},{3,7},{4,8},{5,9},{6,10},{7,11},{8,12},{9,13},{1... | collective-permute-start | bytes 786440 | tf_op jit(solution)/shard_map/ppermute | solution.py:48
  25.9 3.6 %collective-permute-start.6 = (bf16[256,512]{1,0:T(8,128)(2,1)S(1)}, bf16[256,512]{1,0:T(8,128)(2,1)S(1)}, u32[]{:S(2)}, u32[]{:S(2)}) collective-permute-start(bf16[256,512]{1,0:T(8,128)(2,1)S(1)} %pad_maximum_fusion.2), channel_id=1, source_target_pairs={{0,8},{1,9},{2,10},{3,11},{4,12},{5,13},{6,14},{7,15},{8,0},{9,1},... | collective-permute-start | bytes 786440 | tf_op jit(solution)/shard_map/ppermute | solution.py:48
  29.4 1.0 collective-permute-start.5
  30.5 1.2 collective-permute-done.9
  31.7 2.6 %collective-permute-done.7 = bf16[256,512]{1,0:T(8,128)(2,1)S(1)} collective-permute-done((bf16[256,512]{1,0:T(8,128)(2,1)S(1)}, bf16[256,512]{1,0:T(8,128)(2,1)S(1)}, u32[]{:S(2)}, u32[]{:S(2)}) %collective-permute-start.7) | collective-permute-done | bytes 262176 | tf_op jit(solution)/shard_map/ppermute | solution.py:48
  34.3 5.4 %collective-permute-done.6 = bf16[256,512]{1,0:T(8,128)(2,1)S(1)} collective-permute-done((bf16[256,512]{1,0:T(8,128)(2,1)S(1)}, bf16[256,512]{1,0:T(8,128)(2,1)S(1)}, u32[]{:S(2)}, u32[]{:S(2)}) %collective-permute-start.6) | collective-permute-done | bytes 262176 | tf_op jit(solution)/shard_map/ppermute | solution.py:48
  40.0 1.1 pad_maximum_fusion.refs_0_
  41.2 0.5 collective-permute-start.15
  41.7 0.6 collective-permute-start.14
  42.3 2.6 %collective-permute-start.13 = (bf16[4,256,512]{2,1,0:T(8,128)(2,1)S(1)}, bf16[4,256,512]{2,1,0:T(8,128)(2,1)}, u32[]{:S(2)}, u32[]{:S(2)}) collective-permute-start(bf16[4,256,512]{2,1,0:T(8,128)(2,1)S(1)} %pad_maximum_fusion.1.refs_2_.refs_0_), channel_id=1, source_target_pairs={{0,3},{1,0},{2,1},{3,2},{4,7},{5,4},{6,5},{7,6},{8,11},{9,8},{10,9... | collective-permute-start | bytes 3145736 | tf_op jit(solution)/shard_map/ppermute | solution.py:43
  44.9 1.1 collective-permute-start.12
  46.1 2.1 %collective-permute-start.11 = (bf16[4,256,512]{2,1,0:T(8,128)(2,1)}, bf16[4,256,512]{2,1,0:T(8,128)(2,1)}, u32[]{:S(2)}, u32[]{:S(2)}) collective-permute-start(bf16[4,256,512]{2,1,0:T(8,128)(2,1)} %pad_maximum_fusion.refs_0_), channel_id=1, source_target_pairs={{0,12},{1,13},{2,14},{3,15},{4,0},{5,1},{6,2},{7,3},{8,4},{9,5},{1... | collective-permute-start | bytes 3145736 | tf_op jit(solution)/shard_map/ppermute | solution.py:43
  48.4 2.0 %copy-done = bf16[224,8192]{1,0:T(8,128)(2,1)S(1)} copy-done((bf16[224,8192]{1,0:T(8,128)(2,1)S(1)}, bf16[224,8192]{1,0:T(8,128)(2,1)}, u32[]{:S(2)}) %copy-start) | copy-done | bytes 3670040
  50.5 0.8 shard_map.94
  51.4 0.9 slice_bitcast_fusion.2
  52.2 0.7 slice_bitcast_fusion
  53.1 2.0 %copy-done.2 = bf16[224,8192]{1,0:T(8,128)(2,1)S(1)} copy-done((bf16[224,8192]{1,0:T(8,128)(2,1)S(1)}, bf16[224,8192]{1,0:T(8,128)(2,1)}, u32[]{:S(2)}) %copy-start.2) | copy-done | bytes 3670040
  55.1 2.0 %copy-done.4 = bf16[224,8192]{1,0:T(8,128)(2,1)S(1)} copy-done((bf16[224,8192]{1,0:T(8,128)(2,1)S(1)}, bf16[224,8192]{1,0:T(8,128)(2,1)}, u32[]{:S(2)}) %copy-start.4) | copy-done | bytes 3670040
  57.2 4.4 %shard_map.93 = (f32[3,224,256]{2,1,0:T(8,128)S(1)}, f32[3,224,256]{2,1,0:T(8,128)S(1)}) custom-call(s32[48]{0:T(128)S(1)} %concatenate.32.tab, bf16[224,8192]{1,0:T(8,128)(2,1)S(1)} %copy-done.2, bf16[224,8192]{1,0:T(8,128)(2,1)S(1)} %copy-done.4, bf16[224,8192]{1,0:T(8,128)(2,1)S(1)} %copy-done.1, bf16[4,256,512]{2,1,0:T(8,128)(2,1)} %pad_maximum_fusion.refs_0_, ...), custom_call_target="tpu_custom_call" | custom-call | flops 1409286144 | bytes 8388608 | tf_op jit(solution)/shard_map/pallas_call | solution.py:105
  61.6 6.4 %collective-permute-done.14.refs_6_ = bf16[4,256,512]{2,1,0:T(8,128)(2,1)S(1)} collective-permute-done((bf16[4,256,512]{2,1,0:T(8,128)(2,1)S(1)}, bf16[4,256,512]{2,1,0:T(8,128)(2,1)S(1)}, u32[]{:S(2)}, u32[]{:S(2)}) %collective-permute-start.14) | collective-permute-done | bytes 1048608 | tf_op jit(solution)/shard_map/ppermute | solution.py:43
  68.0 3.6 %collective-permute-done.12.refs_4_.refs_6_ = bf16[4,256,512]{2,1,0:T(8,128)(2,1)} collective-permute-done((bf16[4,256,512]{2,1,0:T(8,128)(2,1)}, bf16[4,256,512]{2,1,0:T(8,128)(2,1)}, u32[]{:S(2)}, u32[]{:S(2)}) %collective-permute-start.12) | collective-permute-done | bytes 1048608 | tf_op jit(solution)/shard_map/ppermute | solution.py:43
  71.7 0.5 collective-permute-start.19
  72.3 2.3 %collective-permute-done.20.refs_5_.refs_7_ = bf16[4,256,512]{2,1,0:T(8,128)(2,1)S(1)} collective-permute-done((bf16[4,256,512]{2,1,0:T(8,128)(2,1)}, bf16[4,256,512]{2,1,0:T(8,128)(2,1)S(1)}, u32[]{:S(2)}, u32[]{:S(2)}) %collective-permute-start.20) | collective-permute-done | bytes 1048608 | tf_op jit(solution)/shard_map/ppermute | solution.py:48
  74.9 1.5 collective-permute-start.18
  76.4 2.7 %collective-permute-done.22.refs_7_ = bf16[4,256,512]{2,1,0:T(8,128)(2,1)S(1)} collective-permute-done((bf16[4,256,512]{2,1,0:T(8,128)(2,1)}, bf16[4,256,512]{2,1,0:T(8,128)(2,1)S(1)}, u32[]{:S(2)}, u32[]{:S(2)}) %collective-permute-start.22) | collective-permute-done | bytes 1048608 | tf_op jit(solution)/shard_map/ppermute | solution.py:48
  79.1 7.1 %shard_map.95 = (f32[3,224,256]{2,1,0:T(8,128)S(1)}, f32[3,224,256]{2,1,0:T(8,128)S(1)}) custom-call(s32[48]{0:T(128)S(1)} %concatenate.32.tab, bf16[224,8192]{1,0:T(8,128)(2,1)S(1)} %copy-done.3, bf16[224,8192]{1,0:T(8,128)(2,1)S(1)} %copy-done.5, bf16[224,8192]{1,0:T(8,128)(2,1)S(1)} %copy-done.1, ...), custom_call_target="tpu_custom_call" | custom-call | flops 2818572288 | bytes 16777216 | tf_op jit(solution)/shard_map/pallas_call | solution.py:105
  86.4 3.3 %collective-permute-done.17.x.refs_4_ = bf16[4,256,512]{2,1,0:T(8,128)(2,1)S(1)} collective-permute-done((bf16[4,256,512]{2,1,0:T(8,128)(2,1)}, bf16[4,256,512]{2,1,0:T(8,128)(2,1)S(1)}, u32[]{:S(2)}, u32[]{:S(2)}) %collective-permute-start.17) | collective-permute-done | bytes 1048608 | tf_op jit(solution)/shard_map/ppermute | solution.py:43
  90.4 5.1 %shard_map.96 = (bf16[3,224,256]{2,1,0:T(8,128)(2,1)S(1)}, bf16[3,224,256]{2,1,0:T(8,128)(2,1)S(1)}, bf16[2,2,128,224]{3,2,1,0:T(8,128)(2,1)S(1)}, bf16[2,2,128,224]{3,2,1,0:T(8,128)(2,1)S(1)}) custom-call(s32[48]{0:T(128)S(1)} %concatenate.32.tab, bf16[224,8192]{1,0:T(8,128)(2,1)S(1)} %copy-done.3, bf16[224,8192]{1,0:T(8,128)(2,1)S(1)} %copy-done.5, ...), custom_call_target="tpu_custom_call" | custom-call | flops 1409286144 | bytes 8388608 | tf_op jit(solution)/shard_map/pallas_call | solution.py:160
  95.9 7.0 %shard_map.97 = (bf16[4,128,512]{2,1,0:T(8,128)(2,1)S(1)}, bf16[4,128,512]{2,1,0:T(8,128)(2,1)S(1)}, bf16[4,128,512]{2,1,0:T(8,128)(2,1)S(1)}, bf16[4,128,512]{2...) custom-call(s32[48]{0:T(128)S(1)} %concatenate.32.tab, ...), custom_call_target="tpu_custom_call" | custom-call | flops 3758096384 | bytes 18874368 | tf_op jit(solution)/shard_map/pallas_call | solution.py:257
  103.3 1.3 collective-permute-start.26
  104.6 3.2 %collective-permute-start.27 = (bf16[4,128,512]{2,1,0:T(8,128)(2,1)S(1)}, bf16[4,128,512]{2,1,0:T(8,128)(2,1)S(1)}, u32[]{:S(2)}, u32[]{:S(2)}) collective-permute-start(bf16[4,128,512]{2,1,0:T(8,128)(2,1)S(1)} %get-tuple-element.110), channel_id=1, source_target_pairs={{0,3},{1,0},{2,1},{3,2},{4,7},{5,4},{6,5},{7,6},{8,11},{9,8},{10,9... | collective-permute-start | bytes 1572872 | tf_op jit(solution)/shard_map/ppermute | solution.py:43
  107.8 1.6 %collective-permute-start.28 = (bf16[4,128,512]{2,1,0:T(8,128)(2,1)S(1)}, bf16[4,128,512]{2,1,0:T(8,128)(2,1)S(1)}, u32[]{:S(2)}, u32[]{:S(2)}) collective-permute-start(bf16[4,128,512]{2,1,0:T(8,128)(2,1)S(1)} %get-tuple-element.111), channel_id=1, source_target_pairs={{0,12},{1,13},{2,14},{3,15},{4,0},{5,1},{6,2},{7,3},{8,4},{9,5},{1... | collective-permute-start | bytes 1572872 | tf_op jit(solution)/shard_map/ppermute | solution.py:43
  109.4 8.6 %shard_map.98 = (bf16[224,8192]{1,0:T(8,128)(2,1)}, bf16[224,8192]{1,0:T(8,128)(2,1)}) custom-call(s32[48]{0:T(128)S(1)} %concatenate.32.tab, bf16[3,224,256]{2,1,0:T(8,128)(2,1)S(1)} %get-tuple-element.112.own_t, bf16[3,224,256]{2,1,0:T(8,128)(2,1)S(1)} %collective-permute-done.29.far_t, bf16[4,256,512]{2,1,0:T(8,128)(2,1)} %pad_maximum_fusion.refs_0_, ...), custom_call_target="tpu_custom_call" | custom-call | flops 3758096384 | bytes 12582912 | tf_op jit(solution)/shard_map/pallas_call | solution.py:212
  118.1 1.3 collective-permute-done.28.b
  119.8 1.2 collective-permute-start.32
  121.0 5.6 %shard_map.101 = bf16[224,8192]{1,0:T(8,128)(2,1)} custom-call(s32[48]{0:T(128)S(1)} %concatenate.32.tab, bf16[3,224,256]{2,1,0:T(8,128)(2,1)S(1)} %get-tuple-element.112.own_t, bf16[3,224,256]{2,1,0:T(8,128)(2,1)S(1)} %collective-permute-done.29.far_t, bf16[4,256,512]{2,1,0:T(8,128)(2,1)S(1)} %pad_maximum_fusion.1.refs_2_.refs_0_, ...), custom_call_target="tpu_custom_call" | custom-call | flops 1879048192 | bytes 6291456 | tf_op jit(solution)/shard_map/pallas_call | solution.py:212
  126.6 3.4 %collective-permute-done.31.c = bf16[4,128,512]{2,1,0:T(8,128)(2,1)S(1)} collective-permute-done((bf16[4,128,512]{2,1,0:T(8,128)(2,1)S(1)}, bf16[4,128,512]{2,1,0:T(8,128)(2,1)S(1)}, u32[]{:S(2)}, u32[]{:S(2)}) %collective-permute-start.31) | collective-permute-done | bytes 524320 | tf_op jit(solution)/shard_map/ppermute | solution.py:43
  130.4 3.0 %collective-permute-start.37 = (bf16[128,512]{1,0:T(8,128)(2,1)S(1)}, bf16[128,512]{1,0:T(8,128)(2,1)S(1)}, u32[]{:S(2)}, u32[]{:S(2)}) collective-permute-start(bf16[128,512]{1,0:T(8,128)(2,1)S(1)} %get-tuple-element.130), channel_id=1, source_target_pairs={{0,2},{1,3},{2,0},{3,1},{4,6},{5,7},{6,4},{7,5},{8,10},{9,11},{10,... | collective-permute-start | bytes 393224 | tf_op jit(solution)/shard_map/ppermute | solution.py:48
  133.5 1.1 collective-permute-start.38
  134.6 2.1 %collective-permute-start.39 = (bf16[128,512]{1,0:T(8,128)(2,1)S(1)}, bf16[128,512]{1,0:T(8,128)(2,1)S(1)}, u32[]{:S(2)}, u32[]{:S(2)}) collective-permute-start(bf16[128,512]{1,0:T(8,128)(2,1)S(1)} %get-tuple-element.132), channel_id=1, source_target_pairs={{0,3},{1,0},{2,1},{3,2},{4,7},{5,4},{6,5},{7,6},{8,11},{9,8},{10,9... | collective-permute-start | bytes 393224 | tf_op jit(solution)/shard_map/ppermute | solution.py:43
  136.9 0.8 collective-permute-start.34
  137.7 1.9 %collective-permute-start.35 = (bf16[128,512]{1,0:T(8,128)(2,1)S(1)}, bf16[128,512]{1,0:T(8,128)(2,1)S(1)}, u32[]{:S(2)}, u32[]{:S(2)}) collective-permute-start(bf16[128,512]{1,0:T(8,128)(2,1)S(1)} %get-tuple-element.124), channel_id=1, source_target_pairs={{0,4},{1,5},{2,6},{3,7},{4,8},{5,9},{6,10},{7,11},{8,12},{9,13},{1... | collective-permute-start | bytes 393224 | tf_op jit(solution)/shard_map/ppermute | solution.py:43
  139.5 1.4 collective-permute-start.36
  140.9 3.6 %collective-permute-done.34.refs_1_ = bf16[128,512]{1,0:T(8,128)(2,1)S(1)} collective-permute-done((bf16[128,512]{1,0:T(8,128)(2,1)S(1)}, bf16[128,512]{1,0:T(8,128)(2,1)S(1)}, u32[]{:S(2)}, u32[]{:S(2)}) %collective-permute-start.34) | collective-permute-done | bytes 131104 | tf_op jit(solution)/shard_map/ppermute | solution.py:48
  144.5 1.0 collective-permute-done.35.refs_2_
  145.6 2.4 %collective-permute-start.40 = (bf16[64,512]{1,0:T(8,128)(2,1)S(1)}, bf16[64,512]{1,0:T(8,128)(2,1)S(1)}, u32[]{:S(2)}, u32[]{:S(2)}) collective-permute-start(bf16[64,512]{1,0:T(8,128)(2,1)S(1)} %get-tuple-element.134), channel_id=1, source_target_pairs={{0,64},{16,80},{32,96},{48,112},{64,0},{80,16},{96,32},{112,48},{1... | collective-permute-start | bytes 196616 | tf_op jit(solution)/shard_map/ppermute | solution.py:48
  148.0 0.9 collective-permute-start.41
  148.9 2.4 %collective-permute-start.42 = (bf16[64,512]{1,0:T(8,128)(2,1)S(1)}, bf16[64,512]{1,0:T(8,128)(2,1)S(1)}, u32[]{:S(2)}, u32[]{:S(2)}) collective-permute-start(bf16[64,512]{1,0:T(8,128)(2,1)S(1)} %get-tuple-element.136), channel_id=1, source_target_pairs={{0,96},{16,112},{32,0},{48,16},{64,32},{80,48},{96,64},{112,80},{1... | collective-permute-start | bytes 196616 | tf_op jit(solution)/shard_map/ppermute | solution.py:48
  151.3 0.9 collective-permute-done.40
  152.2 1.3 collective-permute-done.41
  153.5 0.7 add_convert_fusion
  (80 shorter events, 4.3 us)
Async XLA Ops:
  0.6 13.8 %collective-permute-start.3 = (bf16[224,8192]{1,0:T(8,128)(2,1)}, bf16[224,8192]{1,0:T(8,128)(2,1)S(1)}, u32[]{:S(2)}, u32[]{:S(2)}) collective-permute-start(bf16[224,8192]{1,0:T(8,128)(2,1)} %refs_0_.1), channel_id=1, source_target_pairs={{0,16},{16,0},{32,48},{48,32},{64,80},{80,64},{96,112},{112,96},{1... | collective-permute-start | bytes 11010056 | tf_op jit(solution)/shard_map/ppermute | solution.py:48
  0.7 21.4 %collective-permute-start.4 = (bf16[224,8192]{1,0:T(8,128)(2,1)}, bf16[224,8192]{1,0:T(8,128)(2,1)S(1)}, u32[]{:S(2)}, u32[]{:S(2)}) collective-permute-start(bf16[224,8192]{1,0:T(8,128)(2,1)} %refs_1_.1), channel_id=1, source_target_pairs={{0,16},{16,0},{32,48},{48,32},{64,80},{80,64},{96,112},{112,96},{1... | collective-permute-start | bytes 11010056 | tf_op jit(solution)/shard_map/ppermute | solution.py:48
  2.8 7.3 %collective-permute-start.2 = (bf16[144,512]{1,0:T(8,128)(2,1)S(1)}, bf16[144,512]{1,0:T(8,128)(2,1)S(1)}, u32[]{:S(2)}, u32[]{:S(2)}) collective-permute-start(bf16[144,512]{1,0:T(8,128)(2,1)S(1)} %fusion.1), channel_id=1, source_target_pairs={{0,32},{16,48},{32,64},{48,80},{64,96},{80,112},{96,0},{112,16},{1... | collective-permute-start | bytes 442376 | tf_op jit(solution)/shard_map/ppermute | solution.py:48
  4.5 9.9 %collective-permute-start.1 = (bf16[144,512]{1,0:T(8,128)(2,1)S(1)}, bf16[144,512]{1,0:T(8,128)(2,1)S(1)}, u32[]{:S(2)}, u32[]{:S(2)}) collective-permute-start(bf16[144,512]{1,0:T(8,128)(2,1)S(1)} %fusion.1), channel_id=1, source_target_pairs={{0,64},{16,80},{32,96},{48,112},{64,0},{80,16},{96,32},{112,48},{1... | collective-permute-start | bytes 442376 | tf_op jit(solution)/shard_map/ppermute | solution.py:48
  7.4 7.0 %collective-permute-start = (bf16[144,512]{1,0:T(8,128)(2,1)S(1)}, bf16[144,512]{1,0:T(8,128)(2,1)S(1)}, u32[]{:S(2)}, u32[]{:S(2)}) collective-permute-start(bf16[144,512]{1,0:T(8,128)(2,1)S(1)} %fusion.1), channel_id=1, source_target_pairs={{0,96},{16,112},{32,0},{48,16},{64,32},{80,48},{96,64},{112,80},{1... | collective-permute-start | bytes 442376 | tf_op jit(solution)/shard_map/ppermute | solution.py:48
  14.4 15.1 %copy-start.10 = (bf16[144,512]{1,0:T(8,128)(2,1)}, bf16[144,512]{1,0:T(8,128)(2,1)S(1)}, u32[]{:S(2)}) copy-start(bf16[144,512]{1,0:T(8,128)(2,1)S(1)} %collective-permute-done.1) | copy-start | bytes 442372
  14.4 1.9 %copy-start.11 = (bf16[144,512]{1,0:T(8,128)(2,1)}, bf16[144,512]{1,0:T(8,128)(2,1)S(1)}, u32[]{:S(2)}) copy-start(bf16[144,512]{1,0:T(8,128)(2,1)S(1)} %collective-permute-done) | copy-start | bytes 442372
  14.4 1.9 %copy-start.6 = (bf16[224,8192]{1,0:T(8,128)(2,1)}, bf16[224,8192]{1,0:T(8,128)(2,1)S(1)}, u32[]{:S(2)}) copy-start(bf16[224,8192]{1,0:T(8,128)(2,1)S(1)} %collective-permute-done.3.far_wg.refs_2_) | copy-start | bytes 11010052
  16.3 13.1 %collective-permute-start.10 = (bf16[256,512]{1,0:T(8,128)(2,1)S(1)}, bf16[256,512]{1,0:T(8,128)(2,1)S(1)}, u32[]{:S(2)}, u32[]{:S(2)}) collective-permute-start(bf16[256,512]{1,0:T(8,128)(2,1)S(1)} %pad_maximum_fusion.3), channel_id=1, source_target_pairs={{0,1},{1,2},{2,3},{3,0},{4,5},{5,6},{6,7},{7,4},{8,9},{9,10},{10,1... | collective-permute-start | bytes 786440 | tf_op jit(solution)/shard_map/ppermute | solution.py:48
  17.9 13.8 %collective-permute-start.9 = (bf16[256,512]{1,0:T(8,128)(2,1)S(1)}, bf16[256,512]{1,0:T(8,128)(2,1)S(1)}, u32[]{:S(2)}, u32[]{:S(2)}) collective-permute-start(bf16[256,512]{1,0:T(8,128)(2,1)S(1)} %pad_maximum_fusion.3), channel_id=1, source_target_pairs={{0,2},{1,3},{2,0},{3,1},{4,6},{5,7},{6,4},{7,5},{8,10},{9,11},{10,... | collective-permute-start | bytes 786440 | tf_op jit(solution)/shard_map/ppermute | solution.py:48
  20.6 11.1 %collective-permute-start.8 = (bf16[256,512]{1,0:T(8,128)(2,1)S(1)}, bf16[256,512]{1,0:T(8,128)(2,1)S(1)}, u32[]{:S(2)}, u32[]{:S(2)}) collective-permute-start(bf16[256,512]{1,0:T(8,128)(2,1)S(1)} %pad_maximum_fusion.3), channel_id=1, source_target_pairs={{0,3},{1,0},{2,1},{3,2},{4,7},{5,4},{6,5},{7,6},{8,11},{9,8},{10,9... | collective-permute-start | bytes 786440 | tf_op jit(solution)/shard_map/ppermute | solution.py:48
  22.1 1.8 %copy-start.8 = (bf16[224,8192]{1,0:T(8,128)(2,1)}, bf16[224,8192]{1,0:T(8,128)(2,1)S(1)}, u32[]{:S(2)}) copy-start(bf16[224,8192]{1,0:T(8,128)(2,1)S(1)} %collective-permute-done.4.far_wu.refs_3_) | copy-start | bytes 11010052
  23.9 10.4 %collective-permute-start.7 = (bf16[256,512]{1,0:T(8,128)(2,1)S(1)}, bf16[256,512]{1,0:T(8,128)(2,1)S(1)}, u32[]{:S(2)}, u32[]{:S(2)}) collective-permute-start(bf16[256,512]{1,0:T(8,128)(2,1)S(1)} %pad_maximum_fusion.2), channel_id=1, source_target_pairs={{0,4},{1,5},{2,6},{3,7},{4,8},{5,9},{6,10},{7,11},{8,12},{9,13},{1... | collective-permute-start | bytes 786440 | tf_op jit(solution)/shard_map/ppermute | solution.py:48
  25.9 13.8 %collective-permute-start.6 = (bf16[256,512]{1,0:T(8,128)(2,1)S(1)}, bf16[256,512]{1,0:T(8,128)(2,1)S(1)}, u32[]{:S(2)}, u32[]{:S(2)}) collective-permute-start(bf16[256,512]{1,0:T(8,128)(2,1)S(1)} %pad_maximum_fusion.2), channel_id=1, source_target_pairs={{0,8},{1,9},{2,10},{3,11},{4,12},{5,13},{6,14},{7,15},{8,0},{9,1},... | collective-permute-start | bytes 786440 | tf_op jit(solution)/shard_map/ppermute | solution.py:48
  29.4 10.2 %collective-permute-start.5 = (bf16[256,512]{1,0:T(8,128)(2,1)S(1)}, bf16[256,512]{1,0:T(8,128)(2,1)S(1)}, u32[]{:S(2)}, u32[]{:S(2)}) collective-permute-start(bf16[256,512]{1,0:T(8,128)(2,1)S(1)} %pad_maximum_fusion.2), channel_id=1, source_target_pairs={{0,12},{1,13},{2,14},{3,15},{4,0},{5,1},{6,2},{7,3},{8,4},{9,5},{1... | collective-permute-start | bytes 786440 | tf_op jit(solution)/shard_map/ppermute | solution.py:48
  39.8 6.3 %collective-permute-start.16 = (bf16[4,256,512]{2,1,0:T(8,128)(2,1)S(1)}, bf16[4,256,512]{2,1,0:T(8,128)(2,1)S(1)}, u32[]{:S(2)}, u32[]{:S(2)}) collective-permute-start(bf16[4,256,512]{2,1,0:T(8,128)(2,1)S(1)} %pad_maximum_fusion.1.refs_2_.refs_0_), channel_id=1, source_target_pairs={{0,16},{16,0},{32,48},{48,32},{64,80},{80,64},{96,112},{112,96},{1... | collective-permute-start | bytes 3145736 | tf_op jit(solution)/shard_map/ppermute | solution.py:48
  41.2 11.9 %collective-permute-start.15 = (bf16[4,256,512]{2,1,0:T(8,128)(2,1)}, bf16[4,256,512]{2,1,0:T(8,128)(2,1)}, u32[]{:S(2)}, u32[]{:S(2)}) collective-permute-start(bf16[4,256,512]{2,1,0:T(8,128)(2,1)} %pad_maximum_fusion.refs_0_), channel_id=1, source_target_pairs={{0,16},{16,0},{32,48},{48,32},{64,80},{80,64},{96,112},{112,96},{1... | collective-permute-start | bytes 3145736 | tf_op jit(solution)/shard_map/ppermute | solution.py:48
  41.7 26.3 %collective-permute-start.14 = (bf16[4,256,512]{2,1,0:T(8,128)(2,1)S(1)}, bf16[4,256,512]{2,1,0:T(8,128)(2,1)S(1)}, u32[]{:S(2)}, u32[]{:S(2)}) collective-permute-start(bf16[4,256,512]{2,1,0:T(8,128)(2,1)S(1)} %pad_maximum_fusion.1.refs_2_.refs_0_), channel_id=1, source_target_pairs={{0,1},{1,2},{2,3},{3,0},{4,5},{5,6},{6,7},{7,4},{8,9},{9,10},{10,1... | collective-permute-start | bytes 3145736 | tf_op jit(solution)/shard_map/ppermute | solution.py:43
  42.3 25.7 %collective-permute-start.13 = (bf16[4,256,512]{2,1,0:T(8,128)(2,1)S(1)}, bf16[4,256,512]{2,1,0:T(8,128)(2,1)}, u32[]{:S(2)}, u32[]{:S(2)}) collective-permute-start(bf16[4,256,512]{2,1,0:T(8,128)(2,1)S(1)} %pad_maximum_fusion.1.refs_2_.refs_0_), channel_id=1, source_target_pairs={{0,3},{1,0},{2,1},{3,2},{4,7},{5,4},{6,5},{7,6},{8,11},{9,8},{10,9... | collective-permute-start | bytes 3145736 | tf_op jit(solution)/shard_map/ppermute | solution.py:43
  44.9 26.7 %collective-permute-start.12 = (bf16[4,256,512]{2,1,0:T(8,128)(2,1)}, bf16[4,256,512]{2,1,0:T(8,128)(2,1)}, u32[]{:S(2)}, u32[]{:S(2)}) collective-permute-start(bf16[4,256,512]{2,1,0:T(8,128)(2,1)} %pad_maximum_fusion.refs_0_), channel_id=1, source_target_pairs={{0,4},{1,5},{2,6},{3,7},{4,8},{5,9},{6,10},{7,11},{8,12},{9,13},{1... | collective-permute-start | bytes 3145736 | tf_op jit(solution)/shard_map/ppermute | solution.py:43
  46.1 25.5 %collective-permute-start.11 = (bf16[4,256,512]{2,1,0:T(8,128)(2,1)}, bf16[4,256,512]{2,1,0:T(8,128)(2,1)}, u32[]{:S(2)}, u32[]{:S(2)}) collective-permute-start(bf16[4,256,512]{2,1,0:T(8,128)(2,1)} %pad_maximum_fusion.refs_0_), channel_id=1, source_target_pairs={{0,12},{1,13},{2,14},{3,15},{4,0},{5,1},{6,2},{7,3},{8,4},{9,5},{1... | collective-permute-start | bytes 3145736 | tf_op jit(solution)/shard_map/ppermute | solution.py:43
  48.4 2.0 %copy-start = (bf16[224,8192]{1,0:T(8,128)(2,1)S(1)}, bf16[224,8192]{1,0:T(8,128)(2,1)}, u32[]{:S(2)}) copy-start(bf16[224,8192]{1,0:T(8,128)(2,1)} %wd.5) | copy-start | bytes 11010052
  50.5 2.6 %copy-start.1 = (bf16[224,8192]{1,0:T(8,128)(2,1)S(1)}, bf16[224,8192]{1,0:T(8,128)(2,1)}, u32[]{:S(2)}) copy-start(bf16[224,8192]{1,0:T(8,128)(2,1)} %wd.5) | copy-start | bytes 11010052
  53.1 2.0 %copy-start.2 = (bf16[224,8192]{1,0:T(8,128)(2,1)S(1)}, bf16[224,8192]{1,0:T(8,128)(2,1)}, u32[]{:S(2)}) copy-start(bf16[224,8192]{1,0:T(8,128)(2,1)} %refs_0_.1) | copy-start | bytes 11010052
  55.1 2.0 %copy-start.4 = (bf16[224,8192]{1,0:T(8,128)(2,1)S(1)}, bf16[224,8192]{1,0:T(8,128)(2,1)}, u32[]{:S(2)}) copy-start(bf16[224,8192]{1,0:T(8,128)(2,1)} %refs_1_.1) | copy-start | bytes 11010052
  57.2 21.9 %copy-start.3 = (bf16[224,8192]{1,0:T(8,128)(2,1)S(1)}, bf16[224,8192]{1,0:T(8,128)(2,1)}, u32[]{:S(2)}) copy-start(bf16[224,8192]{1,0:T(8,128)(2,1)} %refs_0_.1) | copy-start | bytes 11010052
  57.2 21.9 %copy-start.5 = (bf16[224,8192]{1,0:T(8,128)(2,1)S(1)}, bf16[224,8192]{1,0:T(8,128)(2,1)}, u32[]{:S(2)}) copy-start(bf16[224,8192]{1,0:T(8,128)(2,1)} %refs_1_.1) | copy-start | bytes 11010052
  71.6 18.8 %copy-start.7 = (bf16[224,8192]{1,0:T(8,128)(2,1)S(1)}, bf16[224,8192]{1,0:T(8,128)(2,1)}, u32[]{:S(2)}) copy-start(bf16[224,8192]{1,0:T(8,128)(2,1)} %copy-done.6) | copy-start | bytes 11010052
  71.6 18.8 %copy-start.9 = (bf16[224,8192]{1,0:T(8,128)(2,1)S(1)}, bf16[224,8192]{1,0:T(8,128)(2,1)}, u32[]{:S(2)}) copy-start(bf16[224,8192]{1,0:T(8,128)(2,1)} %copy-done.8) | copy-start | bytes 11010052
  71.6 2.9 %collective-permute-start.20 = (bf16[4,256,512]{2,1,0:T(8,128)(2,1)}, bf16[4,256,512]{2,1,0:T(8,128)(2,1)S(1)}, u32[]{:S(2)}, u32[]{:S(2)}) collective-permute-start(bf16[4,256,512]{2,1,0:T(8,128)(2,1)} %collective-permute-done.11.refs_0_.refs_2_), channel_id=1, source_target_pairs={{0,16},{16,0},{32,48},{48,32},{64,80},{80,64},{96,112},{112,96},{1... | collective-permute-start | bytes 3145736 | tf_op jit(solution)/shard_map/ppermute | solution.py:48
  71.7 4.7 %collective-permute-start.19 = (bf16[4,256,512]{2,1,0:T(8,128)(2,1)}, bf16[4,256,512]{2,1,0:T(8,128)(2,1)S(1)}, u32[]{:S(2)}, u32[]{:S(2)}) collective-permute-start(bf16[4,256,512]{2,1,0:T(8,128)(2,1)} %collective-permute-done.12.refs_4_.refs_6_), channel_id=1, source_target_pairs={{0,16},{16,0},{32,48},{48,32},{64,80},{80,64},{96,112},{112,96},{1... | collective-permute-start | bytes 3145736 | tf_op jit(solution)/shard_map/ppermute | solution.py:48
  72.2 6.9 %collective-permute-start.22 = (bf16[4,256,512]{2,1,0:T(8,128)(2,1)}, bf16[4,256,512]{2,1,0:T(8,128)(2,1)S(1)}, u32[]{:S(2)}, u32[]{:S(2)}) collective-permute-start(bf16[4,256,512]{2,1,0:T(8,128)(2,1)} %collective-permute-done.13.refs_2_), channel_id=1, source_target_pairs={{0,16},{16,0},{32,48},{48,32},{64,80},{80,64},{96,112},{112,96},{1... | collective-permute-start | bytes 3145736 | tf_op jit(solution)/shard_map/ppermute | solution.py:48
  74.5 4.5 %collective-permute-start.21 = (bf16[4,256,512]{2,1,0:T(8,128)(2,1)S(1)}, bf16[4,256,512]{2,1,0:T(8,128)(2,1)S(1)}, u32[]{:S(2)}, u32[]{:S(2)}) collective-permute-start(bf16[4,256,512]{2,1,0:T(8,128)(2,1)S(1)} %collective-permute-done.14.refs_6_), channel_id=1, source_target_pairs={{0,16},{16,0},{32,48},{48,32},{64,80},{80,64},{96,112},{112,96},{1... | collective-permute-start | bytes 3145736 | tf_op jit(solution)/shard_map/ppermute | solution.py:48
  74.7 15.0 %collective-permute-start.17 = (bf16[4,256,512]{2,1,0:T(8,128)(2,1)}, bf16[4,256,512]{2,1,0:T(8,128)(2,1)S(1)}, u32[]{:S(2)}, u32[]{:S(2)}) collective-permute-start(bf16[4,256,512]{2,1,0:T(8,128)(2,1)} %collective-permute-done.11.refs_0_.refs_2_), channel_id=1, source_target_pairs={{0,12},{1,13},{2,14},{3,15},{4,0},{5,1},{6,2},{7,3},{8,4},{9,5},{1... | collective-permute-start | bytes 3145736 | tf_op jit(solution)/shard_map/ppermute | solution.py:43
  74.9 15.0 %collective-permute-start.18 = (bf16[4,256,512]{2,1,0:T(8,128)(2,1)}, bf16[4,256,512]{2,1,0:T(8,128)(2,1)S(1)}, u32[]{:S(2)}, u32[]{:S(2)}) collective-permute-start(bf16[4,256,512]{2,1,0:T(8,128)(2,1)} %collective-permute-done.13.refs_2_), channel_id=1, source_target_pairs={{0,3},{1,0},{2,1},{3,2},{4,7},{5,4},{6,5},{7,6},{8,11},{9,8},{10,9... | collective-permute-start | bytes 3145736 | tf_op jit(solution)/shard_map/ppermute | solution.py:43
  76.4 10.0 %collective-permute-start.24 = (bf16[4,224,512]{2,1,0:T(8,128)(2,1)S(1)}, bf16[4,224,512]{2,1,0:T(8,128)(2,1)S(1)}, u32[]{:S(2)}, u32[]{:S(2)}) collective-permute-start(bf16[4,224,512]{2,1,0:T(8,128)(2,1)S(1)} %shard_map.94), channel_id=1, source_target_pairs={{0,16},{16,0},{32,48},{48,32},{64,80},{80,64},{96,112},{112,96},{1... | collective-permute-start | bytes 2752520 | tf_op jit(solution)/shard_map/ppermute | solution.py:48
  86.2 3.7 %collective-permute-start.23 = (f32[3,224,256]{2,1,0:T(8,128)S(1)}, f32[3,224,256]{2,1,0:T(8,128)S(1)}, u32[]{:S(2)}, u32[]{:S(2)}) collective-permute-start(f32[3,224,256]{2,1,0:T(8,128)S(1)} %get-tuple-element.97), channel_id=1, source_target_pairs={{0,16},{16,0},{32,48},{48,32},{64,80},{80,64},{96,112},{112,96},{1... | collective-permute-start | bytes 2064392 | tf_op jit(solution)/shard_map/ppermute | solution.py:48
  89.9 17.9 %collective-permute-start.30 = (bf16[4,256,512]{2,1,0:T(8,128)(2,1)S(1)}, bf16[4,256,512]{2,1,0:T(8,128)(2,1)S(1)}, u32[]{:S(2)}, u32[]{:S(2)}) collective-permute-start(bf16[4,256,512]{2,1,0:T(8,128)(2,1)S(1)} %collective-permute-done.17.x.refs_4_), channel_id=1, source_target_pairs={{0,16},{16,0},{32,48},{48,32},{64,80},{80,64},{96,112},{112,96},{1... | collective-permute-start | bytes 3145736 | tf_op jit(solution)/shard_map/ppermute | solution.py:48
  90.1 30.9 %collective-permute-start.33 = (bf16[4,256,512]{2,1,0:T(8,128)(2,1)S(1)}, bf16[4,256,512]{2,1,0:T(8,128)(2,1)S(1)}, u32[]{:S(2)}, u32[]{:S(2)}) collective-permute-start(bf16[4,256,512]{2,1,0:T(8,128)(2,1)S(1)} %collective-permute-done.18.g.refs_4_), channel_id=1, source_target_pairs={{0,16},{16,0},{32,48},{48,32},{64,80},{80,64},{96,112},{112,96},{1... | collective-permute-start | bytes 3145736 | tf_op jit(solution)/shard_map/ppermute | solution.py:48
  95.5 9.1 %collective-permute-start.29 = (bf16[3,224,256]{2,1,0:T(8,128)(2,1)S(1)}, bf16[3,224,256]{2,1,0:T(8,128)(2,1)S(1)}, u32[]{:S(2)}, u32[]{:S(2)}) collective-permute-start(bf16[3,224,256]{2,1,0:T(8,128)(2,1)S(1)} %get-tuple-element.113), channel_id=1, source_target_pairs={{0,16},{16,0},{32,48},{48,32},{64,80},{80,64},{96,112},{112,96},{1... | collective-permute-start | bytes 1032200 | tf_op jit(solution)/shard_map/ppermute | solution.py:48
  102.9 15.2 %collective-permute-start.25 = (bf16[4,128,512]{2,1,0:T(8,128)(2,1)S(1)}, bf16[4,128,512]{2,1,0:T(8,128)(2,1)S(1)}, u32[]{:S(2)}, u32[]{:S(2)}) collective-permute-start(bf16[4,128,512]{2,1,0:T(8,128)(2,1)S(1)} %get-tuple-element.108), channel_id=1, source_target_pairs={{0,1},{1,2},{2,3},{3,0},{4,5},{5,6},{6,7},{7,4},{8,9},{9,10},{10,1... | collective-permute-start | bytes 1572872 | tf_op jit(solution)/shard_map/ppermute | solution.py:43
  103.3 14.8 %collective-permute-start.26 = (bf16[4,128,512]{2,1,0:T(8,128)(2,1)S(1)}, bf16[4,128,512]{2,1,0:T(8,128)(2,1)S(1)}, u32[]{:S(2)}, u32[]{:S(2)}) collective-permute-start(bf16[4,128,512]{2,1,0:T(8,128)(2,1)S(1)} %get-tuple-element.109), channel_id=1, source_target_pairs={{0,4},{1,5},{2,6},{3,7},{4,8},{5,9},{6,10},{7,11},{8,12},{9,13},{1... | collective-permute-start | bytes 1572872 | tf_op jit(solution)/shard_map/ppermute | solution.py:43
  104.6 13.5 %collective-permute-start.27 = (bf16[4,128,512]{2,1,0:T(8,128)(2,1)S(1)}, bf16[4,128,512]{2,1,0:T(8,128)(2,1)S(1)}, u32[]{:S(2)}, u32[]{:S(2)}) collective-permute-start(bf16[4,128,512]{2,1,0:T(8,128)(2,1)S(1)} %get-tuple-element.110), channel_id=1, source_target_pairs={{0,3},{1,0},{2,1},{3,2},{4,7},{5,4},{6,5},{7,6},{8,11},{9,8},{10,9... | collective-permute-start | bytes 1572872 | tf_op jit(solution)/shard_map/ppermute | solution.py:43
  107.8 11.7 %collective-permute-start.28 = (bf16[4,128,512]{2,1,0:T(8,128)(2,1)S(1)}, bf16[4,128,512]{2,1,0:T(8,128)(2,1)S(1)}, u32[]{:S(2)}, u32[]{:S(2)}) collective-permute-start(bf16[4,128,512]{2,1,0:T(8,128)(2,1)S(1)} %get-tuple-element.111), channel_id=1, source_target_pairs={{0,12},{1,13},{2,14},{3,15},{4,0},{5,1},{6,2},{7,3},{8,4},{9,5},{1... | collective-permute-start | bytes 1572872 | tf_op jit(solution)/shard_map/ppermute | solution.py:43
  119.6 10.5 %collective-permute-start.31 = (bf16[4,128,512]{2,1,0:T(8,128)(2,1)S(1)}, bf16[4,128,512]{2,1,0:T(8,128)(2,1)S(1)}, u32[]{:S(2)}, u32[]{:S(2)}) collective-permute-start(bf16[4,128,512]{2,1,0:T(8,128)(2,1)S(1)} %shard_map.99), channel_id=1, source_target_pairs={{0,1},{1,2},{2,3},{3,0},{4,5},{5,6},{6,7},{7,4},{8,9},{9,10},{10,1... | collective-permute-start | bytes 1572872 | tf_op jit(solution)/shard_map/ppermute | solution.py:43
  119.8 10.5 %collective-permute-start.32 = (bf16[4,128,512]{2,1,0:T(8,128)(2,1)S(1)}, bf16[4,128,512]{2,1,0:T(8,128)(2,1)S(1)}, u32[]{:S(2)}, u32[]{:S(2)}) collective-permute-start(bf16[4,128,512]{2,1,0:T(8,128)(2,1)S(1)} %shard_map.100), channel_id=1, source_target_pairs={{0,4},{1,5},{2,6},{3,7},{4,8},{5,9},{6,10},{7,11},{8,12},{9,13},{1... | collective-permute-start | bytes 1572872 | tf_op jit(solution)/shard_map/ppermute | solution.py:43
  130.4 9.1 %collective-permute-start.37 = (bf16[128,512]{1,0:T(8,128)(2,1)S(1)}, bf16[128,512]{1,0:T(8,128)(2,1)S(1)}, u32[]{:S(2)}, u32[]{:S(2)}) collective-permute-start(bf16[128,512]{1,0:T(8,128)(2,1)S(1)} %get-tuple-element.130), channel_id=1, source_target_pairs={{0,2},{1,3},{2,0},{3,1},{4,6},{5,7},{6,4},{7,5},{8,10},{9,11},{10,... | collective-permute-start | bytes 393224 | tf_op jit(solution)/shard_map/ppermute | solution.py:48
  133.5 7.5 %collective-permute-start.38 = (bf16[128,512]{1,0:T(8,128)(2,1)S(1)}, bf16[128,512]{1,0:T(8,128)(2,1)S(1)}, u32[]{:S(2)}, u32[]{:S(2)}) collective-permute-start(bf16[128,512]{1,0:T(8,128)(2,1)S(1)} %get-tuple-element.131), channel_id=1, source_target_pairs={{0,1},{1,2},{2,3},{3,0},{4,5},{5,6},{6,7},{7,4},{8,9},{9,10},{10,1... | collective-permute-start | bytes 393224 | tf_op jit(solution)/shard_map/ppermute | solution.py:43
  134.6 6.3 %collective-permute-start.39 = (bf16[128,512]{1,0:T(8,128)(2,1)S(1)}, bf16[128,512]{1,0:T(8,128)(2,1)S(1)}, u32[]{:S(2)}, u32[]{:S(2)}) collective-permute-start(bf16[128,512]{1,0:T(8,128)(2,1)S(1)} %get-tuple-element.132), channel_id=1, source_target_pairs={{0,3},{1,0},{2,1},{3,2},{4,7},{5,4},{6,5},{7,6},{8,11},{9,8},{10,9... | collective-permute-start | bytes 393224 | tf_op jit(solution)/shard_map/ppermute | solution.py:43
  136.9 7.6 %collective-permute-start.34 = (bf16[128,512]{1,0:T(8,128)(2,1)S(1)}, bf16[128,512]{1,0:T(8,128)(2,1)S(1)}, u32[]{:S(2)}, u32[]{:S(2)}) collective-permute-start(bf16[128,512]{1,0:T(8,128)(2,1)S(1)} %get-tuple-element.123), channel_id=1, source_target_pairs={{0,8},{1,9},{2,10},{3,11},{4,12},{5,13},{6,14},{7,15},{8,0},{9,1},... | collective-permute-start | bytes 393224 | tf_op jit(solution)/shard_map/ppermute | solution.py:48
  137.7 7.8 %collective-permute-start.35 = (bf16[128,512]{1,0:T(8,128)(2,1)S(1)}, bf16[128,512]{1,0:T(8,128)(2,1)S(1)}, u32[]{:S(2)}, u32[]{:S(2)}) collective-permute-start(bf16[128,512]{1,0:T(8,128)(2,1)S(1)} %get-tuple-element.124), channel_id=1, source_target_pairs={{0,4},{1,5},{2,6},{3,7},{4,8},{5,9},{6,10},{7,11},{8,12},{9,13},{1... | collective-permute-start | bytes 393224 | tf_op jit(solution)/shard_map/ppermute | solution.py:43
  139.5 5.9 %collective-permute-start.36 = (bf16[128,512]{1,0:T(8,128)(2,1)S(1)}, bf16[128,512]{1,0:T(8,128)(2,1)S(1)}, u32[]{:S(2)}, u32[]{:S(2)}) collective-permute-start(bf16[128,512]{1,0:T(8,128)(2,1)S(1)} %get-tuple-element.125), channel_id=1, source_target_pairs={{0,12},{1,13},{2,14},{3,15},{4,0},{5,1},{6,2},{7,3},{8,4},{9,5},{1... | collective-permute-start | bytes 393224 | tf_op jit(solution)/shard_map/ppermute | solution.py:43
  145.6 6.6 %collective-permute-start.40 = (bf16[64,512]{1,0:T(8,128)(2,1)S(1)}, bf16[64,512]{1,0:T(8,128)(2,1)S(1)}, u32[]{:S(2)}, u32[]{:S(2)}) collective-permute-start(bf16[64,512]{1,0:T(8,128)(2,1)S(1)} %get-tuple-element.134), channel_id=1, source_target_pairs={{0,64},{16,80},{32,96},{48,112},{64,0},{80,16},{96,32},{112,48},{1... | collective-permute-start | bytes 196616 | tf_op jit(solution)/shard_map/ppermute | solution.py:48
  148.0 5.5 %collective-permute-start.41 = (bf16[64,512]{1,0:T(8,128)(2,1)S(1)}, bf16[64,512]{1,0:T(8,128)(2,1)S(1)}, u32[]{:S(2)}, u32[]{:S(2)}) collective-permute-start(bf16[64,512]{1,0:T(8,128)(2,1)S(1)} %get-tuple-element.135), channel_id=1, source_target_pairs={{0,32},{16,48},{32,64},{48,80},{64,96},{80,112},{96,0},{112,16},{1... | collective-permute-start | bytes 196616 | tf_op jit(solution)/shard_map/ppermute | solution.py:48
  148.9 4.6 %collective-permute-start.42 = (bf16[64,512]{1,0:T(8,128)(2,1)S(1)}, bf16[64,512]{1,0:T(8,128)(2,1)S(1)}, u32[]{:S(2)}, u32[]{:S(2)}) collective-permute-start(bf16[64,512]{1,0:T(8,128)(2,1)S(1)} %get-tuple-element.136), channel_id=1, source_target_pairs={{0,96},{16,112},{32,0},{48,16},{64,32},{80,48},{96,64},{112,80},{1... | collective-permute-start | bytes 196616 | tf_op jit(solution)/shard_map/ppermute | solution.py:48
